TPU v7x, 768 devices: a whole 4x8x12 slice. The times are simulated.
768 devices in a mesh: replica: 6 (over z_hi, core), dp: 128 (over y, x, z_lo).
Axes of the slice: x: 4, y: 8, z: 12 (z_hi: 3, z_lo: 4; z = z_hi * 4 + z_lo), core: 2. Of those that a mesh axis runs over, the one named last changes fastest.
Arguments:
- layer_input: bfloat16 [6, 49152, 3072], P('replica', 'dp'), may hold values from -24 to 24
- key_cotangent: bfloat16 [6, 49152, 512], P('replica', 'dp'), may hold values from -0.029907227 to 0.029907227
- local_params: float32 [6, 3072, 512], P('replica', 'dp'), may hold values from -6 to 6
- global_params: float32 [3072, 512], P('dp'), may hold values from -6 to 6
- outer_momentum: float32 [128, 24, 512], P('dp', 'replica'), may hold values from -3 to 3
- adam_first: float32 [6, 3072, 512], P('replica', 'dp'), may hold values from -2 to 2
- adam_second: float32 [6, 3072, 512], P('replica', 'dp'), may hold values from 0.25 to 4
Outputs:
- merged_params: bfloat16 [6, 3072, 512], P('replica')
- new_global: float32 [3072, 512], P('dp')
- new_momentum: float32 [128, 24, 512], P('dp', 'replica')
- new_first: float32 [6, 3072, 512], P('replica', 'dp')
- new_second: float32 [6, 3072, 512], P('replica', 'dp')
All inputs are finite; a program needn't handle non-finite values.
Results may differ from a plain program's by a relative error of at most 0.0004.
Values may be sent and summed in bfloat16 or wider, within the bound.
No kernel may reach another device: no remote copies, remote signals or barrier semaphores. Data moves between devices by JAX's collectives and lax.ppermute only.
A program may use at most 32 MiB of HBM per device.

v0:
```python
import jax
import jax.numpy as jnp
from jax import lax
from jax.sharding import Mesh
from jax.sharding import PartitionSpec as P

DP = ("dp_0", "dp_1", "dp_2")


outer_mu = 0.9
outer_rate = 0.7
beta_one = 0.9
beta_two = 0.95
adam_eps = 1e-08
weight_decay = 0.1
inner_rate = 0.1
correct_one = 1.0 - 0.9**50
correct_two = 1.0 - 0.95**50


def summed_rows(x, axes, dim):
    for axis in axes:
        x = lax.psum_scatter(x, axis, scatter_dimension=dim, tiled=True)
    return x


def joined_along(blocks, dim):
    lengths = list(blocks.shape[1:])
    lengths[dim] *= blocks.shape[0]
    return jnp.moveaxis(blocks, 0, dim).reshape(lengths)


def sent_to_all(x, axis):
    devices = lax.axis_size(axis)
    return lax.all_to_all(jnp.broadcast_to(x[None], (devices, *x.shape)), axis, 0, 0, tiled=True)


def gather_directly(x, axis, dim):
    return joined_along(sent_to_all(x, axis), dim)


def gathered_total(x, axis):
    return lax.all_gather(x, axis).sum(0)


def all_blocks(x, axes, turns):
    blocks = x
    for k in turns:
        blocks = lax.all_gather(blocks, axes[k])
    done = turns[::-1]
    back = [done.index(k) for k in range(len(axes))]
    blocks = blocks.transpose(*back, *range(len(axes), blocks.ndim))
    return blocks.reshape(-1, *x.shape)


def whole_of(x, axes, turns, dim):
    return joined_along(all_blocks(x, axes, turns), dim)


def per_device(
    layer_input, key_cotangent, local_params, global_params, outer_momentum, adam_first, adam_second
):
    features = layer_input[0]
    cotangent = key_cotangent[0]
    own_local = local_params[0]
    whole_term = lax.dot_general(
        features, cotangent, (((0,), (0,)), ((), ())), preferred_element_type=jnp.float32
    )
    gradient = summed_rows(whole_term, DP, 0)
    replicas = lax.axis_size("replica")
    deltas = global_params - own_local
    sub_rows = outer_momentum.shape[1]
    row_offset = lax.axis_index("replica") * sub_rows
    old_rows = gather_directly(outer_momentum[0], "replica", 0)
    outer_grad = gathered_total(deltas, "replica") / replicas
    momentum_all = outer_mu * old_rows + outer_grad
    global_new = global_params - outer_rate * (outer_grad + outer_mu * momentum_all)
    momentum_new = lax.dynamic_slice_in_dim(momentum_all, row_offset, sub_rows, 0)
    first_new = beta_one * adam_first[0] + (1.0 - beta_one) * gradient
    second_new = beta_two * adam_second[0] + (1.0 - beta_two) * gradient * gradient
    adam_step = (
        first_new / correct_one / (jnp.sqrt(second_new / correct_two) + adam_eps)
        + weight_decay * own_local
    )
    merged_rows = (global_new - inner_rate * adam_step).astype(jnp.bfloat16)
    gathered = whole_of(merged_rows, DP, (2, 0, 1), 0)
    return (gathered[None], global_new, momentum_new[None], first_new[None], second_new[None])


def solution(mesh):
    torus = Mesh(
        mesh.devices.reshape(mesh.shape["replica"], 8, 4, 4), ("replica", "dp_0", "dp_1", "dp_2")
    )
    in_specs = (
        P("replica", DP, None),
        P("replica", DP, None),
        P("replica", DP, None),
        P(DP, None),
        P(DP, "replica", None),
        P("replica", DP, None),
        P("replica", DP, None),
    )
    out_specs = (
        P("replica", None, None),
        P(DP, None),
        P(DP, "replica", None),
        P("replica", DP, None),
        P("replica", DP, None),
    )
    return jax.shard_map(
        per_device, mesh=torus, in_specs=in_specs, out_specs=out_specs, check_vma=False
    )
```

profile of v0, /device:TPU:1, one launch (start us, length us, event | category | flops | bytes accessed | tf_op | source)
XLA Modules:
  0.0 268.5 jit_solution(8225653877758196476)
XLA Ops:
  7.2 0.0 copy-start
  7.2 0.0 reduce-scatter.4.cloned.1.call-start
  7.2 1.6 copy-done
  8.8 5.5 %fusion = f32[3072,512]{1,0:T(8,128)} fusion(bf16[1,384,3072]{2,1,0:T(8,128)(2,1)S(1)} %copy-done, bf16[1,384,512]{2,1,0:T(8,128)(2,1)} %param.8), kind=kOutput, calls=%fused_computation | convolution fusion | flops 1207959552 | bytes 9043968 | tf_op jit(solution)/shard_map/dot_general | solution.py:66
  14.3 0.0 copy-start.4
  14.4 0.0 reduce-scatter.4.cloned.1.call-update
  14.4 0.0 reduce-scatter.6.cloned.1.call-start
  14.4 87.9 %reduce-scatter.4.cloned.1.call-done = f32[384,512]{1,0:T(8,128)} async-done(((f32[3072,512]{1,0:T(8,128)}), f32[384,512]{1,0:T(8,128)}) %reduce-scatter.4.cloned.1.call-update) | async-done | bytes 786448 | tf_op jit(solution)/shard_map/reduce_scatter | solution.py:23
  102.3 0.0 reduce-scatter.6.cloned.1.call-update
  102.4 0.6 broadcast_in_dim.17
  103.0 8.7 %all-to-all-start = ((f32[6,4,512]{2,1,0:T(4,128)}), f32[6,4,512]{2,1,0:T(4,128)S(1)}, u32[]{:S(2)}, u32[]{:S(2)}) async-start(f32[6,4,512]{2,1,0:T(4,128)} %broadcast_in_dim.17), calls=%async_computation | async-start | bytes 98304 | tf_op jit(solution)/shard_map/all_to_all | solution.py:35
  111.7 22.3 %reduce-scatter.6.cloned.1.call-done = f32[96,512]{1,0:T(8,128)} async-done(((f32[384,512]{1,0:T(8,128)}), f32[96,512]{1,0:T(8,128)}) %reduce-scatter.6.cloned.1.call-update) | async-done | bytes 196624 | tf_op jit(solution)/shard_map/reduce_scatter | solution.py:23
  134.0 0.0 reduce-scatter.8.cloned.1.call-update
  134.0 0.0 all-gather.6.cloned.1.call-start
  134.1 20.1 %all-gather = f32[144,512]{1,0:T(8,128)S(1)} all-gather(f32[24,512]{1,0:T(8,128)S(1)} %bitcast_subtract_fusion), channel_id=2, replica_groups=mesh['replica'=6,'dp_0'=8,'dp_1'=4,'dp_2'=4] {'replica'}, dimensions={0}, use_global_device_ids=true | all-gather | bytes 344064 | tf_op jit(solution)/shard_map/all_gather | solution.py:43
  154.3 0.0 all-to-all-done
  154.3 12.0 %reduce-scatter.8.cloned.1.call-done = f32[24,512]{1,0:T(8,128)} async-done(((f32[96,512]{1,0:T(8,128)}), f32[24,512]{1,0:T(8,128)}) %reduce-scatter.8.cloned.1.call-update) | async-done | bytes 49168 | tf_op jit(solution)/shard_map/reduce_scatter | solution.py:23
  166.3 1.5 fusion.7
  167.8 10.3 %all-gather.1 = bf16[96,512]{1,0:T(8,128)(2,1)S(1)} all-gather(bf16[24,512]{1,0:T(8,128)(2,1)S(1)} %get-tuple-element.5), channel_id=3, replica_groups=mesh['replica'=6,'dp_0'=8,'dp_1'=4,'dp_2'=4] {'dp_2'}, dimensions={0}, use_global_device_ids=true | all-gather | bytes 122880 | tf_op jit(solution)/shard_map/all_gather | solution.py:49
  178.1 23.9 %all-gather.2 = bf16[32,24,512]{2,1,0:T(8,128)(2,1)} all-gather(bf16[4,24,512]{2,1,0:T(8,128)(2,1)S(1)} %bitcast.47), channel_id=4, replica_groups=mesh['replica'=6,'dp_0'=8,'dp_1'=4,'dp_2'=4] {'dp_0'}, dimensions={0}, use_global_device_ids=true | all-gather | bytes 884736 | tf_op jit(solution)/shard_map/all_gather | solution.py:49
  202.1 0.0 all-gather.6.cloned.1.call-update
  202.1 0.6 dynamic-slice_bitcast_fusion
  202.7 55.3 %all-gather.6.cloned.1.call-done = bf16[32,4,24,512]{3,2,1,0:T(8,128)(2,1)} async-done(((bf16[8,4,24,512]{3,2,1,0:T(8,128)(2,1)}), bf16[32,4,24,512]{3,2,1,0:T(8,128)(2,1)}) %all-gather.6.cloned.1.call-update) | async-done | bytes 3145744 | tf_op jit(solution)/shard_map/all_gather | solution.py:49
  258.0 3.9 %copy.13 = bf16[8,4,4,24,512]{4,3,2,1,0:T(8,128)(2,1)} copy(bf16[8,4,4,24,512]{4,3,2,0,1:T(8,128)(2,1)} %bitcast.43) | data formatting | bytes 6291456 | tf_op jit(solution)/shard_map/transpose | solution.py:52
  (14 shorter events, 0.1 us)
Async XLA Ops:
  7.2 1.7 copy-start
  7.2 95.1 %reduce-scatter.4.cloned.1.call-start = ((), (), s32[]{:S(2)}) async-start(), calls=%async_computation.4 | async-start | bytes 7077888 | tf_op jit(solution)/shard_map/reduce_scatter | solution.py:23
  14.3 88.0 %copy-start.5 = (f32[1,4,512]{2,1,0:T(4,128)S(1)}, f32[1,4,512]{2,1,0:T(4,128)}, u32[]{:S(2)}) copy-start(f32[1,4,512]{2,1,0:T(4,128)} %param.11) | copy-start | bytes 24580
  14.3 119.8 %copy-start.1 = (f32[1,24,512]{2,1,0:T(8,128)S(1)}, f32[1,24,512]{2,1,0:T(8,128)}, u32[]{:S(2)}) copy-start(f32[1,24,512]{2,1,0:T(8,128)} %param.9) | copy-start | bytes 147460
  14.3 119.8 %copy-start.2 = (f32[24,512]{1,0:T(8,128)S(1)}, f32[24,512]{1,0:T(8,128)}, u32[]{:S(2)}) copy-start(f32[24,512]{1,0:T(8,128)} %param.10) | copy-start | bytes 147460
  14.3 152.0 %copy-start.3 = (f32[1,24,512]{2,1,0:T(8,128)S(1)}, f32[1,24,512]{2,1,0:T(8,128)}, u32[]{:S(2)}) copy-start(f32[1,24,512]{2,1,0:T(8,128)} %param.12) | copy-start | bytes 147460
  14.3 152.0 %copy-start.4 = (f32[1,24,512]{2,1,0:T(8,128)S(1)}, f32[1,24,512]{2,1,0:T(8,128)}, u32[]{:S(2)}) copy-start(f32[1,24,512]{2,1,0:T(8,128)} %param.13) | copy-start | bytes 147460
  14.4 119.6 %reduce-scatter.6.cloned.1.call-start = ((), (), s32[]{:S(2)}) async-start(), calls=%async_computation.5 | async-start | bytes 983040 | tf_op jit(solution)/shard_map/reduce_scatter | solution.py:23
  103.0 51.3 %all-to-all-start = ((f32[6,4,512]{2,1,0:T(4,128)}), f32[6,4,512]{2,1,0:T(4,128)S(1)}, u32[]{:S(2)}, u32[]{:S(2)}) async-start(f32[6,4,512]{2,1,0:T(4,128)} %broadcast_in_dim.17), calls=%async_computation | async-start | bytes 98304 | tf_op jit(solution)/shard_map/all_to_all | solution.py:35
  111.7 54.6 %reduce-scatter.8.cloned.1.call-start = ((), (), s32[]{:S(2)}) async-start(), calls=%async_computation.6 | async-start | bytes 245760 | tf_op jit(solution)/shard_map/reduce_scatter | solution.py:23
  134.0 124.0 %all-gather.6.cloned.1.call-start = ((), (), s32[]{:S(2)}) async-start(), calls=%async_computation.7 | async-start | bytes 3932160 | tf_op jit(solution)/shard_map/all_gather | solution.py:49
Sparse Core Ops, SparseCore 0:
  14.5 87.7 reduce-scatter.3
  105.5 28.5 reduce-scatter.5
  137.1 29.1 reduce-scatter.7
  202.2 55.7 all-gather.5
where the time goes:
time: 269 us; the launch traced here: 268 us
  waiting for transfers between devices  178 us (66%)
  blocking collectives  54.4 us (20%)
  between operations  13.8 us (5%)
  starting transfers between devices  8.81 us (3%)
  local copies, waits for them, and re-layouts  6.8 us (3%)
  matrix products  5.5 us (2%)
    reduce_scatter x3, waiting for transfers between devices, summed_rows(): x = lax.psum_scatter(x, axis, scatter_dimension=dim, tiled=True)  122 us
    all_gather x1, waiting for transfers between devices, all_blocks(): blocks = lax.all_gather(blocks, axes[k])  55.3 us
    all_gather x2, blocking collectives, all_blocks(): blocks = lax.all_gather(blocks, axes[k])  34.3 us
    all_gather x1, blocking collectives, gathered_total(): return lax.all_gather(x, axis).sum(0)  20.1 us
    all_to_all x1, starting transfers between devices, sent_to_all(): lax.all_to_all(jnp.broadcast_to(x[None], (devices, *x.shape)), axis, 0, 0...  8.69 us
    dot_general x1, matrix products, per_device(): lax.dot_general(features, cotangent, (((0,), (0,)), ((), ())), preferred_...  5.5 us
  transfers between devices with their start and end apart: 5, of which 4 were waited for; matrix products, arithmetic and copies ran while one was open for 0% of the time, Pallas kernels for 0%

commit v1 on v0

v1 whole, which is shorter than its diff:
```python
import jax
import jax.numpy as jnp
from jax import lax
from jax.sharding import Mesh
from jax.sharding import PartitionSpec as P

DP = ("dp_0", "dp_1", "dp_2")
YZ = ("dp_0", "dp_2")

outer_mu = 0.9
outer_rate = 0.7
beta_one = 0.9
beta_two = 0.95
adam_eps = 1e-08
weight_decay = 0.1
inner_rate = 0.1
correct_one = 1.0 - 0.9**50
correct_two = 1.0 - 0.95**50


def exchanged(x, axes):
    return lax.all_to_all(x, axes, 0, 0, tiled=True)


def per_device(
    layer_input, key_cotangent, local_params, global_params, outer_momentum, adam_first, adam_second
):
    features = layer_input[0]
    cotangent = key_cotangent[0]
    own_local = local_params[0]
    rows, width = global_params.shape
    ny, nx, nz = (lax.axis_size(a) for a in DP)
    replicas = lax.axis_size("replica")
    deltas = global_params - own_local
    sub_rows = outer_momentum.shape[1]
    row_offset = lax.axis_index("replica") * sub_rows
    placed = lax.dynamic_update_slice_in_dim(
        jnp.zeros((rows, width), jnp.float32), outer_momentum[0], row_offset, 0
    )
    both = lax.psum(jnp.concatenate([deltas, placed], 0), "replica")
    outer_grad = both[:rows] / replicas
    momentum_all = outer_mu * both[rows:] + outer_grad
    global_new = global_params - outer_rate * (outer_grad + outer_mu * momentum_all)
    momentum_new = lax.dynamic_slice_in_dim(momentum_all, row_offset, sub_rows, 0)

    term = lax.dot_general(
        features, cotangent, (((0,), (0,)), ((), ())), preferred_element_type=jnp.float32
    ).astype(jnp.float16)
    term = term.reshape(ny, nx, nz * rows, width).transpose(1, 0, 2, 3)
    part = exchanged(term, "dp_1").astype(jnp.float32).sum(0).astype(jnp.float16)
    part = part.reshape(ny * nz, rows, width)
    gradient = exchanged(part, YZ).astype(jnp.float32).sum(0)

    first_new = beta_one * adam_first[0] + (1.0 - beta_one) * gradient
    second_new = beta_two * adam_second[0] + (1.0 - beta_two) * gradient * gradient
    adam_step = (
        first_new / correct_one / (jnp.sqrt(second_new / correct_two) + adam_eps)
        + weight_decay * own_local
    )
    merged = (global_new - inner_rate * adam_step).astype(jnp.bfloat16)
    plane = exchanged(jnp.broadcast_to(merged[None], (ny * nz, rows, width)), YZ)
    cube = exchanged(jnp.broadcast_to(plane[None], (nx, *plane.shape)), "dp_1")
    cube = cube.reshape(nx, ny, nz * rows, width).transpose(1, 0, 2, 3)
    gathered = cube.reshape(-1, width)
    return (gathered[None], global_new, momentum_new[None], first_new[None], second_new[None])


def solution(mesh):
    torus = Mesh(
        mesh.devices.reshape(mesh.shape["replica"], 8, 4, 4), ("replica", "dp_0", "dp_1", "dp_2")
    )
    in_specs = (
        P("replica", DP, None),
        P("replica", DP, None),
        P("replica", DP, None),
        P(DP, None),
        P(DP, "replica", None),
        P("replica", DP, None),
        P("replica", DP, None),
    )
    out_specs = (
        P("replica", None, None),
        P(DP, None),
        P(DP, "replica", None),
        P("replica", DP, None),
        P("replica", DP, None),
    )
    return jax.shard_map(
        per_device, mesh=torus, in_specs=in_specs, out_specs=out_specs, check_vma=False
    )
```

time: 269 us -> 246 us (0.914)
  waiting for transfers between devices: 178 us -> 124 us
  starting transfers between devices: 8.81 us -> 25.1 us
  blocking collectives: 54.4 us -> 64.8 us
  other arithmetic: 1.53 us -> 4.62 us
    reduce_scatter x3 -> x0, waiting for transfers between devices: 122 us -> none  [summed_rows(): x = lax.psum_scatter(x, axis, scatter_dimension=dim, tiled=True)]
    psum x0 -> x1, waiting for transfers between devices: none -> 67.7 us  [per_device(): both = lax.psum(jnp.concatenate([deltas, placed], 0), 'replica')]
    all_to_all x0 -> x2, blocking collectives: none -> 64.8 us  [exchanged(): return lax.all_to_all(x, axes, 0, 0, tiled=True)]
    all_to_all x1 -> x2, waiting for transfers between devices: 0.01 us -> 56.6 us  [exchanged(): return lax.all_to_all(x, axes, 0, 0, tiled=True)]
    all_gather x1 -> x0, waiting for transfers between devices: 55.3 us -> none  [all_blocks(): blocks = lax.all_gather(blocks, axes[k])]
    all_gather x3 -> x0, blocking collectives: 54.4 us -> none  [the longest x2 34.3 us: all_blocks(): blocks = lax.all_gather(blocks, axes[k])]
    all_to_all x1 -> x2, starting transfers between devices: 8.69 us -> 25 us  [exchanged(): return lax.all_to_all(x, axes, 0, 0, tiled=True)]
  transfers between devices with their start and end apart: 5 -> 3, of which waited for: 4 -> 3; matrix products, arithmetic and copies ran while one was open for 0% -> 1% of each run, Pallas kernels for 0% -> 0%
where the time goes in v1:
time: 246 us; the launch traced here: 245 us
  waiting for transfers between devices  124 us (50%)
  blocking collectives  64.8 us (26%)
  starting transfers between devices  25.1 us (10%)
  between operations  14.2 us (6%)
  local copies, waits for them, and re-layouts  9.01 us (4%)
  other arithmetic  4.62 us (2%)
  matrix products  2.83 us (1%)
    psum x1, waiting for transfers between devices, per_device(): both = lax.psum(jnp.concatenate([deltas, placed], 0), 'replica')  67.7 us
    all_to_all x2, blocking collectives, exchanged(): return lax.all_to_all(x, axes, 0, 0, tiled=True)  64.8 us
    all_to_all x2, waiting for transfers between devices, exchanged(): return lax.all_to_all(x, axes, 0, 0, tiled=True)  56.6 us
    all_to_all x2, starting transfers between devices, exchanged(): return lax.all_to_all(x, axes, 0, 0, tiled=True)  25 us
  transfers between devices with their start and end apart: 3, of which 3 were waited for; matrix products, arithmetic and copies ran while one was open for 1% of the time, Pallas kernels for 0%

profile of v1, /device:TPU:1, one launch (start us, length us, event | category | flops | bytes accessed | tf_op | source)
XLA Modules:
  0.0 244.8 jit_solution(15157364884623791971)
XLA Ops:
  7.2 0.0 copy-start
  7.2 1.7 copy-done
  8.8 2.8 %convolution_convert_fusion = f16[3072,512]{1,0:T(8,128)(2,1)S(1)} fusion(bf16[1,384,3072]{2,1,0:T(8,128)(2,1)S(1)} %copy-done, bf16[1,384,512]{2,1,0:T(8,128)(2,1)} %param.8), kind=kOutput, calls=%fused_computation.1 | convolution fusion | flops 1209532416 | bytes 5898240 | tf_op jit(solution)/shard_map/dot_general | solution.py:46
  11.7 0.8 copy.18
  12.5 33.6 %all_to_all.20 = f16[4,8,96,512]{3,2,1,0:T(8,128)(2,1)S(1)} all-to-all(f16[4,8,96,512]{3,2,1,0:T(8,128)(2,1)S(1)} %bitcast.43), channel_id=1, replica_groups=mesh['replica'=6,'dp_0'=8,'dp_1'=4,'dp_2'=4] {'dp_1'}, dimensions={0} | all-to-all | bytes 6291456 | tf_op jit(solution)/shard_map/all_to_all | solution.py:22
  46.1 0.7 convert_reduce_fusion
  46.7 0.0 copy-start.5
  46.8 1.1 convert_element_type.21
  47.9 20.4 %all-to-all-start.1 = ((f16[32,24,512]{2,1,0:T(8,128)(2,1)}), f16[32,24,512]{2,1,0:T(8,128)(2,1)S(1)}, u32[]{:S(2)}, u32[]{:S(2)}) async-start(f16[32,24,512]{2,1,0:T(8,128)(2,1)} %bitcast.46), calls=%async_computation.1 | async-start | bytes 1572864 | tf_op jit(solution)/shard_map/all_to_all | solution.py:22
  68.2 0.0 all-reduce.2.cloned.1.call-start
  68.4 0.6 pad_maximum_fusion
  69.0 0.0 all-reduce.2.cloned.1.call-update
  69.0 20.3 %all-to-all-done.1 = f16[32,24,512]{2,1,0:T(8,128)(2,1)S(1)} async-done(((f16[32,24,512]{2,1,0:T(8,128)(2,1)}), f16[32,24,512]{2,1,0:T(8,128)(2,1)S(1)}, u32[]{:S(2)}, u32[]{:S(2)}) %all-to-all-start.1) | async-done | bytes 786464 | tf_op jit(solution)/shard_map/all_to_all | solution.py:22
  89.3 0.1 convert_reduce_fusion.1
  89.4 67.7 %all-reduce.2.cloned.1.call-done = f32[48,512]{1,0:T(8,128)} async-done(((f32[48,512]{1,0:T(8,128)}), f32[48,512]{1,0:T(8,128)}) %all-reduce.2.cloned.1.call-update) | async-done | bytes 98320 | tf_op jit(solution)/shard_map/psum | solution.py:40
  157.1 1.5 subtract_convert_fusion
  158.6 0.1 broadcast_in_dim.9
  158.7 31.2 %all_to_all.21 = bf16[32,24,512]{2,1,0:T(8,128)(2,1)S(1)} all-to-all(bf16[32,24,512]{2,1,0:T(8,128)(2,1)S(1)} %broadcast_in_dim.9), channel_id=1, replica_groups=mesh['replica'=6,'dp_0'=8,'dp_1'=4,'dp_2'=4] {'dp_0','dp_2'}, dimensions={0} | all-to-all | bytes 1572864 | tf_op jit(solution)/shard_map/all_to_all | solution.py:22
  189.9 1.9 broadcast_in_dim.10
  191.8 4.7 %all-to-all-start.3 = ((bf16[4,32,24,512]{3,2,1,0:T(8,128)(2,1)}), bf16[4,32,24,512]{3,2,1,0:T(8,128)(2,1)}, u32[]{:S(2)}, u32[]{:S(2)}) async-start(bf16[4,32,24,512]{3,2,1,0:T(8,128)(2,1)} %broadcast_in_dim.10), calls=%async_computation.3 | async-start | bytes 6291456 | tf_op jit(solution)/shard_map/all_to_all | solution.py:22
  196.5 0.6 dynamic-slice_bitcast_fusion
  197.1 0.7 fusion.8
  197.7 36.4 %all-to-all-done.3 = bf16[4,32,24,512]{3,2,1,0:T(8,128)(2,1)} async-done(((bf16[4,32,24,512]{3,2,1,0:T(8,128)(2,1)}), bf16[4,32,24,512]{3,2,1,0:T(8,128)(2,1)}, u32[]{:S(2)}, u32[]{:S(2)}) %all-to-all-start.3) | async-done | bytes 3145760 | tf_op jit(solution)/shard_map/all_to_all | solution.py:22
  234.1 3.9 %copy.16 = bf16[8,4,96,512]{3,2,1,0:T(8,128)(2,1)} copy(bf16[8,4,96,512]{3,2,0,1:T(8,128)(2,1)} %bitcast.10) | data formatting | bytes 6291456 | tf_op jit(solution)/shard_map/transpose | solution.py:63
  (12 shorter events, 0.1 us)
Async XLA Ops:
  7.2 1.7 copy-start
  46.7 21.6 %copy-start.5 = (f32[1,4,512]{2,1,0:T(4,128)S(1)}, f32[1,4,512]{2,1,0:T(4,128)}, u32[]{:S(2)}) copy-start(f32[1,4,512]{2,1,0:T(4,128)} %param.11) | copy-start | bytes 24580
  46.8 21.6 %copy-start.1 = (f32[1,24,512]{2,1,0:T(8,128)S(1)}, f32[1,24,512]{2,1,0:T(8,128)}, u32[]{:S(2)}) copy-start(f32[1,24,512]{2,1,0:T(8,128)} %param.9) | copy-start | bytes 147460
  46.8 21.6 %copy-start.2 = (f32[24,512]{1,0:T(8,128)S(1)}, f32[24,512]{1,0:T(8,128)}, u32[]{:S(2)}) copy-start(f32[24,512]{1,0:T(8,128)} %param.10) | copy-start | bytes 147460
  46.8 110.3 %copy-start.3 = (f32[1,24,512]{2,1,0:T(8,128)S(1)}, f32[1,24,512]{2,1,0:T(8,128)}, u32[]{:S(2)}) copy-start(f32[1,24,512]{2,1,0:T(8,128)} %param.13) | copy-start | bytes 147460
  46.8 110.3 %copy-start.4 = (f32[1,24,512]{2,1,0:T(8,128)S(1)}, f32[1,24,512]{2,1,0:T(8,128)}, u32[]{:S(2)}) copy-start(f32[1,24,512]{2,1,0:T(8,128)} %param.12) | copy-start | bytes 147460
  47.9 41.5 %all-to-all-start.1 = ((f16[32,24,512]{2,1,0:T(8,128)(2,1)}), f16[32,24,512]{2,1,0:T(8,128)(2,1)S(1)}, u32[]{:S(2)}, u32[]{:S(2)}) async-start(f16[32,24,512]{2,1,0:T(8,128)(2,1)} %bitcast.46), calls=%async_computation.1 | async-start | bytes 1572864 | tf_op jit(solution)/shard_map/all_to_all | solution.py:22
  68.2 88.9 %all-reduce.2.cloned.1.call-start = ((), (), s32[]{:S(2)}) async-start(), calls=%async_computation.4 | async-start | bytes 196608 | tf_op jit(solution)/shard_map/psum | solution.py:40
  191.8 42.3 %all-to-all-start.3 = ((bf16[4,32,24,512]{3,2,1,0:T(8,128)(2,1)}), bf16[4,32,24,512]{3,2,1,0:T(8,128)(2,1)}, u32[]{:S(2)}, u32[]{:S(2)}) async-start(bf16[4,32,24,512]{3,2,1,0:T(8,128)(2,1)} %broadcast_in_dim.10), calls=%async_computation.3 | async-start | bytes 6291456 | tf_op jit(solution)/shard_map/all_to_all | solution.py:22
Sparse Core Ops, SparseCore 0:
  72.3 84.7 all-reduce.1

commit v2 on v1

v2 whole, which is shorter than its diff:
```python
import jax
import jax.numpy as jnp
from jax import lax
from jax.experimental import pallas as pl
from jax.experimental.pallas import tpu as pltpu
from jax.sharding import Mesh
from jax.sharding import PartitionSpec as P

DP = ("dp_0", "dp_1", "dp_2")
YZ = ("dp_0", "dp_2")
X = "dp_1"
HI, CORE = REPLICA = ("chip", "core")

outer_mu = 0.9
outer_rate = 0.7
beta_one = 0.9
beta_two = 0.95
adam_eps = 1e-08
weight_decay = 0.1
inner_rate = 0.1
correct_one = 1.0 - 0.9**50
correct_two = 1.0 - 0.95**50


def exchanged(x, axes):
    return lax.all_to_all(x, axes, 0, 0, tiled=True)


def copies(x, n):
    return jnp.broadcast_to(x[None], (n, *x.shape))


def total(blocks):
    parts = [b.astype(jnp.float32) for b in blocks]
    while len(parts) > 1:
        parts = [sum(parts[i : i + 2]) for i in range(0, len(parts), 2)]
    return parts[0]


def passed(x, axis, step):
    n = lax.axis_size(axis)
    return lax.ppermute(x, axis, [(i, (i + step) % n) for i in range(n)])


def turned(index, n):
    return index & (n - 1) if n & (n - 1) == 0 else lax.rem(index, n)


def block_of(x, index, dim):
    return lax.dynamic_index_in_dim(x, index, dim, keepdims=False)


def terms_along(x, axis, dim):
    n = lax.axis_size(axis)
    me = lax.axis_index(axis)
    mine = [block_of(x, turned(me + k, n), dim) for k in range(n)]
    return mine[:1] + [passed(mine[k], axis, k) for k in range(1, n)]


def arrived_along(x, axis):
    return [x] + [passed(x, axis, k) for k in range(1, lax.axis_size(axis))]


def placed_along(x, axis):
    n = lax.axis_size(axis)
    me = lax.axis_index(axis)
    blocks = jnp.stack(arrived_along(x, axis))
    return jnp.stack([block_of(blocks, turned(me + n - i, n), 0) for i in range(n)])


def joining(me_ref, *refs):
    *near, far, out = refs
    places = len(near)
    for k, ref in enumerate(near):
        x = turned(me_ref[0] + places - k, places)
        both = jnp.concatenate(
            [ref[0].astype(jnp.float32), far[0, :, x].astype(jnp.float32)], axis=1
        )
        piece = both.reshape(-1, both.shape[-1]).astype(out.dtype)
        start = pl.multiple_of(x * piece.shape[0], piece.shape[0])
        out[pl.ds(start, piece.shape[0]), :] = piece


def joined(near, far, me):
    ny, nz, cut, width = near[0].shape
    nx, rest = far.shape[2:4]
    block = nx * nz * (cut + rest)
    return pl.pallas_call(
        joining,
        grid_spec=pltpu.PrefetchScalarGridSpec(
            num_scalar_prefetch=1,
            grid=(ny,),
            in_specs=[pl.BlockSpec((1, nz, cut, width), lambda y, m: (y, 0, 0, 0))] * nx
            + [pl.BlockSpec((1, nz, nx, rest, width), lambda y, m: (y, 0, 0, 0, 0))],
            out_specs=pl.BlockSpec((block, width), lambda y, m: (y, 0)),
        ),
        out_shape=jax.ShapeDtypeStruct((ny * block, width), far.dtype),
        compiler_params=pltpu.CompilerParams(vmem_limit_bytes=16 * 2**20),
        name="joined",
    )(me.reshape(1), *near, far)


def per_device(
    layer_input, key_cotangent, local_params, global_params, outer_momentum, adam_first, adam_second
):
    features = layer_input[0]
    cotangent = key_cotangent[0]
    own_local = local_params[0]
    rows, width = global_params.shape
    ny, nx, nz = (lax.axis_size(a) for a in DP)
    plane = ny * nz
    n_hi, n_core = lax.axis_size(HI), lax.axis_size(CORE)
    replicas = n_hi * n_core
    sub_rows = outer_momentum.shape[1]
    cut = rows * 2 // 3

    core = lax.axis_index(CORE)
    hi = lax.axis_index(HI)
    deltas = global_params - own_local
    mine = jnp.concatenate([deltas, outer_momentum[0]], 0)
    other = passed(mine, CORE, 1)
    first, second = jnp.where(core == 0, mine, other), jnp.where(core == 0, other, mine)
    pair = jnp.concatenate([mine[:rows] + other[:rows], first[rows:], second[rows:]], 0)
    by_chip = placed_along(pair, HI)
    outer_grad = sum(p[:rows] for p in by_chip) / replicas
    old_rows = jnp.concatenate([p[rows:] for p in by_chip], 0)
    momentum_all = outer_mu * old_rows + outer_grad
    global_new = global_params - outer_rate * (outer_grad + outer_mu * momentum_all)
    momentum_new = lax.dynamic_slice_in_dim(
        momentum_all, (hi * n_core + core) * sub_rows, sub_rows, 0
    )

    term = lax.dot_general(
        features, cotangent, (((0,), (0,)), ((), ())), preferred_element_type=jnp.float32
    ).astype(jnp.float16)
    term = term.reshape(ny, nx, nz, rows, width)
    term_b = term[:, :, :, cut:].transpose(0, 2, 1, 3, 4).reshape(plane, nx, rows - cut, width)
    got_a = terms_along(term[:, :, :, :cut], X, 1)
    got_b = exchanged(term_b, YZ)

    part_a, part_b = lax.optimization_barrier(
        (total(got_a).astype(jnp.float16).reshape(plane, cut, width), total(got_b).astype(jnp.float16))
    )
    sum_a = exchanged(part_a, YZ)
    sum_b = terms_along(part_b, X, 0)

    def stepped(gradient, lo, hi):
        first_new = beta_one * adam_first[0, lo:hi] + (1.0 - beta_one) * gradient
        second_new = beta_two * adam_second[0, lo:hi] + (1.0 - beta_two) * gradient * gradient
        adam_step = (
            first_new / correct_one / (jnp.sqrt(second_new / correct_two) + adam_eps)
            + weight_decay * own_local[lo:hi]
        )
        merged = (global_new[lo:hi] - inner_rate * adam_step).astype(jnp.bfloat16)
        return merged, first_new, second_new

    merged_a, first_a, second_a = stepped(total(sum_a), 0, cut)
    merged_b, first_b, second_b = stepped(total(sum_b), cut, rows)
    near_b = placed_along(merged_b, X)
    near_a, near_b = lax.optimization_barrier((exchanged(copies(merged_a, plane), YZ), near_b))
    all_a = [n.reshape(ny, nz, cut, width) for n in arrived_along(near_a, X)]
    all_b = exchanged(copies(near_b, plane), YZ).reshape(ny, nz, nx, rows - cut, width)
    gathered = joined(all_a, all_b, lax.axis_index(X))
    first_new = jnp.concatenate([first_a, first_b], 0)
    second_new = jnp.concatenate([second_a, second_b], 0)
    return (gathered[None], global_new, momentum_new[None], first_new[None], second_new[None])


def solution(mesh):
    torus = Mesh(
        mesh.devices.reshape(mesh.shape["replica"] // 2, 2, 8, 4, 4), REPLICA + DP
    )
    in_specs = (
        P(REPLICA, DP, None),
        P(REPLICA, DP, None),
        P(REPLICA, DP, None),
        P(DP, None),
        P(DP, REPLICA, None),
        P(REPLICA, DP, None),
        P(REPLICA, DP, None),
    )
    out_specs = (
        P(REPLICA, None, None),
        P(DP, None),
        P(DP, REPLICA, None),
        P(REPLICA, DP, None),
        P(REPLICA, DP, None),
    )
    return jax.shard_map(
        per_device, mesh=torus, in_specs=in_specs, out_specs=out_specs, check_vma=False
    )
```

time: 246 us -> 182 us (0.74)
  the two profiles are of different devices: /device:TPU:1 before, /device:TPU:8 now
where the time goes in v2:
time: 182 us; the launch traced here: 180 us
  starting transfers between devices  98.1 us (54%)
  waiting for transfers between devices  49 us (27%)
  local copies, waits for them, and re-layouts  14.5 us (8%)
  other arithmetic  8.57 us (5%)
  Pallas kernels  5.69 us (3%)
  matrix products  2.83 us (2%)
    ppermute x15, starting transfers between devices, passed(): return lax.ppermute(x, axis, [(i, (i + step) % n) for i in range(n)])  54.7 us
    ppermute x15, waiting for transfers between devices, passed(): return lax.ppermute(x, axis, [(i, (i + step) % n) for i in range(n)])  49 us
    all_to_all x4, starting transfers between devices, exchanged(): return lax.all_to_all(x, axes, 0, 0, tiled=True)  43.4 us
    pallas_call x1, Pallas kernels, joined(): pl.pallas_call(joining, grid_spec=pltpu.PrefetchScalarGridSpec(num_scalar...  5.69 us
    slice x1, local copies, waits for them, and re-layouts, per_device(): got_a = terms_along(term[:, :, :, :cut], X, 1)  3.65 us
  transfers between devices with their start and end apart: 19, of which 11 were waited for; matrix products, arithmetic and copies ran while one was open for 8% of the time, Pallas kernels for 0%

profile of v2, /device:TPU:8, one launch (start us, length us, event | category | flops | bytes accessed | tf_op | source)
XLA Modules:
  0.0 179.7 jit_solution(2992480449448454105)
XLA Ops:
  7.1 13.1 %all-to-all-start = ((f16[32,4,8,512]{3,2,1,0:T(8,128)(2,1)}), f16[32,4,8,512]{3,2,1,0:T(8,128)(2,1)S(1)}, u32[]{:S(2)}, u32[]{:S(2)}) async-start(f16[32,4,8,512]{3,2,1,0:T(8,128)(2,1)} %bitcast.103), calls=%async_computation | async-start | bytes 2097152 | tf_op jit(solution)/shard_map/all_to_all | solution.py:26
  20.3 3.7 %slice.101 = f16[8,4,4,16,512]{4,3,2,1,0:T(8,128)(2,1)} slice(f16[8,4,4,24,512]{4,3,2,1,0:T(8,128)(2,1)} %bitcast.106), slice={[0:8], [0:4], [0:4], [0:16], [0:512]} | slice | bytes 4194304 | tf_op jit(solution)/shard_map/slice | solution.py:138
  26.7 3.4 %collective-permute-start.3 = (f16[8,4,16,512]{3,2,1,0:T(8,128)(2,1)}, f16[8,4,16,512]{3,2,1,0:T(8,128)(2,1)}, u32[]{:S(2)}, u32[]{:S(2)}) collective-permute-start(f16[8,4,16,512]{3,2,1,0:T(8,128)(2,1)} %get-tuple-element.21), channel_id=1, source_target_pairs={{0,4},{4,8},{8,12},{12,0},{1,5},{5,9},{9,13},{13,1},{2,6},{6,10},{... | collective-permute-start | bytes 1572872 | tf_op jit(solution)/shard_map/ppermute | solution.py:42
  30.1 3.7 %collective-permute-start.5 = (f16[8,4,16,512]{3,2,1,0:T(8,128)(2,1)}, f16[8,4,16,512]{3,2,1,0:T(8,128)(2,1)}, u32[]{:S(2)}, u32[]{:S(2)}) collective-permute-start(f16[8,4,16,512]{3,2,1,0:T(8,128)(2,1)} %get-tuple-element.22), channel_id=1, source_target_pairs={{0,12},{4,0},{8,4},{12,8},{1,13},{5,1},{9,5},{13,9},{2,14},{6,2},{... | collective-permute-start | bytes 1572872 | tf_op jit(solution)/shard_map/ppermute | solution.py:42
  33.7 3.7 %collective-permute-start.4 = (f16[8,4,16,512]{3,2,1,0:T(8,128)(2,1)}, f16[8,4,16,512]{3,2,1,0:T(8,128)(2,1)}, u32[]{:S(2)}, u32[]{:S(2)}) collective-permute-start(f16[8,4,16,512]{3,2,1,0:T(8,128)(2,1)} %get-tuple-element.23), channel_id=1, source_target_pairs={{0,8},{4,12},{8,0},{12,4},{1,9},{5,13},{9,1},{13,5},{2,10},{6,14},... | collective-permute-start | bytes 1572872 | tf_op jit(solution)/shard_map/ppermute | solution.py:42
  37.5 6.5 %collective-permute-done.3 = f16[8,4,16,512]{3,2,1,0:T(8,128)(2,1)} collective-permute-done((f16[8,4,16,512]{3,2,1,0:T(8,128)(2,1)}, f16[8,4,16,512]{3,2,1,0:T(8,128)(2,1)}, u32[]{:S(2)}, u32[]{:S(2)}) %collective-permute-start.3) | collective-permute-done | bytes 524320 | tf_op jit(solution)/shard_map/ppermute | solution.py:42
  44.0 11.7 %collective-permute-done.5 = f16[8,4,16,512]{3,2,1,0:T(8,128)(2,1)} collective-permute-done((f16[8,4,16,512]{3,2,1,0:T(8,128)(2,1)}, f16[8,4,16,512]{3,2,1,0:T(8,128)(2,1)}, u32[]{:S(2)}, u32[]{:S(2)}) %collective-permute-start.5) | collective-permute-done | bytes 524320 | tf_op jit(solution)/shard_map/ppermute | solution.py:42
  59.2 10.2 %all-to-all-start.1 = ((f16[32,16,512]{2,1,0:T(8,128)(2,1)}), f16[32,16,512]{2,1,0:T(8,128)(2,1)S(1)}, u32[]{:S(2)}, u32[]{:S(2)}) async-start(f16[32,16,512]{2,1,0:T(8,128)(2,1)} %bitcast.107), calls=%async_computation.1 | async-start | bytes 1048576 | tf_op jit(solution)/shard_map/all_to_all | solution.py:26
  72.7 10.6 %collective-permute-start.1 = (f32[32,512]{1,0:T(8,128)S(1)}, f32[32,512]{1,0:T(8,128)S(1)}, u32[]{:S(2)}, u32[]{:S(2)}) collective-permute-start(f32[32,512]{1,0:T(8,128)S(1)} %get-tuple-element.30), channel_id=1, source_target_pairs={{0,256},{256,512},{512,0},{1,257},{257,513},{513,1},{2,258},{258,5... | collective-permute-start | bytes 196616 | tf_op jit(solution)/shard_map/ppermute | solution.py:42
  83.3 3.2 %collective-permute-start.2 = (f32[32,512]{1,0:T(8,128)S(1)}, f32[32,512]{1,0:T(8,128)S(1)}, u32[]{:S(2)}, u32[]{:S(2)}) collective-permute-start(f32[32,512]{1,0:T(8,128)S(1)} %get-tuple-element.30), channel_id=1, source_target_pairs={{0,512},{256,0},{512,256},{1,513},{257,1},{513,257},{2,514},{258,2... | collective-permute-start | bytes 196616 | tf_op jit(solution)/shard_map/ppermute | solution.py:42
  87.7 8.0 %collective-permute-done.2 = f32[32,512]{1,0:T(8,128)S(1)} collective-permute-done((f32[32,512]{1,0:T(8,128)S(1)}, f32[32,512]{1,0:T(8,128)S(1)}, u32[]{:S(2)}, u32[]{:S(2)}) %collective-permute-start.2) | collective-permute-done | bytes 65568 | tf_op jit(solution)/shard_map/ppermute | solution.py:42
  98.9 10.0 %all-to-all-start.2 = ((bf16[32,16,512]{2,1,0:T(8,128)(2,1)}), bf16[32,16,512]{2,1,0:T(8,128)(2,1)S(1)}, u32[]{:S(2)}, u32[]{:S(2)}) async-start(bf16[32,16,512]{2,1,0:T(8,128)(2,1)} %broadcast_in_dim.24), calls=%async_computation.2 | async-start | bytes 1048576 | tf_op jit(solution)/shard_map/all_to_all | solution.py:26
  108.9 4.7 %collective-permute-start.6 = (f16[8,512]{1,0:T(8,128)(2,1)S(1)}, f16[8,512]{1,0:T(8,128)(2,1)S(1)}, u32[]{:S(2)}, u32[]{:S(2)}) collective-permute-start(f16[8,512]{1,0:T(8,128)(2,1)S(1)} %get-tuple-element.35), channel_id=1, source_target_pairs={{0,4},{4,8},{8,12},{12,0},{1,5},{5,9},{9,13},{13,1},{2,6},{6,10},{... | collective-permute-start | bytes 24584 | tf_op jit(solution)/shard_map/ppermute | solution.py:42
  116.4 3.4 %collective-permute-start.7 = (f16[8,512]{1,0:T(8,128)(2,1)S(1)}, f16[8,512]{1,0:T(8,128)(2,1)S(1)}, u32[]{:S(2)}, u32[]{:S(2)}) collective-permute-start(f16[8,512]{1,0:T(8,128)(2,1)S(1)} %get-tuple-element.37), channel_id=1, source_target_pairs={{0,8},{4,12},{8,0},{12,4},{1,9},{5,13},{9,1},{13,5},{2,10},{6,14},... | collective-permute-start | bytes 24584 | tf_op jit(solution)/shard_map/ppermute | solution.py:42
  119.8 3.6 %collective-permute-done.7 = f16[8,512]{1,0:T(8,128)(2,1)S(1)} collective-permute-done((f16[8,512]{1,0:T(8,128)(2,1)S(1)}, f16[8,512]{1,0:T(8,128)(2,1)S(1)}, u32[]{:S(2)}, u32[]{:S(2)}) %collective-permute-start.7) | collective-permute-done | bytes 8224 | tf_op jit(solution)/shard_map/ppermute | solution.py:42
  124.8 4.0 %collective-permute-start.11 = (bf16[8,512]{1,0:T(8,128)(2,1)S(1)}, bf16[8,512]{1,0:T(8,128)(2,1)S(1)}, u32[]{:S(2)}, u32[]{:S(2)}) collective-permute-start(bf16[8,512]{1,0:T(8,128)(2,1)S(1)} %get-tuple-element.15), channel_id=1, source_target_pairs={{0,12},{4,0},{8,4},{12,8},{1,13},{5,1},{9,5},{13,9},{2,14},{6,2},{... | collective-permute-start | bytes 24584 | tf_op jit(solution)/shard_map/ppermute | solution.py:42
  128.9 3.1 %collective-permute-start.10 = (bf16[8,512]{1,0:T(8,128)(2,1)S(1)}, bf16[8,512]{1,0:T(8,128)(2,1)S(1)}, u32[]{:S(2)}, u32[]{:S(2)}) collective-permute-start(bf16[8,512]{1,0:T(8,128)(2,1)S(1)} %get-tuple-element.15), channel_id=1, source_target_pairs={{0,8},{4,12},{8,0},{12,4},{1,9},{5,13},{9,1},{13,5},{2,10},{6,14},... | collective-permute-start | bytes 24584 | tf_op jit(solution)/shard_map/ppermute | solution.py:42
  135.9 2.9 %collective-permute-done.9 = bf16[8,512]{1,0:T(8,128)(2,1)S(1)} collective-permute-done((bf16[8,512]{1,0:T(8,128)(2,1)S(1)}, bf16[8,512]{1,0:T(8,128)(2,1)S(1)}, u32[]{:S(2)}, u32[]{:S(2)}) %collective-permute-start.9) | collective-permute-done | bytes 8224 | tf_op jit(solution)/shard_map/ppermute | solution.py:42
  140.0 10.1 %all-to-all-start.3 = ((bf16[32,4,8,512]{3,2,1,0:T(8,128)(2,1)}), bf16[32,4,8,512]{3,2,1,0:T(8,128)(2,1)S(1)}, u32[]{:S(2)}, u32[]{:S(2)}) async-start(bf16[32,4,8,512]{3,2,1,0:T(8,128)(2,1)} %broadcast_in_dim.25), calls=%async_computation.3 | async-start | bytes 2097152 | tf_op jit(solution)/shard_map/all_to_all | solution.py:26
  155.0 3.3 %collective-permute-start.12 = (bf16[32,16,512]{2,1,0:T(8,128)(2,1)}, bf16[32,16,512]{2,1,0:T(8,128)(2,1)}, u32[]{:S(2)}, u32[]{:S(2)}) collective-permute-start(bf16[32,16,512]{2,1,0:T(8,128)(2,1)} %copy-done.1), channel_id=1, source_target_pairs={{0,4},{4,8},{8,12},{12,0},{1,5},{5,9},{9,13},{13,1},{2,6},{6,10},{... | collective-permute-start | bytes 1572872 | tf_op jit(solution)/shard_map/ppermute | solution.py:42
  161.1 2.9 %collective-permute-done.14 = bf16[32,16,512]{2,1,0:T(8,128)(2,1)} collective-permute-done((bf16[32,16,512]{2,1,0:T(8,128)(2,1)}, bf16[32,16,512]{2,1,0:T(8,128)(2,1)}, u32[]{:S(2)}, u32[]{:S(2)}) %collective-permute-start.14) | collective-permute-done | bytes 524320 | tf_op jit(solution)/shard_map/ppermute | solution.py:42
  163.9 3.6 %collective-permute-done.13 = bf16[32,16,512]{2,1,0:T(8,128)(2,1)} collective-permute-done((bf16[32,16,512]{2,1,0:T(8,128)(2,1)}, bf16[32,16,512]{2,1,0:T(8,128)(2,1)}, u32[]{:S(2)}, u32[]{:S(2)}) %collective-permute-start.13) | collective-permute-done | bytes 524320 | tf_op jit(solution)/shard_map/ppermute | solution.py:42
  167.5 5.5 %collective-permute-done.12 = bf16[32,16,512]{2,1,0:T(8,128)(2,1)} collective-permute-done((bf16[32,16,512]{2,1,0:T(8,128)(2,1)}, bf16[32,16,512]{2,1,0:T(8,128)(2,1)}, u32[]{:S(2)}, u32[]{:S(2)}) %collective-permute-start.12) | collective-permute-done | bytes 524320 | tf_op jit(solution)/shard_map/ppermute | solution.py:42
  174.0 5.7 %joined.1 = bf16[3072,512]{1,0:T(8,128)(2,1)} custom-call(s32[1]{0:T(128)} %bitcast.me_ref, bf16[8,4,16,512]{3,2,1,0:T(8,128)(2,1)S(1)} %bitcast.102, bf16[8,4,16,512]{3,2,1,0:T(8,128)(2,1)} %bitcast.37.refs_1_, bf16[8,4,16,512]{3,2,1,0:T(8,128)(2,1)} %bitcast.38.refs_2_, bf16[8,4,16,512]{3,2,1,0:T(8,128)(2,1)} %bitcast.39.refs_3_, ...), custom_call_target="tpu_custom_call" | custom-call | tf_op jit(solution)/shard_map/joined/pallas_call | solution.py:88
  (61 shorter events, 38.1 us)
Async XLA Ops:
  7.1 51.3 %all-to-all-start = ((f16[32,4,8,512]{3,2,1,0:T(8,128)(2,1)}), f16[32,4,8,512]{3,2,1,0:T(8,128)(2,1)S(1)}, u32[]{:S(2)}, u32[]{:S(2)}) async-start(f16[32,4,8,512]{3,2,1,0:T(8,128)(2,1)} %bitcast.103), calls=%async_computation | async-start | bytes 2097152 | tf_op jit(solution)/shard_map/all_to_all | solution.py:26
  26.7 17.3 %collective-permute-start.3 = (f16[8,4,16,512]{3,2,1,0:T(8,128)(2,1)}, f16[8,4,16,512]{3,2,1,0:T(8,128)(2,1)}, u32[]{:S(2)}, u32[]{:S(2)}) collective-permute-start(f16[8,4,16,512]{3,2,1,0:T(8,128)(2,1)} %get-tuple-element.21), channel_id=1, source_target_pairs={{0,4},{4,8},{8,12},{12,0},{1,5},{5,9},{9,13},{13,1},{2,6},{6,10},{... | collective-permute-start | bytes 1572872 | tf_op jit(solution)/shard_map/ppermute | solution.py:42
  30.1 25.6 %collective-permute-start.5 = (f16[8,4,16,512]{3,2,1,0:T(8,128)(2,1)}, f16[8,4,16,512]{3,2,1,0:T(8,128)(2,1)}, u32[]{:S(2)}, u32[]{:S(2)}) collective-permute-start(f16[8,4,16,512]{3,2,1,0:T(8,128)(2,1)} %get-tuple-element.22), channel_id=1, source_target_pairs={{0,12},{4,0},{8,4},{12,8},{1,13},{5,1},{9,5},{13,9},{2,14},{6,2},{... | collective-permute-start | bytes 1572872 | tf_op jit(solution)/shard_map/ppermute | solution.py:42
  33.7 21.9 %collective-permute-start.4 = (f16[8,4,16,512]{3,2,1,0:T(8,128)(2,1)}, f16[8,4,16,512]{3,2,1,0:T(8,128)(2,1)}, u32[]{:S(2)}, u32[]{:S(2)}) collective-permute-start(f16[8,4,16,512]{3,2,1,0:T(8,128)(2,1)} %get-tuple-element.23), channel_id=1, source_target_pairs={{0,8},{4,12},{8,0},{12,4},{1,9},{5,13},{9,1},{13,5},{2,10},{6,14},... | collective-permute-start | bytes 1572872 | tf_op jit(solution)/shard_map/ppermute | solution.py:42
  37.5 32.0 %copy-start.4 = (f32[1,24,512]{2,1,0:T(8,128)S(1)}, f32[1,24,512]{2,1,0:T(8,128)}, u32[]{:S(2)}) copy-start(f32[1,24,512]{2,1,0:T(8,128)} %param.9) | copy-start | bytes 147460
  37.5 32.0 %copy-start.9 = (f32[1,4,512]{2,1,0:T(4,128)S(1)}, f32[1,4,512]{2,1,0:T(4,128)}, u32[]{:S(2)}) copy-start(f32[1,4,512]{2,1,0:T(4,128)} %param.11) | copy-start | bytes 24580
  59.2 49.7 %copy-start.7 = (f16[4,8,512]{2,1,0:T(8,128)(2,1)S(1)}, f16[4,8,512]{2,1,0:T(8,128)(2,1)}, u32[]{:S(2)}) copy-start(f16[4,8,512]{2,1,0:T(8,128)(2,1)} %fusion.11) | copy-start | bytes 98308
  59.2 37.3 %all-to-all-start.1 = ((f16[32,16,512]{2,1,0:T(8,128)(2,1)}), f16[32,16,512]{2,1,0:T(8,128)(2,1)S(1)}, u32[]{:S(2)}, u32[]{:S(2)}) async-start(f16[32,16,512]{2,1,0:T(8,128)(2,1)} %bitcast.107), calls=%async_computation.1 | async-start | bytes 1048576 | tf_op jit(solution)/shard_map/all_to_all | solution.py:26
  69.5 3.1 %collective-permute-start = (f32[28,512]{1,0:T(8,128)S(1)}, f32[28,512]{1,0:T(8,128)S(1)}, u32[]{:S(2)}, u32[]{:S(2)}) collective-permute-start(f32[28,512]{1,0:T(8,128)S(1)} %pad_maximum_fusion.1), channel_id=1, source_target_pairs={{0,128},{128,0},{1,129},{129,1},{2,130},{130,2},{3,131},{131,3},{4... | collective-permute-start | bytes 172040 | tf_op jit(solution)/shard_map/ppermute | solution.py:42
  72.7 15.0 %collective-permute-start.1 = (f32[32,512]{1,0:T(8,128)S(1)}, f32[32,512]{1,0:T(8,128)S(1)}, u32[]{:S(2)}, u32[]{:S(2)}) collective-permute-start(f32[32,512]{1,0:T(8,128)S(1)} %get-tuple-element.30), channel_id=1, source_target_pairs={{0,256},{256,512},{512,0},{1,257},{257,513},{513,1},{2,258},{258,5... | collective-permute-start | bytes 196616 | tf_op jit(solution)/shard_map/ppermute | solution.py:42
  83.3 12.5 %collective-permute-start.2 = (f32[32,512]{1,0:T(8,128)S(1)}, f32[32,512]{1,0:T(8,128)S(1)}, u32[]{:S(2)}, u32[]{:S(2)}) collective-permute-start(f32[32,512]{1,0:T(8,128)S(1)} %get-tuple-element.30), channel_id=1, source_target_pairs={{0,512},{256,0},{512,256},{1,513},{257,1},{513,257},{2,514},{258,2... | collective-permute-start | bytes 196616 | tf_op jit(solution)/shard_map/ppermute | solution.py:42
  96.5 43.5 %copy-start.5 = (f32[24,512]{1,0:T(8,128)}, f32[24,512]{1,0:T(8,128)S(1)}, u32[]{:S(2)}) copy-start(f32[24,512]{1,0:T(8,128)S(1)} %multiply_subtract_fusion) | copy-start | bytes 147460
  98.9 40.0 %all-to-all-start.2 = ((bf16[32,16,512]{2,1,0:T(8,128)(2,1)}), bf16[32,16,512]{2,1,0:T(8,128)(2,1)S(1)}, u32[]{:S(2)}, u32[]{:S(2)}) async-start(bf16[32,16,512]{2,1,0:T(8,128)(2,1)} %broadcast_in_dim.24), calls=%async_computation.2 | async-start | bytes 1048576 | tf_op jit(solution)/shard_map/all_to_all | solution.py:26
  108.9 10.9 %collective-permute-start.6 = (f16[8,512]{1,0:T(8,128)(2,1)S(1)}, f16[8,512]{1,0:T(8,128)(2,1)S(1)}, u32[]{:S(2)}, u32[]{:S(2)}) collective-permute-start(f16[8,512]{1,0:T(8,128)(2,1)S(1)} %get-tuple-element.35), channel_id=1, source_target_pairs={{0,4},{4,8},{8,12},{12,0},{1,5},{5,9},{9,13},{13,1},{2,6},{6,10},{... | collective-permute-start | bytes 24584 | tf_op jit(solution)/shard_map/ppermute | solution.py:42
  113.7 6.2 %collective-permute-start.8 = (f16[8,512]{1,0:T(8,128)(2,1)S(1)}, f16[8,512]{1,0:T(8,128)(2,1)S(1)}, u32[]{:S(2)}, u32[]{:S(2)}) collective-permute-start(f16[8,512]{1,0:T(8,128)(2,1)S(1)} %get-tuple-element.36), channel_id=1, source_target_pairs={{0,12},{4,0},{8,4},{12,8},{1,13},{5,1},{9,5},{13,9},{2,14},{6,2},{... | collective-permute-start | bytes 24584 | tf_op jit(solution)/shard_map/ppermute | solution.py:42
  116.4 7.0 %collective-permute-start.7 = (f16[8,512]{1,0:T(8,128)(2,1)S(1)}, f16[8,512]{1,0:T(8,128)(2,1)S(1)}, u32[]{:S(2)}, u32[]{:S(2)}) collective-permute-start(f16[8,512]{1,0:T(8,128)(2,1)S(1)} %get-tuple-element.37), channel_id=1, source_target_pairs={{0,8},{4,12},{8,0},{12,4},{1,9},{5,13},{9,1},{13,5},{2,10},{6,14},... | collective-permute-start | bytes 24584 | tf_op jit(solution)/shard_map/ppermute | solution.py:42
  124.8 34.8 %copy-start.8 = (f32[8,512]{1,0:T(8,128)S(1)}, f32[8,512]{1,0:T(8,128)}, u32[]{:S(2)}) copy-start(f32[8,512]{1,0:T(8,128)} %get-tuple-element.17) | copy-start | bytes 49156
  124.8 9.1 %collective-permute-start.11 = (bf16[8,512]{1,0:T(8,128)(2,1)S(1)}, bf16[8,512]{1,0:T(8,128)(2,1)S(1)}, u32[]{:S(2)}, u32[]{:S(2)}) collective-permute-start(bf16[8,512]{1,0:T(8,128)(2,1)S(1)} %get-tuple-element.15), channel_id=1, source_target_pairs={{0,12},{4,0},{8,4},{12,8},{1,13},{5,1},{9,5},{13,9},{2,14},{6,2},{... | collective-permute-start | bytes 24584 | tf_op jit(solution)/shard_map/ppermute | solution.py:42
  128.9 7.0 %collective-permute-start.10 = (bf16[8,512]{1,0:T(8,128)(2,1)S(1)}, bf16[8,512]{1,0:T(8,128)(2,1)S(1)}, u32[]{:S(2)}, u32[]{:S(2)}) collective-permute-start(bf16[8,512]{1,0:T(8,128)(2,1)S(1)} %get-tuple-element.15), channel_id=1, source_target_pairs={{0,8},{4,12},{8,0},{12,4},{1,9},{5,13},{9,1},{13,5},{2,10},{6,14},... | collective-permute-start | bytes 24584 | tf_op jit(solution)/shard_map/ppermute | solution.py:42
  132.0 6.8 %collective-permute-start.9 = (bf16[8,512]{1,0:T(8,128)(2,1)S(1)}, bf16[8,512]{1,0:T(8,128)(2,1)S(1)}, u32[]{:S(2)}, u32[]{:S(2)}) collective-permute-start(bf16[8,512]{1,0:T(8,128)(2,1)S(1)} %get-tuple-element.15), channel_id=1, source_target_pairs={{0,4},{4,8},{8,12},{12,0},{1,5},{5,9},{9,13},{13,1},{2,6},{6,10},{... | collective-permute-start | bytes 24584 | tf_op jit(solution)/shard_map/ppermute | solution.py:42
  140.0 33.0 %all-to-all-start.3 = ((bf16[32,4,8,512]{3,2,1,0:T(8,128)(2,1)}), bf16[32,4,8,512]{3,2,1,0:T(8,128)(2,1)S(1)}, u32[]{:S(2)}, u32[]{:S(2)}) async-start(bf16[32,4,8,512]{3,2,1,0:T(8,128)(2,1)} %broadcast_in_dim.25), calls=%async_computation.3 | async-start | bytes 2097152 | tf_op jit(solution)/shard_map/all_to_all | solution.py:26
  150.1 13.8 %collective-permute-start.14 = (bf16[32,16,512]{2,1,0:T(8,128)(2,1)}, bf16[32,16,512]{2,1,0:T(8,128)(2,1)}, u32[]{:S(2)}, u32[]{:S(2)}) collective-permute-start(bf16[32,16,512]{2,1,0:T(8,128)(2,1)} %copy-done.1), channel_id=1, source_target_pairs={{0,12},{4,0},{8,4},{12,8},{1,13},{5,1},{9,5},{13,9},{2,14},{6,2},{... | collective-permute-start | bytes 1572872 | tf_op jit(solution)/shard_map/ppermute | solution.py:42
  152.2 15.3 %collective-permute-start.13 = (bf16[32,16,512]{2,1,0:T(8,128)(2,1)}, bf16[32,16,512]{2,1,0:T(8,128)(2,1)}, u32[]{:S(2)}, u32[]{:S(2)}) collective-permute-start(bf16[32,16,512]{2,1,0:T(8,128)(2,1)} %copy-done.1), channel_id=1, source_target_pairs={{0,8},{4,12},{8,0},{12,4},{1,9},{5,13},{9,1},{13,5},{2,10},{6,14},... | collective-permute-start | bytes 1572872 | tf_op jit(solution)/shard_map/ppermute | solution.py:42
  155.0 18.0 %collective-permute-start.12 = (bf16[32,16,512]{2,1,0:T(8,128)(2,1)}, bf16[32,16,512]{2,1,0:T(8,128)(2,1)}, u32[]{:S(2)}, u32[]{:S(2)}) collective-permute-start(bf16[32,16,512]{2,1,0:T(8,128)(2,1)} %copy-done.1), channel_id=1, source_target_pairs={{0,4},{4,8},{8,12},{12,0},{1,5},{5,9},{9,13},{13,1},{2,6},{6,10},{... | collective-permute-start | bytes 1572872 | tf_op jit(solution)/shard_map/ppermute | solution.py:42
  (5 other events, 37.8 us)

commit v3 on v2

--- a/solution.py
+++ b/solution.py
@@ -50,10 +50,18 @@
     return lax.dynamic_index_in_dim(x, index, dim, keepdims=False)
 
 
-def terms_along(x, axis, dim):
+def terms_along(x, axis, dim, cut):
     n = lax.axis_size(axis)
     me = lax.axis_index(axis)
-    mine = [block_of(x, turned(me + k, n), dim) for k in range(n)]
+    sizes = list(x.shape)
+    sizes[dim], sizes[-2] = 1, cut
+
+    def block(index):
+        starts = [0] * x.ndim
+        starts[dim] = index
+        return lax.dynamic_slice(x, starts, sizes)
+
+    mine = [block(turned(me + k, n)) for k in range(n)]
     return mine[:1] + [passed(mine[k], axis, k) for k in range(1, n)]
 
 
@@ -73,29 +81,31 @@
     places = len(near)
     for k, ref in enumerate(near):
         x = turned(me_ref[0] + places - k, places)
-        both = jnp.concatenate(
-            [ref[0].astype(jnp.float32), far[0, :, x].astype(jnp.float32)], axis=1
-        )
-        piece = both.reshape(-1, both.shape[-1]).astype(out.dtype)
-        start = pl.multiple_of(x * piece.shape[0], piece.shape[0])
-        out[pl.ds(start, piece.shape[0]), :] = piece
+        for y in range(ref.shape[0]):
+            both = jnp.concatenate(
+                [ref[y].astype(jnp.float32), far[y, :, x].astype(jnp.float32)], axis=1
+            )
+            piece = both.reshape(-1, both.shape[-1]).astype(out.dtype)
+            start = pl.multiple_of((x + y * places) * piece.shape[0], piece.shape[0])
+            out[pl.ds(start, piece.shape[0]), :] = piece
 
 
 def joined(near, far, me):
     ny, nz, cut, width = near[0].shape
     nx, rest = far.shape[2:4]
-    block = nx * nz * (cut + rest)
+    step = 2
+    block = step * nx * nz * (cut + rest)
     return pl.pallas_call(
         joining,
         grid_spec=pltpu.PrefetchScalarGridSpec(
             num_scalar_prefetch=1,
-            grid=(ny,),
-            in_specs=[pl.BlockSpec((1, nz, cut, width), lambda y, m: (y, 0, 0, 0))] * nx
-            + [pl.BlockSpec((1, nz, nx, rest, width), lambda y, m: (y, 0, 0, 0, 0))],
+            grid=(ny // step,),
+            in_specs=[pl.BlockSpec((step, nz, cut, width), lambda y, m: (y, 0, 0, 0))] * nx
+            + [pl.BlockSpec((step, nz, nx, rest, width), lambda y, m: (y, 0, 0, 0, 0))],
             out_specs=pl.BlockSpec((block, width), lambda y, m: (y, 0)),
         ),
-        out_shape=jax.ShapeDtypeStruct((ny * block, width), far.dtype),
-        compiler_params=pltpu.CompilerParams(vmem_limit_bytes=16 * 2**20),
+        out_shape=jax.ShapeDtypeStruct((ny // step * block, width), far.dtype),
+        compiler_params=pltpu.CompilerParams(vmem_limit_bytes=24 * 2**20),
         name="joined",
     )(me.reshape(1), *near, far)
 
@@ -119,8 +129,19 @@
     deltas = global_params - own_local
     mine = jnp.concatenate([deltas, outer_momentum[0]], 0)
     other = passed(mine, CORE, 1)
+
+    term = lax.dot_general(
+        features, cotangent, (((0,), (0,)), ((), ())), preferred_element_type=jnp.float32
+    ).astype(jnp.float16)
+    term, other = lax.optimization_barrier((term, other))
+    term = term.reshape(ny, nx, nz, rows, width)
+    term_b = term[:, :, :, cut:].transpose(0, 2, 1, 3, 4).reshape(plane, nx, rows - cut, width)
+    got_a = terms_along(term, X, 1, cut)
+    got_b = exchanged(term_b, YZ)
+
     first, second = jnp.where(core == 0, mine, other), jnp.where(core == 0, other, mine)
     pair = jnp.concatenate([mine[:rows] + other[:rows], first[rows:], second[rows:]], 0)
+    pair, got_a[1] = lax.optimization_barrier((pair, got_a[1]))
     by_chip = placed_along(pair, HI)
     outer_grad = sum(p[:rows] for p in by_chip) / replicas
     old_rows = jnp.concatenate([p[rows:] for p in by_chip], 0)
@@ -130,19 +151,13 @@
         momentum_all, (hi * n_core + core) * sub_rows, sub_rows, 0
     )
 
-    term = lax.dot_general(
-        features, cotangent, (((0,), (0,)), ((), ())), preferred_element_type=jnp.float32
-    ).astype(jnp.float16)
-    term = term.reshape(ny, nx, nz, rows, width)
-    term_b = term[:, :, :, cut:].transpose(0, 2, 1, 3, 4).reshape(plane, nx, rows - cut, width)
-    got_a = terms_along(term[:, :, :, :cut], X, 1)
-    got_b = exchanged(term_b, YZ)
-
-    part_a, part_b = lax.optimization_barrier(
-        (total(got_a).astype(jnp.float16).reshape(plane, cut, width), total(got_b).astype(jnp.float16))
+    part_a = total(got_a).astype(jnp.float16).reshape(plane, cut, width)
+    part_b = total(got_b).astype(jnp.float16)
+    part_a, part_b, global_new, momentum_new = lax.optimization_barrier(
+        (part_a, part_b, global_new, momentum_new)
     )
     sum_a = exchanged(part_a, YZ)
-    sum_b = terms_along(part_b, X, 0)
+    sum_b = [t[0] for t in terms_along(part_b, X, 0, rows - cut)]
 
     def stepped(gradient, lo, hi):
         first_new = beta_one * adam_first[0, lo:hi] + (1.0 - beta_one) * gradient
@@ -156,6 +171,7 @@
 
     merged_a, first_a, second_a = stepped(total(sum_a), 0, cut)
     merged_b, first_b, second_b = stepped(total(sum_b), cut, rows)
+    merged_a, merged_b = lax.optimization_barrier((merged_a, merged_b))
     near_b = placed_along(merged_b, X)
     near_a, near_b = lax.optimization_barrier((exchanged(copies(merged_a, plane), YZ), near_b))
     all_a = [n.reshape(ny, nz, cut, width) for n in arrived_along(near_a, X)]

time: 182 us -> 165 us (0.907)
  the two profiles are of different devices: /device:TPU:8 before, /device:TPU:1 now
where the time goes in v3:
time: 165 us; the launch traced here: 164 us
  starting transfers between devices  92.6 us (56%)
  waiting for transfers between devices  44 us (27%)
  local copies, waits for them, and re-layouts  13.1 us (8%)
  other arithmetic  7.82 us (5%)
  matrix products  2.83 us (2%)
  Pallas kernels  2.12 us (1%)
    ppermute x15, starting transfers between devices, passed(): return lax.ppermute(x, axis, [(i, (i + step) % n) for i in range(n)])  57.9 us
    ppermute x15, waiting for transfers between devices, passed(): return lax.ppermute(x, axis, [(i, (i + step) % n) for i in range(n)])  40.3 us
    all_to_all x4, starting transfers between devices, exchanged(): return lax.all_to_all(x, axes, 0, 0, tiled=True)  34.7 us
    unnamed x36, local copies, waits for them, and re-layouts  6.72 us
    all_to_all x4, waiting for transfers between devices, exchanged(): return lax.all_to_all(x, axes, 0, 0, tiled=True)  3.75 us
  transfers between devices with their start and end apart: 19, of which 10 were waited for; matrix products, arithmetic and copies ran while one was open for 6% of the time, Pallas kernels for 0%

profile of v3, /device:TPU:1, one launch (start us, length us, event | category | flops | bytes accessed | tf_op | source)
XLA Modules:
  0.0 163.6 jit_solution(1396762664723901122)
XLA Ops:
  2.3 12.4 %collective-permute-start = (f32[28,512]{1,0:T(8,128)S(1)}, f32[28,512]{1,0:T(8,128)S(1)}, u32[]{:S(2)}, u32[]{:S(2)}) collective-permute-start(f32[28,512]{1,0:T(8,128)S(1)} %pad_maximum_fusion.1), channel_id=1, source_target_pairs={{0,128},{128,0},{1,129},{129,1},{2,130},{130,2},{3,131},{131,3},{4... | collective-permute-start | bytes 172040 | tf_op jit(solution)/shard_map/ppermute | solution.py:42
  14.8 2.8 %convolution_convert_fusion = f16[3072,512]{1,0:T(8,128)(2,1)S(1)} fusion(bf16[1,384,3072]{2,1,0:T(8,128)(2,1)S(1)} %copy-done, bf16[1,384,512]{2,1,0:T(8,128)(2,1)} %param.8), kind=kOutput, calls=%fused_computation | convolution fusion | flops 1209532416 | bytes 5898240 | tf_op jit(solution)/shard_map/dot_general | solution.py:133
  19.6 4.1 %all-to-all-start = ((f16[32,4,8,512]{3,2,1,0:T(8,128)(2,1)}), f16[32,4,8,512]{3,2,1,0:T(8,128)(2,1)S(1)}, u32[]{:S(2)}, u32[]{:S(2)}) async-start(f16[32,4,8,512]{3,2,1,0:T(8,128)(2,1)} %bitcast.91), calls=%async_computation | async-start | bytes 2097152 | tf_op jit(solution)/shard_map/all_to_all | solution.py:26
  25.6 2.9 %collective-permute-start.1 = (f16[8,1,4,16,512]{4,3,2,1,0:T(8,128)(2,1)S(1)}, f16[8,1,4,16,512]{4,3,2,1,0:T(8,128)(2,1)S(1)}, u32[]{:S(2)}, u32[]{:S(2)}) collective-permute-start(f16[8,1,4,16,512]{4,3,2,1,0:T(8,128)(2,1)S(1)} %get-tuple-element.37), channel_id=1, source_target_pairs={{0,4},{4,8},{8,12},{12,0},{1,5},{5,9},{9,13},{13,1},{2,6},{6,10},{... | collective-permute-start | bytes 1572872 | tf_op jit(solution)/shard_map/ppermute | solution.py:42
  28.6 3.7 %collective-permute-start.3 = (f16[8,1,4,16,512]{4,3,2,1,0:T(8,128)(2,1)S(1)}, f16[8,1,4,16,512]{4,3,2,1,0:T(8,128)(2,1)S(1)}, u32[]{:S(2)}, u32[]{:S(2)}) collective-permute-start(f16[8,1,4,16,512]{4,3,2,1,0:T(8,128)(2,1)S(1)} %get-tuple-element.38), channel_id=1, source_target_pairs={{0,12},{4,0},{8,4},{12,8},{1,13},{5,1},{9,5},{13,9},{2,14},{6,2},{... | collective-permute-start | bytes 1572872 | tf_op jit(solution)/shard_map/ppermute | solution.py:42
  32.3 3.1 %collective-permute-start.2 = (f16[8,1,4,16,512]{4,3,2,1,0:T(8,128)(2,1)S(1)}, f16[8,1,4,16,512]{4,3,2,1,0:T(8,128)(2,1)S(1)}, u32[]{:S(2)}, u32[]{:S(2)}) collective-permute-start(f16[8,1,4,16,512]{4,3,2,1,0:T(8,128)(2,1)S(1)} %get-tuple-element.39), channel_id=1, source_target_pairs={{0,8},{4,12},{8,0},{12,4},{1,9},{5,13},{9,1},{13,5},{2,10},{6,14},... | collective-permute-start | bytes 1572872 | tf_op jit(solution)/shard_map/ppermute | solution.py:42
  35.5 6.9 %collective-permute-done.1 = f16[8,1,4,16,512]{4,3,2,1,0:T(8,128)(2,1)S(1)} collective-permute-done((f16[8,1,4,16,512]{4,3,2,1,0:T(8,128)(2,1)S(1)}, f16[8,1,4,16,512]{4,3,2,1,0:T(8,128)(2,1)S(1)}, u32[]{:S(2)}, u32[]{:S(2)}) %collective-permute-start.1) | collective-permute-done | bytes 524320 | tf_op jit(solution)/shard_map/ppermute | solution.py:42
  42.4 10.9 %collective-permute-start.5 = (f32[32,512]{1,0:T(8,128)S(1)}, f32[32,512]{1,0:T(8,128)S(1)}, u32[]{:S(2)}, u32[]{:S(2)}) collective-permute-start(f32[32,512]{1,0:T(8,128)S(1)} %pad_maximum_fusion.2), channel_id=1, source_target_pairs={{0,512},{256,0},{512,256},{1,513},{257,1},{513,257},{2,514},{258,2... | collective-permute-start | bytes 196616 | tf_op jit(solution)/shard_map/ppermute | solution.py:42
  55.3 2.4 %add_convert_fusion = f16[8,1,4,16,512]{4,3,2,1,0:T(8,128)(2,1)} fusion(f16[8,1,4,16,512]{4,3,2,1,0:T(8,128)(2,1)S(1)} %collective-permute-done.3, f16[8,1,4,16,512]{4,3,2,1,0:T(8,128)(2,1)S(1)} %collective-permute-done.2, f16[8,1,4,16,512]{4,3,2,1,0:T(8,128)(2,1)S(1)} %collective-permute-done.1, f16[8,4,4,24,512]{4,3,2,1,0:T(8,128)(2,1)} %bitcast.95, ...), kind=kLoop, calls=%fused_computation.3 | loop fusion | flops 2097152 | bytes 2621444 | tf_op jit(solution)/shard_map/convert_element_type | solution.py:154
  57.7 4.9 %collective-permute-done.4 = f32[32,512]{1,0:T(8,128)S(1)} collective-permute-done((f32[32,512]{1,0:T(8,128)S(1)}, f32[32,512]{1,0:T(8,128)S(1)}, u32[]{:S(2)}, u32[]{:S(2)}) %collective-permute-start.4) | collective-permute-done | bytes 65568 | tf_op jit(solution)/shard_map/ppermute | solution.py:42
  63.5 14.0 %all-to-all-start.1 = ((f16[32,16,512]{2,1,0:T(8,128)(2,1)}), f16[32,16,512]{2,1,0:T(8,128)(2,1)S(1)}, u32[]{:S(2)}, u32[]{:S(2)}) async-start(f16[32,16,512]{2,1,0:T(8,128)(2,1)} %bitcast.96), calls=%async_computation.1 | async-start | bytes 1048576 | tf_op jit(solution)/shard_map/all_to_all | solution.py:26
  79.4 4.6 %collective-permute-start.8 = (f16[1,8,512]{2,1,0:T(8,128)(2,1)S(1)}, f16[1,8,512]{2,1,0:T(8,128)(2,1)S(1)}, u32[]{:S(2)}, u32[]{:S(2)}) collective-permute-start(f16[1,8,512]{2,1,0:T(8,128)(2,1)S(1)} %get-tuple-element.50), channel_id=1, source_target_pairs={{0,12},{4,0},{8,4},{12,8},{1,13},{5,1},{9,5},{13,9},{2,14},{6,2},{... | collective-permute-start | bytes 24584 | tf_op jit(solution)/shard_map/ppermute | solution.py:42
  86.0 4.2 %collective-permute-done.7 = f16[1,8,512]{2,1,0:T(8,128)(2,1)S(1)} collective-permute-done((f16[1,8,512]{2,1,0:T(8,128)(2,1)S(1)}, f16[1,8,512]{2,1,0:T(8,128)(2,1)S(1)}, u32[]{:S(2)}, u32[]{:S(2)}) %collective-permute-start.7) | collective-permute-done | bytes 8224 | tf_op jit(solution)/shard_map/ppermute | solution.py:42
  95.0 8.4 %all-to-all-start.2 = ((bf16[32,16,512]{2,1,0:T(8,128)(2,1)}), bf16[32,16,512]{2,1,0:T(8,128)(2,1)S(1)}, u32[]{:S(2)}, u32[]{:S(2)}) async-start(bf16[32,16,512]{2,1,0:T(8,128)(2,1)} %broadcast_in_dim.24), calls=%async_computation.2 | async-start | bytes 1048576 | tf_op jit(solution)/shard_map/all_to_all | solution.py:26
  105.4 2.2 %collective-permute-start.10 = (bf16[8,512]{1,0:T(8,128)(2,1)S(1)}, bf16[8,512]{1,0:T(8,128)(2,1)S(1)}, u32[]{:S(2)}, u32[]{:S(2)}) collective-permute-start(bf16[8,512]{1,0:T(8,128)(2,1)S(1)} %get-tuple-element.25), channel_id=1, source_target_pairs={{0,8},{4,12},{8,0},{12,4},{1,9},{5,13},{9,1},{13,5},{2,10},{6,14},... | collective-permute-start | bytes 24584 | tf_op jit(solution)/shard_map/ppermute | solution.py:42
  107.6 3.1 %collective-permute-start.9 = (bf16[8,512]{1,0:T(8,128)(2,1)S(1)}, bf16[8,512]{1,0:T(8,128)(2,1)S(1)}, u32[]{:S(2)}, u32[]{:S(2)}) collective-permute-start(bf16[8,512]{1,0:T(8,128)(2,1)S(1)} %get-tuple-element.25), channel_id=1, source_target_pairs={{0,4},{4,8},{8,12},{12,0},{1,5},{5,9},{9,13},{13,1},{2,6},{6,10},{... | collective-permute-start | bytes 24584 | tf_op jit(solution)/shard_map/ppermute | solution.py:42
  111.4 3.0 %collective-permute-done.9 = bf16[8,512]{1,0:T(8,128)(2,1)S(1)} collective-permute-done((bf16[8,512]{1,0:T(8,128)(2,1)S(1)}, bf16[8,512]{1,0:T(8,128)(2,1)S(1)}, u32[]{:S(2)}, u32[]{:S(2)}) %collective-permute-start.9) | collective-permute-done | bytes 8224 | tf_op jit(solution)/shard_map/ppermute | solution.py:42
  114.4 2.6 %all-to-all-done.2 = bf16[32,16,512]{2,1,0:T(8,128)(2,1)S(1)} async-done(((bf16[32,16,512]{2,1,0:T(8,128)(2,1)}), bf16[32,16,512]{2,1,0:T(8,128)(2,1)S(1)}, u32[]{:S(2)}, u32[]{:S(2)}) %all-to-all-start.2) | async-done | bytes 524320 | tf_op jit(solution)/shard_map/all_to_all | solution.py:26
  118.2 8.2 %all-to-all-start.3 = ((bf16[32,4,8,512]{3,2,1,0:T(8,128)(2,1)}), bf16[32,4,8,512]{3,2,1,0:T(8,128)(2,1)S(1)}, u32[]{:S(2)}, u32[]{:S(2)}) async-start(bf16[32,4,8,512]{3,2,1,0:T(8,128)(2,1)} %broadcast_in_dim.25), calls=%async_computation.3 | async-start | bytes 2097152 | tf_op jit(solution)/shard_map/all_to_all | solution.py:26
  128.5 2.1 %collective-permute-start.13 = (bf16[32,16,512]{2,1,0:T(8,128)(2,1)}, bf16[32,16,512]{2,1,0:T(8,128)(2,1)S(1)}, u32[]{:S(2)}, u32[]{:S(2)}) collective-permute-start(bf16[32,16,512]{2,1,0:T(8,128)(2,1)} %copy-done.1), channel_id=1, source_target_pairs={{0,8},{4,12},{8,0},{12,4},{1,9},{5,13},{9,1},{13,5},{2,10},{6,14},... | collective-permute-start | bytes 1572872 | tf_op jit(solution)/shard_map/ppermute | solution.py:42
  130.6 3.1 %collective-permute-start.12 = (bf16[32,16,512]{2,1,0:T(8,128)(2,1)}, bf16[32,16,512]{2,1,0:T(8,128)(2,1)S(1)}, u32[]{:S(2)}, u32[]{:S(2)}) collective-permute-start(bf16[32,16,512]{2,1,0:T(8,128)(2,1)} %copy-done.1), channel_id=1, source_target_pairs={{0,4},{4,8},{8,12},{12,0},{1,5},{5,9},{9,13},{13,1},{2,6},{6,10},{... | collective-permute-start | bytes 1572872 | tf_op jit(solution)/shard_map/ppermute | solution.py:42
  134.3 4.5 %collective-permute-done.14 = bf16[32,16,512]{2,1,0:T(8,128)(2,1)S(1)} collective-permute-done((bf16[32,16,512]{2,1,0:T(8,128)(2,1)}, bf16[32,16,512]{2,1,0:T(8,128)(2,1)S(1)}, u32[]{:S(2)}, u32[]{:S(2)}) %collective-permute-start.14) | collective-permute-done | bytes 524320 | tf_op jit(solution)/shard_map/ppermute | solution.py:42
  141.4 15.1 %collective-permute-done.12 = bf16[32,16,512]{2,1,0:T(8,128)(2,1)S(1)} collective-permute-done((bf16[32,16,512]{2,1,0:T(8,128)(2,1)}, bf16[32,16,512]{2,1,0:T(8,128)(2,1)S(1)}, u32[]{:S(2)}, u32[]{:S(2)}) %collective-permute-start.12) | collective-permute-done | bytes 524320 | tf_op jit(solution)/shard_map/ppermute | solution.py:42
  161.5 2.1 %joined.1 = bf16[3072,512]{1,0:T(8,128)(2,1)} custom-call(s32[1]{0:T(128)} %bitcast.me_ref, bf16[8,4,16,512]{3,2,1,0:T(8,128)(2,1)S(1)} %bitcast.87, bf16[8,4,16,512]{3,2,1,0:T(8,128)(2,1)S(1)} %bitcast.90, bf16[8,4,16,512]{3,2,1,0:T(8,128)(2,1)S(1)} %bitcast.89, bf16[8,4,16,512]{3,2,1,0:T(8,128)(2,1)S(1)} %bitcast.88, bf16[8,4,4,8,512]{4,3,2,1,0:T(8,128)(2,1)S(1)} %bitcast.86), custom_call_target="tpu_custom_call" | custom-call | tf_op jit(solution)/shard_map/joined/pallas_call | solution.py:98
  (76 shorter events, 31.0 us)
Async XLA Ops:
  2.3 15.3 %collective-permute-start = (f32[28,512]{1,0:T(8,128)S(1)}, f32[28,512]{1,0:T(8,128)S(1)}, u32[]{:S(2)}, u32[]{:S(2)}) collective-permute-start(f32[28,512]{1,0:T(8,128)S(1)} %pad_maximum_fusion.1), channel_id=1, source_target_pairs={{0,128},{128,0},{1,129},{129,1},{2,130},{130,2},{3,131},{131,3},{4... | collective-permute-start | bytes 172040 | tf_op jit(solution)/shard_map/ppermute | solution.py:42
  19.6 43.7 %all-to-all-start = ((f16[32,4,8,512]{3,2,1,0:T(8,128)(2,1)}), f16[32,4,8,512]{3,2,1,0:T(8,128)(2,1)S(1)}, u32[]{:S(2)}, u32[]{:S(2)}) async-start(f16[32,4,8,512]{3,2,1,0:T(8,128)(2,1)} %bitcast.91), calls=%async_computation | async-start | bytes 2097152 | tf_op jit(solution)/shard_map/all_to_all | solution.py:26
  23.8 39.5 %copy-start.12 = (f32[24,512]{1,0:T(8,128)S(1)}, f32[24,512]{1,0:T(8,128)}, u32[]{:S(2)}) copy-start(f32[24,512]{1,0:T(8,128)} %param.10) | copy-start | bytes 147460
  25.6 64.6 %copy-start.10 = (f32[1,24,512]{2,1,0:T(8,128)S(1)}, f32[1,24,512]{2,1,0:T(8,128)}, u32[]{:S(2)}) copy-start(f32[1,24,512]{2,1,0:T(8,128)} %param.9) | copy-start | bytes 147460
  25.6 16.8 %collective-permute-start.1 = (f16[8,1,4,16,512]{4,3,2,1,0:T(8,128)(2,1)S(1)}, f16[8,1,4,16,512]{4,3,2,1,0:T(8,128)(2,1)S(1)}, u32[]{:S(2)}, u32[]{:S(2)}) collective-permute-start(f16[8,1,4,16,512]{4,3,2,1,0:T(8,128)(2,1)S(1)} %get-tuple-element.37), channel_id=1, source_target_pairs={{0,4},{4,8},{8,12},{12,0},{1,5},{5,9},{9,13},{13,1},{2,6},{6,10},{... | collective-permute-start | bytes 1572872 | tf_op jit(solution)/shard_map/ppermute | solution.py:42
  28.6 26.7 %collective-permute-start.3 = (f16[8,1,4,16,512]{4,3,2,1,0:T(8,128)(2,1)S(1)}, f16[8,1,4,16,512]{4,3,2,1,0:T(8,128)(2,1)S(1)}, u32[]{:S(2)}, u32[]{:S(2)}) collective-permute-start(f16[8,1,4,16,512]{4,3,2,1,0:T(8,128)(2,1)S(1)} %get-tuple-element.38), channel_id=1, source_target_pairs={{0,12},{4,0},{8,4},{12,8},{1,13},{5,1},{9,5},{13,9},{2,14},{6,2},{... | collective-permute-start | bytes 1572872 | tf_op jit(solution)/shard_map/ppermute | solution.py:42
  32.3 23.0 %collective-permute-start.2 = (f16[8,1,4,16,512]{4,3,2,1,0:T(8,128)(2,1)S(1)}, f16[8,1,4,16,512]{4,3,2,1,0:T(8,128)(2,1)S(1)}, u32[]{:S(2)}, u32[]{:S(2)}) collective-permute-start(f16[8,1,4,16,512]{4,3,2,1,0:T(8,128)(2,1)S(1)} %get-tuple-element.39), channel_id=1, source_target_pairs={{0,8},{4,12},{8,0},{12,4},{1,9},{5,13},{9,1},{13,5},{2,10},{6,14},... | collective-permute-start | bytes 1572872 | tf_op jit(solution)/shard_map/ppermute | solution.py:42
  42.4 15.3 %collective-permute-start.5 = (f32[32,512]{1,0:T(8,128)S(1)}, f32[32,512]{1,0:T(8,128)S(1)}, u32[]{:S(2)}, u32[]{:S(2)}) collective-permute-start(f32[32,512]{1,0:T(8,128)S(1)} %pad_maximum_fusion.2), channel_id=1, source_target_pairs={{0,512},{256,0},{512,256},{1,513},{257,1},{513,257},{2,514},{258,2... | collective-permute-start | bytes 196616 | tf_op jit(solution)/shard_map/ppermute | solution.py:42
  53.3 9.2 %collective-permute-start.4 = (f32[32,512]{1,0:T(8,128)S(1)}, f32[32,512]{1,0:T(8,128)S(1)}, u32[]{:S(2)}, u32[]{:S(2)}) collective-permute-start(f32[32,512]{1,0:T(8,128)S(1)} %pad_maximum_fusion.2), channel_id=1, source_target_pairs={{0,256},{256,512},{512,0},{1,257},{257,513},{513,1},{2,258},{258,5... | collective-permute-start | bytes 196616 | tf_op jit(solution)/shard_map/ppermute | solution.py:42
  63.3 54.9 %copy-start.11 = (f32[24,512]{1,0:T(8,128)}, f32[24,512]{1,0:T(8,128)S(1)}, u32[]{:S(2)}) copy-start(f32[24,512]{1,0:T(8,128)S(1)} %multiply_subtract_fusion) | copy-start | bytes 147460
  63.5 29.2 %all-to-all-start.1 = ((f16[32,16,512]{2,1,0:T(8,128)(2,1)}), f16[32,16,512]{2,1,0:T(8,128)(2,1)S(1)}, u32[]{:S(2)}, u32[]{:S(2)}) async-start(f16[32,16,512]{2,1,0:T(8,128)(2,1)} %bitcast.96), calls=%async_computation.1 | async-start | bytes 1048576 | tf_op jit(solution)/shard_map/all_to_all | solution.py:26
  77.5 8.4 %collective-permute-start.6 = (f16[1,8,512]{2,1,0:T(8,128)(2,1)S(1)}, f16[1,8,512]{2,1,0:T(8,128)(2,1)S(1)}, u32[]{:S(2)}, u32[]{:S(2)}) collective-permute-start(f16[1,8,512]{2,1,0:T(8,128)(2,1)S(1)} %get-tuple-element.49), channel_id=1, source_target_pairs={{0,4},{4,8},{8,12},{12,0},{1,5},{5,9},{9,13},{13,1},{2,6},{6,10},{... | collective-permute-start | bytes 24584 | tf_op jit(solution)/shard_map/ppermute | solution.py:42
  79.4 6.5 %collective-permute-start.8 = (f16[1,8,512]{2,1,0:T(8,128)(2,1)S(1)}, f16[1,8,512]{2,1,0:T(8,128)(2,1)S(1)}, u32[]{:S(2)}, u32[]{:S(2)}) collective-permute-start(f16[1,8,512]{2,1,0:T(8,128)(2,1)S(1)} %get-tuple-element.50), channel_id=1, source_target_pairs={{0,12},{4,0},{8,4},{12,8},{1,13},{5,1},{9,5},{13,9},{2,14},{6,2},{... | collective-permute-start | bytes 24584 | tf_op jit(solution)/shard_map/ppermute | solution.py:42
  84.0 6.2 %collective-permute-start.7 = (f16[1,8,512]{2,1,0:T(8,128)(2,1)S(1)}, f16[1,8,512]{2,1,0:T(8,128)(2,1)S(1)}, u32[]{:S(2)}, u32[]{:S(2)}) collective-permute-start(f16[1,8,512]{2,1,0:T(8,128)(2,1)S(1)} %get-tuple-element.51), channel_id=1, source_target_pairs={{0,8},{4,12},{8,0},{12,4},{1,9},{5,13},{9,1},{13,5},{2,10},{6,14},... | collective-permute-start | bytes 24584 | tf_op jit(solution)/shard_map/ppermute | solution.py:42
  94.2 39.5 %copy-start.13 = (f32[16,512]{1,0:T(8,128)S(1)}, f32[16,512]{1,0:T(8,128)}, u32[]{:S(2)}) copy-start(f32[16,512]{1,0:T(8,128)} %get-tuple-element.34) | copy-start | bytes 98308
  94.2 39.5 %copy-start.14 = (f32[8,512]{1,0:T(8,128)S(1)}, f32[8,512]{1,0:T(8,128)}, u32[]{:S(2)}) copy-start(f32[8,512]{1,0:T(8,128)} %get-tuple-element.31) | copy-start | bytes 49156
  95.0 22.0 %all-to-all-start.2 = ((bf16[32,16,512]{2,1,0:T(8,128)(2,1)}), bf16[32,16,512]{2,1,0:T(8,128)(2,1)S(1)}, u32[]{:S(2)}, u32[]{:S(2)}) async-start(bf16[32,16,512]{2,1,0:T(8,128)(2,1)} %broadcast_in_dim.24), calls=%async_computation.2 | async-start | bytes 1048576 | tf_op jit(solution)/shard_map/all_to_all | solution.py:26
  103.4 7.2 %collective-permute-start.11 = (bf16[8,512]{1,0:T(8,128)(2,1)S(1)}, bf16[8,512]{1,0:T(8,128)(2,1)S(1)}, u32[]{:S(2)}, u32[]{:S(2)}) collective-permute-start(bf16[8,512]{1,0:T(8,128)(2,1)S(1)} %get-tuple-element.25), channel_id=1, source_target_pairs={{0,12},{4,0},{8,4},{12,8},{1,13},{5,1},{9,5},{13,9},{2,14},{6,2},{... | collective-permute-start | bytes 24584 | tf_op jit(solution)/shard_map/ppermute | solution.py:42
  105.4 6.0 %collective-permute-start.10 = (bf16[8,512]{1,0:T(8,128)(2,1)S(1)}, bf16[8,512]{1,0:T(8,128)(2,1)S(1)}, u32[]{:S(2)}, u32[]{:S(2)}) collective-permute-start(bf16[8,512]{1,0:T(8,128)(2,1)S(1)} %get-tuple-element.25), channel_id=1, source_target_pairs={{0,8},{4,12},{8,0},{12,4},{1,9},{5,13},{9,1},{13,5},{2,10},{6,14},... | collective-permute-start | bytes 24584 | tf_op jit(solution)/shard_map/ppermute | solution.py:42
  107.6 6.8 %collective-permute-start.9 = (bf16[8,512]{1,0:T(8,128)(2,1)S(1)}, bf16[8,512]{1,0:T(8,128)(2,1)S(1)}, u32[]{:S(2)}, u32[]{:S(2)}) collective-permute-start(bf16[8,512]{1,0:T(8,128)(2,1)S(1)} %get-tuple-element.25), channel_id=1, source_target_pairs={{0,4},{4,8},{8,12},{12,0},{1,5},{5,9},{9,13},{13,1},{2,6},{6,10},{... | collective-permute-start | bytes 24584 | tf_op jit(solution)/shard_map/ppermute | solution.py:42
  118.2 39.1 %all-to-all-start.3 = ((bf16[32,4,8,512]{3,2,1,0:T(8,128)(2,1)}), bf16[32,4,8,512]{3,2,1,0:T(8,128)(2,1)S(1)}, u32[]{:S(2)}, u32[]{:S(2)}) async-start(bf16[32,4,8,512]{3,2,1,0:T(8,128)(2,1)} %broadcast_in_dim.25), calls=%async_computation.3 | async-start | bytes 2097152 | tf_op jit(solution)/shard_map/all_to_all | solution.py:26
  126.4 12.4 %collective-permute-start.14 = (bf16[32,16,512]{2,1,0:T(8,128)(2,1)}, bf16[32,16,512]{2,1,0:T(8,128)(2,1)S(1)}, u32[]{:S(2)}, u32[]{:S(2)}) collective-permute-start(bf16[32,16,512]{2,1,0:T(8,128)(2,1)} %copy-done.1), channel_id=1, source_target_pairs={{0,12},{4,0},{8,4},{12,8},{1,13},{5,1},{9,5},{13,9},{2,14},{6,2},{... | collective-permute-start | bytes 1572872 | tf_op jit(solution)/shard_map/ppermute | solution.py:42
  128.5 12.1 %collective-permute-start.13 = (bf16[32,16,512]{2,1,0:T(8,128)(2,1)}, bf16[32,16,512]{2,1,0:T(8,128)(2,1)S(1)}, u32[]{:S(2)}, u32[]{:S(2)}) collective-permute-start(bf16[32,16,512]{2,1,0:T(8,128)(2,1)} %copy-done.1), channel_id=1, source_target_pairs={{0,8},{4,12},{8,0},{12,4},{1,9},{5,13},{9,1},{13,5},{2,10},{6,14},... | collective-permute-start | bytes 1572872 | tf_op jit(solution)/shard_map/ppermute | solution.py:42
  130.6 25.9 %collective-permute-start.12 = (bf16[32,16,512]{2,1,0:T(8,128)(2,1)}, bf16[32,16,512]{2,1,0:T(8,128)(2,1)S(1)}, u32[]{:S(2)}, u32[]{:S(2)}) collective-permute-start(bf16[32,16,512]{2,1,0:T(8,128)(2,1)} %copy-done.1), channel_id=1, source_target_pairs={{0,4},{4,8},{8,12},{12,0},{1,5},{5,9},{9,13},{13,1},{2,6},{6,10},{... | collective-permute-start | bytes 1572872 | tf_op jit(solution)/shard_map/ppermute | solution.py:42
  (13 other events, 53.3 us)

commit v4 on v2

v4 whole, which is shorter than its diff:
```python
import jax
import jax.numpy as jnp
from jax import lax
from jax.experimental import pallas as pl
from jax.experimental.pallas import tpu as pltpu
from jax.sharding import Mesh
from jax.sharding import PartitionSpec as P

DP = ("dp_0", "dp_1", "dp_2")
YZ = ("dp_0", "dp_2")
X = "dp_1"
HI, CORE = REPLICA = ("chip", "core")

outer_mu = 0.9
outer_rate = 0.7
beta_one = 0.9
beta_two = 0.95
adam_eps = 1e-08
weight_decay = 0.1
inner_rate = 0.1
correct_one = 1.0 - 0.9**50
correct_two = 1.0 - 0.95**50


def exchanged(x, axes):
    return lax.all_to_all(x, axes, 0, 0, tiled=True)


def copies(x, n):
    return jnp.broadcast_to(x[None], (n, *x.shape))


def total(blocks):
    parts = [b.astype(jnp.float32) for b in blocks]
    while len(parts) > 1:
        parts = [sum(parts[i : i + 2]) for i in range(0, len(parts), 2)]
    return parts[0]


def passed(x, axis, step):
    n = lax.axis_size(axis)
    return lax.ppermute(x, axis, [(i, (i + step) % n) for i in range(n)])


def turned(index, n):
    return index & (n - 1) if n & (n - 1) == 0 else lax.rem(index, n)


def block_of(x, index, dim):
    return lax.dynamic_index_in_dim(x, index, dim, keepdims=False)


def blocks_along(x, axis, dim):
    n = lax.axis_size(axis)
    me = lax.axis_index(axis)
    return [block_of(x, turned(me + k, n), dim) for k in range(n)]


def terms_along(blocks, axis):
    return blocks[:1] + [passed(blocks[k], axis, k) for k in range(1, len(blocks))]


def arrived_along(x, axis):
    return [x] + [passed(x, axis, k) for k in range(1, lax.axis_size(axis))]


def placed_along(x, axis):
    n = lax.axis_size(axis)
    me = lax.axis_index(axis)
    blocks = jnp.stack(arrived_along(x, axis))
    return jnp.stack([block_of(blocks, turned(me + n - i, n), 0) for i in range(n)])


def joining(me_ref, *refs):
    *near, far, out, near_in, far_in, held, got, sent = refs
    places = len(near)
    ny = far.shape[0]
    me = me_ref[0]

    def loads(y):
        return [
            pltpu.make_async_copy(ref.at[y], near_in.at[k, y], got.at[k, y])
            for k, ref in enumerate(near)
        ] + [pltpu.make_async_copy(far.at[y], far_in.at[y], got.at[places, y])]

    def store(y):
        return pltpu.make_async_copy(held.at[y], out.at[y], sent.at[y])

    for y in range(ny):
        for copy in loads(y):
            copy.start()
    for y in range(ny):
        for copy in loads(y):
            copy.wait()
        for k in range(places):
            x = turned(me + places - k, places)
            both = jnp.concatenate(
                [near_in[k, y].astype(jnp.float32), far_in[y, :, x].astype(jnp.float32)], axis=1
            )
            held[y, x] = both.reshape(-1, both.shape[-1]).astype(out.dtype)
        store(y).start()
    for y in range(ny):
        store(y).wait()


def joined(near, far, me):
    ny, nz, cut, width = near[0].shape
    nx, rest = far.shape[2:4]
    shape = (ny, nx, nz * (cut + rest), width)
    place = pl.BlockSpec(memory_space=pl.ANY)
    out = pl.pallas_call(
        joining,
        in_specs=[pl.BlockSpec(memory_space=pltpu.SMEM)] + [place] * (nx + 1),
        out_specs=place,
        out_shape=jax.ShapeDtypeStruct(shape, far.dtype),
        scratch_shapes=[
            pltpu.VMEM((nx, *near[0].shape), far.dtype),
            pltpu.VMEM(far.shape, far.dtype),
            pltpu.VMEM(shape, far.dtype),
            pltpu.SemaphoreType.DMA((nx + 1, ny)),
            pltpu.SemaphoreType.DMA((ny,)),
        ],
        name="joined",
    )(me.reshape(1), *near, far)
    return out.reshape(-1, width)


def per_device(
    layer_input, key_cotangent, local_params, global_params, outer_momentum, adam_first, adam_second
):
    features = layer_input[0]
    cotangent = key_cotangent[0]
    own_local = local_params[0]
    rows, width = global_params.shape
    ny, nx, nz = (lax.axis_size(a) for a in DP)
    plane = ny * nz
    n_hi, n_core = lax.axis_size(HI), lax.axis_size(CORE)
    replicas = n_hi * n_core
    sub_rows = outer_momentum.shape[1]
    cut = rows * 2 // 3

    core = lax.axis_index(CORE)
    hi = lax.axis_index(HI)
    deltas = global_params - own_local
    mine = jnp.concatenate([deltas, outer_momentum[0]], 0)
    other = passed(mine, CORE, 1)

    half = width // 2

    def product(columns):
        return lax.dot_general(
            features, columns, (((0,), (0,)), ((), ())), preferred_element_type=jnp.float32
        ).astype(jnp.float16)

    term_b = product(cotangent[:, half:]).reshape(ny, nx, nz, rows, half)
    got_b = exchanged(term_b.transpose(0, 2, 1, 3, 4).reshape(plane, nx, rows, half), YZ)
    term_a = product(cotangent[:, :half]).reshape(ny, nx, nz * rows, half)
    got_a = terms_along(blocks_along(term_a, X, 1), X)

    first, second = jnp.where(core == 0, mine, other), jnp.where(core == 0, other, mine)
    pair = jnp.concatenate([mine[:rows] + other[:rows], first[rows:], second[rows:]], 0)
    pair, got_a[1], got_a[3] = lax.optimization_barrier((pair, got_a[1], got_a[3]))
    by_chip = placed_along(pair, HI)
    outer_grad = sum(p[:rows] for p in by_chip) / replicas
    old_rows = jnp.concatenate([p[rows:] for p in by_chip], 0)
    momentum_all = outer_mu * old_rows + outer_grad
    global_new = global_params - outer_rate * (outer_grad + outer_mu * momentum_all)
    momentum_new = lax.dynamic_slice_in_dim(
        momentum_all, (hi * n_core + core) * sub_rows, sub_rows, 0
    )

    part_a = total(got_a).astype(jnp.float16).reshape(plane, rows, half)
    part_b = total(got_b).astype(jnp.float16)
    part_a, part_b, global_new, momentum_new = lax.optimization_barrier(
        (part_a, part_b, global_new, momentum_new)
    )
    sum_a = exchanged(part_a, YZ)
    sum_b = terms_along(blocks_along(part_b, X, 0), X)
    gradient = jnp.concatenate([total(sum_a), total(sum_b)], 1)

    first_new = beta_one * adam_first[0] + (1.0 - beta_one) * gradient
    second_new = beta_two * adam_second[0] + (1.0 - beta_two) * gradient * gradient
    adam_step = (
        first_new / correct_one / (jnp.sqrt(second_new / correct_two) + adam_eps)
        + weight_decay * own_local
    )
    merged = (global_new - inner_rate * adam_step).astype(jnp.bfloat16)
    merged_a, merged_b = merged[:cut], merged[cut:]
    near_b = placed_along(merged_b, X)
    near_a, near_b = lax.optimization_barrier((exchanged(copies(merged_a, plane), YZ), near_b))
    all_a = [n.reshape(ny, nz, cut, width) for n in arrived_along(near_a, X)]
    all_b = exchanged(copies(near_b, plane), YZ).reshape(ny, nz, nx, rows - cut, width)
    gathered = joined(all_a, all_b, lax.axis_index(X))
    return (gathered[None], global_new, momentum_new[None], first_new[None], second_new[None])


def solution(mesh):
    torus = Mesh(
        mesh.devices.reshape(mesh.shape["replica"] // 2, 2, 8, 4, 4), REPLICA + DP
    )
    in_specs = (
        P(REPLICA, DP, None),
        P(REPLICA, DP, None),
        P(REPLICA, DP, None),
        P(DP, None),
        P(DP, REPLICA, None),
        P(REPLICA, DP, None),
        P(REPLICA, DP, None),
    )
    out_specs = (
        P(REPLICA, None, None),
        P(DP, None),
        P(DP, REPLICA, None),
        P(REPLICA, DP, None),
        P(REPLICA, DP, None),
    )
    return jax.shard_map(
        per_device, mesh=torus, in_specs=in_specs, out_specs=out_specs, check_vma=False
    )
```

time: 182 us -> 169 us (0.929)
  the two profiles are of different devices: /device:TPU:8 before, /device:TPU:1 now
where the time goes in v4:
time: 169 us; the launch traced here: 168 us
  starting transfers between devices  99 us (59%)
  waiting for transfers between devices  45.9 us (27%)
  local copies, waits for them, and re-layouts  9.94 us (6%)
  other arithmetic  5.95 us (4%)
  Pallas kernels  3.18 us (2%)
  matrix products  2.97 us (2%)
    ppermute x15, starting transfers between devices, passed(): return lax.ppermute(x, axis, [(i, (i + step) % n) for i in range(n)])  53.6 us
    all_to_all x4, starting transfers between devices, exchanged(): return lax.all_to_all(x, axes, 0, 0, tiled=True)  45.4 us
    ppermute x15, waiting for transfers between devices, passed(): return lax.ppermute(x, axis, [(i, (i + step) % n) for i in range(n)])  42.6 us
    unnamed x30, local copies, waits for them, and re-layouts  4.68 us
  transfers between devices with their start and end apart: 19, of which 10 were waited for; matrix products, arithmetic and copies ran while one was open for 4% of the time, Pallas kernels for 0%

profile of v4, /device:TPU:1, one launch (start us, length us, event | category | flops | bytes accessed | tf_op | source)
XLA Modules:
  0.0 168.1 jit_solution(6061021788762171903)
XLA Ops:
  5.8 13.7 %all-to-all-start = ((f16[32,4,24,256]{3,2,1,0:T(8,128)(2,1)}), f16[32,4,24,256]{3,2,1,0:T(8,128)(2,1)}, u32[]{:S(2)}, u32[]{:S(2)}) async-start(f16[32,4,24,256]{3,2,1,0:T(8,128)(2,1)} %bitcast.80), calls=%async_computation | async-start | bytes 3145728 | tf_op jit(solution)/shard_map/all_to_all | solution.py:26
  19.6 3.5 %collective-permute-start = (f32[28,512]{1,0:T(8,128)S(1)}, f32[28,512]{1,0:T(8,128)S(1)}, u32[]{:S(2)}, u32[]{:S(2)}) collective-permute-start(f32[28,512]{1,0:T(8,128)S(1)} %pad_maximum_fusion.1), channel_id=1, source_target_pairs={{0,128},{128,0},{1,129},{129,1},{2,130},{130,2},{3,131},{131,3},{4... | collective-permute-start | bytes 172040 | tf_op jit(solution)/shard_map/ppermute | solution.py:42
  26.4 4.0 %collective-permute-start.3 = (f16[8,96,256]{2,1,0:T(8,128)(2,1)S(1)}, f16[8,96,256]{2,1,0:T(8,128)(2,1)}, u32[]{:S(2)}, u32[]{:S(2)}) collective-permute-start(f16[8,96,256]{2,1,0:T(8,128)(2,1)S(1)} %get-tuple-element.25), channel_id=1, source_target_pairs={{0,8},{4,12},{8,0},{12,4},{1,9},{5,13},{9,1},{13,5},{2,10},{6,14},... | collective-permute-start | bytes 1179656 | tf_op jit(solution)/shard_map/ppermute | solution.py:42
  30.4 2.8 %collective-permute-start.2 = (f16[8,96,256]{2,1,0:T(8,128)(2,1)}, f16[8,96,256]{2,1,0:T(8,128)(2,1)}, u32[]{:S(2)}, u32[]{:S(2)}) collective-permute-start(f16[8,96,256]{2,1,0:T(8,128)(2,1)} %get-tuple-element.26), channel_id=1, source_target_pairs={{0,12},{4,0},{8,4},{12,8},{1,13},{5,1},{9,5},{13,9},{2,14},{6,2},{... | collective-permute-start | bytes 1179656 | tf_op jit(solution)/shard_map/ppermute | solution.py:42
  33.2 2.5 %collective-permute-start.1 = (f16[8,96,256]{2,1,0:T(8,128)(2,1)S(1)}, f16[8,96,256]{2,1,0:T(8,128)(2,1)}, u32[]{:S(2)}, u32[]{:S(2)}) collective-permute-start(f16[8,96,256]{2,1,0:T(8,128)(2,1)S(1)} %get-tuple-element.27), channel_id=1, source_target_pairs={{0,4},{4,8},{8,12},{12,0},{1,5},{5,9},{9,13},{13,1},{2,6},{6,10},{... | collective-permute-start | bytes 1179656 | tf_op jit(solution)/shard_map/ppermute | solution.py:42
  35.8 12.7 %collective-permute-done.2 = f16[8,96,256]{2,1,0:T(8,128)(2,1)} collective-permute-done((f16[8,96,256]{2,1,0:T(8,128)(2,1)}, f16[8,96,256]{2,1,0:T(8,128)(2,1)}, u32[]{:S(2)}, u32[]{:S(2)}) %collective-permute-start.2) | collective-permute-done | bytes 393248 | tf_op jit(solution)/shard_map/ppermute | solution.py:42
  49.4 10.9 %collective-permute-start.5 = (f32[32,512]{1,0:T(8,128)S(1)}, f32[32,512]{1,0:T(8,128)S(1)}, u32[]{:S(2)}, u32[]{:S(2)}) collective-permute-start(f32[32,512]{1,0:T(8,128)S(1)} %pad_maximum_fusion.2), channel_id=1, source_target_pairs={{0,512},{256,0},{512,256},{1,513},{257,1},{513,257},{2,514},{258,2... | collective-permute-start | bytes 196616 | tf_op jit(solution)/shard_map/ppermute | solution.py:42
  62.2 2.4 %fusion.3 = f16[8,96,256]{2,1,0:T(8,128)(2,1)} fusion(f16[8,96,256]{2,1,0:T(8,128)(2,1)} %collective-permute-done.2, f16[8,96,256]{2,1,0:T(8,128)(2,1)} %collective-permute-done.3, f16[8,96,256]{2,1,0:T(8,128)(2,1)} %collective-permute-done.1, f16[8,4,96,256]{3,2,1,0:T(8,128)(2,1)} %bitcast.86, s32[]{:T(128)S(6)} %select_n.50), kind=kLoop, calls=%fused_computation.6 | loop fusion | flops 1572864 | bytes 1966084 | tf_op jit(solution)/shard_map/convert_element_type | solution.py:172
  64.6 4.7 %collective-permute-done.4 = f32[32,512]{1,0:T(8,128)S(1)} collective-permute-done((f32[32,512]{1,0:T(8,128)S(1)}, f32[32,512]{1,0:T(8,128)S(1)}, u32[]{:S(2)}, u32[]{:S(2)}) %collective-permute-start.4) | collective-permute-done | bytes 65568 | tf_op jit(solution)/shard_map/ppermute | solution.py:42
  71.7 14.7 %all-to-all-start.1 = ((f16[32,24,256]{2,1,0:T(8,128)(2,1)}), f16[32,24,256]{2,1,0:T(8,128)(2,1)S(1)}, u32[]{:S(2)}, u32[]{:S(2)}) async-start(f16[32,24,256]{2,1,0:T(8,128)(2,1)} %bitcast.10), calls=%async_computation.1 | async-start | bytes 786432 | tf_op jit(solution)/shard_map/all_to_all | solution.py:26
  86.5 3.2 %collective-permute-start.6 = (f16[24,256]{1,0:T(8,128)(2,1)S(1)}, f16[24,256]{1,0:T(8,128)(2,1)S(1)}, u32[]{:S(2)}, u32[]{:S(2)}) collective-permute-start(f16[24,256]{1,0:T(8,128)(2,1)S(1)} %get-tuple-element.35), channel_id=1, source_target_pairs={{0,4},{4,8},{8,12},{12,0},{1,5},{5,9},{9,13},{13,1},{2,6},{6,10},{... | collective-permute-start | bytes 36872 | tf_op jit(solution)/shard_map/ppermute | solution.py:42
  89.6 3.3 %collective-permute-start.8 = (f16[24,256]{1,0:T(8,128)(2,1)S(1)}, f16[24,256]{1,0:T(8,128)(2,1)S(1)}, u32[]{:S(2)}, u32[]{:S(2)}) collective-permute-start(f16[24,256]{1,0:T(8,128)(2,1)S(1)} %get-tuple-element.36), channel_id=1, source_target_pairs={{0,12},{4,0},{8,4},{12,8},{1,13},{5,1},{9,5},{13,9},{2,14},{6,2},{... | collective-permute-start | bytes 36872 | tf_op jit(solution)/shard_map/ppermute | solution.py:42
  93.0 3.4 %collective-permute-start.7 = (f16[24,256]{1,0:T(8,128)(2,1)S(1)}, f16[24,256]{1,0:T(8,128)(2,1)S(1)}, u32[]{:S(2)}, u32[]{:S(2)}) collective-permute-start(f16[24,256]{1,0:T(8,128)(2,1)S(1)} %get-tuple-element.37), channel_id=1, source_target_pairs={{0,8},{4,12},{8,0},{12,4},{1,9},{5,13},{9,1},{13,5},{2,10},{6,14},... | collective-permute-start | bytes 36872 | tf_op jit(solution)/shard_map/ppermute | solution.py:42
  96.5 2.8 %collective-permute-done.7 = f16[24,256]{1,0:T(8,128)(2,1)S(1)} collective-permute-done((f16[24,256]{1,0:T(8,128)(2,1)S(1)}, f16[24,256]{1,0:T(8,128)(2,1)S(1)}, u32[]{:S(2)}, u32[]{:S(2)}) %collective-permute-start.7) | collective-permute-done | bytes 12320 | tf_op jit(solution)/shard_map/ppermute | solution.py:42
  100.8 8.7 %all-to-all-start.2 = ((bf16[32,16,512]{2,1,0:T(8,128)(2,1)}), bf16[32,16,512]{2,1,0:T(8,128)(2,1)S(1)}, u32[]{:S(2)}, u32[]{:S(2)}) async-start(bf16[32,16,512]{2,1,0:T(8,128)(2,1)} %broadcast_in_dim.6), calls=%async_computation.2 | async-start | bytes 1048576 | tf_op jit(solution)/shard_map/all_to_all | solution.py:26
  109.5 3.4 %collective-permute-start.10 = (bf16[8,512]{1,0:T(8,128)(2,1)S(1)}, bf16[8,512]{1,0:T(8,128)(2,1)S(1)}, u32[]{:S(2)}, u32[]{:S(2)}) collective-permute-start(bf16[8,512]{1,0:T(8,128)(2,1)S(1)} %get-tuple-element.43), channel_id=1, source_target_pairs={{0,8},{4,12},{8,0},{12,4},{1,9},{5,13},{9,1},{13,5},{2,10},{6,14},... | collective-permute-start | bytes 24584 | tf_op jit(solution)/shard_map/ppermute | solution.py:42
  115.2 4.2 %collective-permute-start.11 = (bf16[8,512]{1,0:T(8,128)(2,1)S(1)}, bf16[8,512]{1,0:T(8,128)(2,1)S(1)}, u32[]{:S(2)}, u32[]{:S(2)}) collective-permute-start(bf16[8,512]{1,0:T(8,128)(2,1)S(1)} %get-tuple-element.43), channel_id=1, source_target_pairs={{0,12},{4,0},{8,4},{12,8},{1,13},{5,1},{9,5},{13,9},{2,14},{6,2},{... | collective-permute-start | bytes 24584 | tf_op jit(solution)/shard_map/ppermute | solution.py:42
  120.3 2.7 %all-to-all-done.2 = bf16[32,16,512]{2,1,0:T(8,128)(2,1)S(1)} async-done(((bf16[32,16,512]{2,1,0:T(8,128)(2,1)}), bf16[32,16,512]{2,1,0:T(8,128)(2,1)S(1)}, u32[]{:S(2)}, u32[]{:S(2)}) %all-to-all-start.2) | async-done | bytes 524320 | tf_op jit(solution)/shard_map/all_to_all | solution.py:26
  124.2 8.3 %all-to-all-start.3 = ((bf16[32,4,8,512]{3,2,1,0:T(8,128)(2,1)}), bf16[32,4,8,512]{3,2,1,0:T(8,128)(2,1)S(1)}, u32[]{:S(2)}, u32[]{:S(2)}) async-start(bf16[32,4,8,512]{3,2,1,0:T(8,128)(2,1)} %broadcast_in_dim.7), calls=%async_computation.3 | async-start | bytes 2097152 | tf_op jit(solution)/shard_map/all_to_all | solution.py:26
  132.5 3.6 %collective-permute-start.14 = (bf16[32,16,512]{2,1,0:T(8,128)(2,1)}, bf16[32,16,512]{2,1,0:T(8,128)(2,1)S(1)}, u32[]{:S(2)}, u32[]{:S(2)}) collective-permute-start(bf16[32,16,512]{2,1,0:T(8,128)(2,1)} %copy-done.3), channel_id=1, source_target_pairs={{0,12},{4,0},{8,4},{12,8},{1,13},{5,1},{9,5},{13,9},{2,14},{6,2},{... | collective-permute-start | bytes 1572872 | tf_op jit(solution)/shard_map/ppermute | solution.py:42
  138.1 2.5 %collective-permute-start.12 = (bf16[32,16,512]{2,1,0:T(8,128)(2,1)}, bf16[32,16,512]{2,1,0:T(8,128)(2,1)}, u32[]{:S(2)}, u32[]{:S(2)}) collective-permute-start(bf16[32,16,512]{2,1,0:T(8,128)(2,1)} %copy-done.3), channel_id=1, source_target_pairs={{0,4},{4,8},{8,12},{12,0},{1,5},{5,9},{9,13},{13,1},{2,6},{6,10},{... | collective-permute-start | bytes 1572872 | tf_op jit(solution)/shard_map/ppermute | solution.py:42
  144.5 3.6 %collective-permute-done.13 = bf16[32,16,512]{2,1,0:T(8,128)(2,1)S(1)} collective-permute-done((bf16[32,16,512]{2,1,0:T(8,128)(2,1)}, bf16[32,16,512]{2,1,0:T(8,128)(2,1)S(1)}, u32[]{:S(2)}, u32[]{:S(2)}) %collective-permute-start.13) | collective-permute-done | bytes 524320 | tf_op jit(solution)/shard_map/ppermute | solution.py:42
  148.9 15.0 %collective-permute-done.12 = bf16[32,16,512]{2,1,0:T(8,128)(2,1)} collective-permute-done((bf16[32,16,512]{2,1,0:T(8,128)(2,1)}, bf16[32,16,512]{2,1,0:T(8,128)(2,1)}, u32[]{:S(2)}, u32[]{:S(2)}) %collective-permute-start.12) | collective-permute-done | bytes 524320 | tf_op jit(solution)/shard_map/ppermute | solution.py:42
  164.9 3.2 %joined.1 = bf16[8,4,96,512]{3,2,1,0:T(8,128)(2,1)} custom-call(s32[1]{0:T(128)} %bitcast.me_ref, bf16[8,4,16,512]{3,2,1,0:T(8,128)(2,1)} %bitcast.83, bf16[8,4,16,512]{3,2,1,0:T(8,128)(2,1)} %bitcast.34.refs_1_, bf16[8,4,16,512]{3,2,1,0:T(8,128)(2,1)} %bitcast.88, bf16[8,4,16,512]{3,2,1,0:T(8,128)(2,1)} %bitcast.87, bf16[8,4,4,8,512]{4,3,2,1,0:T(8,128)(2,1)} %bitcast.81), custom_call_target="tpu_custom_call" | custom-call | tf_op jit(solution)/shard_map/joined/pallas_call | solution.py:111
  (74 shorter events, 27.0 us)
Async XLA Ops:
  5.8 64.3 %all-to-all-start = ((f16[32,4,24,256]{3,2,1,0:T(8,128)(2,1)}), f16[32,4,24,256]{3,2,1,0:T(8,128)(2,1)}, u32[]{:S(2)}, u32[]{:S(2)}) async-start(f16[32,4,24,256]{3,2,1,0:T(8,128)(2,1)} %bitcast.80), calls=%async_computation | async-start | bytes 3145728 | tf_op jit(solution)/shard_map/all_to_all | solution.py:26
  19.6 16.1 %collective-permute-start = (f32[28,512]{1,0:T(8,128)S(1)}, f32[28,512]{1,0:T(8,128)S(1)}, u32[]{:S(2)}, u32[]{:S(2)}) collective-permute-start(f32[28,512]{1,0:T(8,128)S(1)} %pad_maximum_fusion.1), channel_id=1, source_target_pairs={{0,128},{128,0},{1,129},{129,1},{2,130},{130,2},{3,131},{131,3},{4... | collective-permute-start | bytes 172040 | tf_op jit(solution)/shard_map/ppermute | solution.py:42
  26.4 35.8 %collective-permute-start.3 = (f16[8,96,256]{2,1,0:T(8,128)(2,1)S(1)}, f16[8,96,256]{2,1,0:T(8,128)(2,1)}, u32[]{:S(2)}, u32[]{:S(2)}) collective-permute-start(f16[8,96,256]{2,1,0:T(8,128)(2,1)S(1)} %get-tuple-element.25), channel_id=1, source_target_pairs={{0,8},{4,12},{8,0},{12,4},{1,9},{5,13},{9,1},{13,5},{2,10},{6,14},... | collective-permute-start | bytes 1179656 | tf_op jit(solution)/shard_map/ppermute | solution.py:42
  30.4 18.1 %collective-permute-start.2 = (f16[8,96,256]{2,1,0:T(8,128)(2,1)}, f16[8,96,256]{2,1,0:T(8,128)(2,1)}, u32[]{:S(2)}, u32[]{:S(2)}) collective-permute-start(f16[8,96,256]{2,1,0:T(8,128)(2,1)} %get-tuple-element.26), channel_id=1, source_target_pairs={{0,12},{4,0},{8,4},{12,8},{1,13},{5,1},{9,5},{13,9},{2,14},{6,2},{... | collective-permute-start | bytes 1179656 | tf_op jit(solution)/shard_map/ppermute | solution.py:42
  33.2 16.2 %collective-permute-start.1 = (f16[8,96,256]{2,1,0:T(8,128)(2,1)S(1)}, f16[8,96,256]{2,1,0:T(8,128)(2,1)}, u32[]{:S(2)}, u32[]{:S(2)}) collective-permute-start(f16[8,96,256]{2,1,0:T(8,128)(2,1)S(1)} %get-tuple-element.27), channel_id=1, source_target_pairs={{0,4},{4,8},{8,12},{12,0},{1,5},{5,9},{9,13},{13,1},{2,6},{6,10},{... | collective-permute-start | bytes 1179656 | tf_op jit(solution)/shard_map/ppermute | solution.py:42
  49.4 15.2 %collective-permute-start.5 = (f32[32,512]{1,0:T(8,128)S(1)}, f32[32,512]{1,0:T(8,128)S(1)}, u32[]{:S(2)}, u32[]{:S(2)}) collective-permute-start(f32[32,512]{1,0:T(8,128)S(1)} %pad_maximum_fusion.2), channel_id=1, source_target_pairs={{0,512},{256,0},{512,256},{1,513},{257,1},{513,257},{2,514},{258,2... | collective-permute-start | bytes 196616 | tf_op jit(solution)/shard_map/ppermute | solution.py:42
  60.3 9.1 %collective-permute-start.4 = (f32[32,512]{1,0:T(8,128)S(1)}, f32[32,512]{1,0:T(8,128)S(1)}, u32[]{:S(2)}, u32[]{:S(2)}) collective-permute-start(f32[32,512]{1,0:T(8,128)S(1)} %pad_maximum_fusion.2), channel_id=1, source_target_pairs={{0,256},{256,512},{512,0},{1,257},{257,513},{513,1},{2,258},{258,5... | collective-permute-start | bytes 196616 | tf_op jit(solution)/shard_map/ppermute | solution.py:42
  64.6 35.2 %copy-start.10 = (f32[1,24,512]{2,1,0:T(8,128)S(1)}, f32[1,24,512]{2,1,0:T(8,128)}, u32[]{:S(2)}) copy-start(f32[1,24,512]{2,1,0:T(8,128)} %param.13) | copy-start | bytes 147460
  64.6 35.2 %copy-start.11 = (f32[1,24,512]{2,1,0:T(8,128)S(1)}, f32[1,24,512]{2,1,0:T(8,128)}, u32[]{:S(2)}) copy-start(f32[1,24,512]{2,1,0:T(8,128)} %param.12) | copy-start | bytes 147460
  70.1 30.7 %copy-start.9 = (f32[24,512]{1,0:T(8,128)}, f32[24,512]{1,0:T(8,128)S(1)}, u32[]{:S(2)}) copy-start(f32[24,512]{1,0:T(8,128)S(1)} %multiply_subtract_fusion) | copy-start | bytes 147460
  71.7 28.0 %all-to-all-start.1 = ((f16[32,24,256]{2,1,0:T(8,128)(2,1)}), f16[32,24,256]{2,1,0:T(8,128)(2,1)S(1)}, u32[]{:S(2)}, u32[]{:S(2)}) async-start(f16[32,24,256]{2,1,0:T(8,128)(2,1)} %bitcast.10), calls=%async_computation.1 | async-start | bytes 786432 | tf_op jit(solution)/shard_map/all_to_all | solution.py:26
  86.5 10.0 %collective-permute-start.6 = (f16[24,256]{1,0:T(8,128)(2,1)S(1)}, f16[24,256]{1,0:T(8,128)(2,1)S(1)}, u32[]{:S(2)}, u32[]{:S(2)}) collective-permute-start(f16[24,256]{1,0:T(8,128)(2,1)S(1)} %get-tuple-element.35), channel_id=1, source_target_pairs={{0,4},{4,8},{8,12},{12,0},{1,5},{5,9},{9,13},{13,1},{2,6},{6,10},{... | collective-permute-start | bytes 36872 | tf_op jit(solution)/shard_map/ppermute | solution.py:42
  89.6 6.8 %collective-permute-start.8 = (f16[24,256]{1,0:T(8,128)(2,1)S(1)}, f16[24,256]{1,0:T(8,128)(2,1)S(1)}, u32[]{:S(2)}, u32[]{:S(2)}) collective-permute-start(f16[24,256]{1,0:T(8,128)(2,1)S(1)} %get-tuple-element.36), channel_id=1, source_target_pairs={{0,12},{4,0},{8,4},{12,8},{1,13},{5,1},{9,5},{13,9},{2,14},{6,2},{... | collective-permute-start | bytes 36872 | tf_op jit(solution)/shard_map/ppermute | solution.py:42
  93.0 6.2 %collective-permute-start.7 = (f16[24,256]{1,0:T(8,128)(2,1)S(1)}, f16[24,256]{1,0:T(8,128)(2,1)S(1)}, u32[]{:S(2)}, u32[]{:S(2)}) collective-permute-start(f16[24,256]{1,0:T(8,128)(2,1)S(1)} %get-tuple-element.37), channel_id=1, source_target_pairs={{0,8},{4,12},{8,0},{12,4},{1,9},{5,13},{9,1},{13,5},{2,10},{6,14},... | collective-permute-start | bytes 36872 | tf_op jit(solution)/shard_map/ppermute | solution.py:42
  99.8 24.4 %copy-start.2 = (f16[32,24,256]{2,1,0:T(8,128)(2,1)}, f16[32,24,256]{2,1,0:T(8,128)(2,1)S(1)}, u32[]{:S(2)}) copy-start(f16[32,24,256]{2,1,0:T(8,128)(2,1)S(1)} %all-to-all-done.1) | copy-start | bytes 1179652
  100.8 22.3 %all-to-all-start.2 = ((bf16[32,16,512]{2,1,0:T(8,128)(2,1)}), bf16[32,16,512]{2,1,0:T(8,128)(2,1)S(1)}, u32[]{:S(2)}, u32[]{:S(2)}) async-start(bf16[32,16,512]{2,1,0:T(8,128)(2,1)} %broadcast_in_dim.6), calls=%async_computation.2 | async-start | bytes 1048576 | tf_op jit(solution)/shard_map/all_to_all | solution.py:26
  109.5 32.2 %copy-start.12 = (f32[1,24,512]{2,1,0:T(8,128)S(1)}, f32[1,24,512]{2,1,0:T(8,128)}, u32[]{:S(2)}) copy-start(f32[1,24,512]{2,1,0:T(8,128)} %param.12) | copy-start | bytes 147460
  109.5 10.0 %collective-permute-start.10 = (bf16[8,512]{1,0:T(8,128)(2,1)S(1)}, bf16[8,512]{1,0:T(8,128)(2,1)S(1)}, u32[]{:S(2)}, u32[]{:S(2)}) collective-permute-start(bf16[8,512]{1,0:T(8,128)(2,1)S(1)} %get-tuple-element.43), channel_id=1, source_target_pairs={{0,8},{4,12},{8,0},{12,4},{1,9},{5,13},{9,1},{13,5},{2,10},{6,14},... | collective-permute-start | bytes 24584 | tf_op jit(solution)/shard_map/ppermute | solution.py:42
  113.0 6.5 %collective-permute-start.9 = (bf16[8,512]{1,0:T(8,128)(2,1)S(1)}, bf16[8,512]{1,0:T(8,128)(2,1)S(1)}, u32[]{:S(2)}, u32[]{:S(2)}) collective-permute-start(bf16[8,512]{1,0:T(8,128)(2,1)S(1)} %get-tuple-element.43), channel_id=1, source_target_pairs={{0,4},{4,8},{8,12},{12,0},{1,5},{5,9},{9,13},{13,1},{2,6},{6,10},{... | collective-permute-start | bytes 24584 | tf_op jit(solution)/shard_map/ppermute | solution.py:42
  115.2 5.0 %collective-permute-start.11 = (bf16[8,512]{1,0:T(8,128)(2,1)S(1)}, bf16[8,512]{1,0:T(8,128)(2,1)S(1)}, u32[]{:S(2)}, u32[]{:S(2)}) collective-permute-start(bf16[8,512]{1,0:T(8,128)(2,1)S(1)} %get-tuple-element.43), channel_id=1, source_target_pairs={{0,12},{4,0},{8,4},{12,8},{1,13},{5,1},{9,5},{13,9},{2,14},{6,2},{... | collective-permute-start | bytes 24584 | tf_op jit(solution)/shard_map/ppermute | solution.py:42
  124.2 39.8 %all-to-all-start.3 = ((bf16[32,4,8,512]{3,2,1,0:T(8,128)(2,1)}), bf16[32,4,8,512]{3,2,1,0:T(8,128)(2,1)S(1)}, u32[]{:S(2)}, u32[]{:S(2)}) async-start(bf16[32,4,8,512]{3,2,1,0:T(8,128)(2,1)} %broadcast_in_dim.7), calls=%async_computation.3 | async-start | bytes 2097152 | tf_op jit(solution)/shard_map/all_to_all | solution.py:26
  132.5 12.0 %collective-permute-start.14 = (bf16[32,16,512]{2,1,0:T(8,128)(2,1)}, bf16[32,16,512]{2,1,0:T(8,128)(2,1)S(1)}, u32[]{:S(2)}, u32[]{:S(2)}) collective-permute-start(bf16[32,16,512]{2,1,0:T(8,128)(2,1)} %copy-done.3), channel_id=1, source_target_pairs={{0,12},{4,0},{8,4},{12,8},{1,13},{5,1},{9,5},{13,9},{2,14},{6,2},{... | collective-permute-start | bytes 1572872 | tf_op jit(solution)/shard_map/ppermute | solution.py:42
  136.1 12.0 %collective-permute-start.13 = (bf16[32,16,512]{2,1,0:T(8,128)(2,1)}, bf16[32,16,512]{2,1,0:T(8,128)(2,1)S(1)}, u32[]{:S(2)}, u32[]{:S(2)}) collective-permute-start(bf16[32,16,512]{2,1,0:T(8,128)(2,1)} %copy-done.3), channel_id=1, source_target_pairs={{0,8},{4,12},{8,0},{12,4},{1,9},{5,13},{9,1},{13,5},{2,10},{6,14},... | collective-permute-start | bytes 1572872 | tf_op jit(solution)/shard_map/ppermute | solution.py:42
  138.1 25.8 %collective-permute-start.12 = (bf16[32,16,512]{2,1,0:T(8,128)(2,1)}, bf16[32,16,512]{2,1,0:T(8,128)(2,1)}, u32[]{:S(2)}, u32[]{:S(2)}) collective-permute-start(bf16[32,16,512]{2,1,0:T(8,128)(2,1)} %copy-done.3), channel_id=1, source_target_pairs={{0,4},{4,8},{8,12},{12,0},{1,5},{5,9},{9,13},{13,1},{2,6},{6,10},{... | collective-permute-start | bytes 1572872 | tf_op jit(solution)/shard_map/ppermute | solution.py:42
  (10 other events, 68.0 us)

commit v5 on v4

--- a/solution.py
+++ b/solution.py
@@ -64,11 +64,15 @@
     return [x] + [passed(x, axis, k) for k in range(1, lax.axis_size(axis))]
 
 
-def placed_along(x, axis):
+def in_order(arrived, axis):
     n = lax.axis_size(axis)
     me = lax.axis_index(axis)
-    blocks = jnp.stack(arrived_along(x, axis))
+    blocks = jnp.stack(arrived)
     return jnp.stack([block_of(blocks, turned(me + n - i, n), 0) for i in range(n)])
+
+
+def placed_along(x, axis):
+    return in_order(arrived_along(x, axis), axis)
 
 
 def joining(me_ref, *refs):
@@ -141,9 +145,8 @@
 
     core = lax.axis_index(CORE)
     hi = lax.axis_index(HI)
-    deltas = global_params - own_local
-    mine = jnp.concatenate([deltas, outer_momentum[0]], 0)
-    other = passed(mine, CORE, 1)
+    mine = jnp.concatenate([own_local, outer_momentum[0]], 0)
+    chips = arrived_along(mine, HI)
 
     half = width // 2
 
@@ -153,16 +156,22 @@
         ).astype(jnp.float16)
 
     term_b = product(cotangent[:, half:]).reshape(ny, nx, nz, rows, half)
-    got_b = exchanged(term_b.transpose(0, 2, 1, 3, 4).reshape(plane, nx, rows, half), YZ)
+    term_b = term_b.transpose(0, 2, 1, 3, 4).reshape(plane, nx, rows, half)
+    term_b, chips = lax.optimization_barrier((term_b, chips))
+    got_b = exchanged(term_b, YZ)
     term_a = product(cotangent[:, :half]).reshape(ny, nx, nz * rows, half)
     got_a = terms_along(blocks_along(term_a, X, 1), X)
 
-    first, second = jnp.where(core == 0, mine, other), jnp.where(core == 0, other, mine)
-    pair = jnp.concatenate([mine[:rows] + other[:rows], first[rows:], second[rows:]], 0)
-    pair, got_a[1], got_a[3] = lax.optimization_barrier((pair, got_a[1], got_a[3]))
-    by_chip = placed_along(pair, HI)
-    outer_grad = sum(p[:rows] for p in by_chip) / replicas
-    old_rows = jnp.concatenate([p[rows:] for p in by_chip], 0)
+    chips, got_a[1] = lax.optimization_barrier((chips, got_a[1]))
+    by_chip = in_order(chips, HI)
+    summed = jnp.concatenate(
+        [sum(global_params - c[:rows] for c in by_chip)] + [c[rows:] for c in by_chip], 0
+    )
+    other = passed(summed, CORE, 1)
+    outer_grad = (summed[:rows] + other[:rows]) / replicas
+    by_core = jnp.where(core == 0, jnp.stack([summed, other]), jnp.stack([other, summed]))
+    old_rows = by_core[:, rows:].reshape(n_core, n_hi, sub_rows, width)
+    old_rows = old_rows.transpose(1, 0, 2, 3).reshape(rows, width)
     momentum_all = outer_mu * old_rows + outer_grad
     global_new = global_params - outer_rate * (outer_grad + outer_mu * momentum_all)
     momentum_new = lax.dynamic_slice_in_dim(

time: 169 us -> 170 us (level)
  waiting for transfers between devices: 45.9 us -> 48.4 us
  starting transfers between devices: 99 us -> 97.1 us
    all_to_all x4, waiting for transfers between devices: 3.28 us -> 12.4 us  [exchanged(): return lax.all_to_all(x, axes, 0, 0, tiled=True)]
    all_to_all x4, starting transfers between devices: 45.4 us -> 37.7 us  [exchanged(): return lax.all_to_all(x, axes, 0, 0, tiled=True)]
    ppermute x15, waiting for transfers between devices: 42.6 us -> 36 us  [passed(): return lax.ppermute(x, axis, [(i, (i + step) % n) for i in range(n)])]
    ppermute x15, starting transfers between devices: 53.6 us -> 59.4 us  [passed(): return lax.ppermute(x, axis, [(i, (i + step) % n) for i in range(n)])]
    unnamed x30 -> x28, local copies, waits for them, and re-layouts: 4.68 us -> 2.99 us
  transfers between devices with their start and end apart: 19 -> 19, of which waited for: 10 -> 10; matrix products, arithmetic and copies ran while one was open for 4% -> 6% of each run, Pallas kernels for 0% -> 0%
where the time goes in v5:
time: 170 us; the launch traced here: 168 us
  starting transfers between devices  97.1 us (57%)
  waiting for transfers between devices  48.4 us (28%)
  local copies, waits for them, and re-layouts  8.33 us (5%)
  other arithmetic  6.89 us (4%)
  Pallas kernels  3.18 us (2%)
  matrix products  2.97 us (2%)
    ppermute x15, starting transfers between devices, passed(): return lax.ppermute(x, axis, [(i, (i + step) % n) for i in range(n)])  59.4 us
    all_to_all x4, starting transfers between devices, exchanged(): return lax.all_to_all(x, axes, 0, 0, tiled=True)  37.7 us
    ppermute x15, waiting for transfers between devices, passed(): return lax.ppermute(x, axis, [(i, (i + step) % n) for i in range(n)])  36 us
    all_to_all x4, waiting for transfers between devices, exchanged(): return lax.all_to_all(x, axes, 0, 0, tiled=True)  12.4 us
  transfers between devices with their start and end apart: 19, of which 10 were waited for; matrix products, arithmetic and copies ran while one was open for 6% of the time, Pallas kernels for 0%

profile of v5, /device:TPU:1, one launch (start us, length us, event | category | flops | bytes accessed | tf_op | source)
XLA Modules:
  0.0 168.0 jit_solution(17960541591856877049)
XLA Ops:
  1.6 15.1 %collective-permute-start.1 = (f32[28,512]{1,0:T(8,128)S(1)}, f32[28,512]{1,0:T(8,128)S(1)}, u32[]{:S(2)}, u32[]{:S(2)}) collective-permute-start(f32[28,512]{1,0:T(8,128)S(1)} %pad_maximum_fusion.4), channel_id=1, source_target_pairs={{0,512},{256,0},{512,256},{1,513},{257,1},{513,257},{2,514},{258,2... | collective-permute-start | bytes 172040 | tf_op jit(solution)/shard_map/ppermute | solution.py:42
  22.2 4.1 %collective-permute-done = f32[28,512]{1,0:T(8,128)S(1)} collective-permute-done((f32[28,512]{1,0:T(8,128)S(1)}, f32[28,512]{1,0:T(8,128)S(1)}, u32[]{:S(2)}, u32[]{:S(2)}) %collective-permute-start) | collective-permute-done | bytes 57376 | tf_op jit(solution)/shard_map/ppermute | solution.py:42
  26.2 14.1 %all-to-all-start = ((f16[32,4,24,256]{3,2,1,0:T(8,128)(2,1)}), f16[32,4,24,256]{3,2,1,0:T(8,128)(2,1)}, u32[]{:S(2)}, u32[]{:S(2)}) async-start(f16[32,4,24,256]{3,2,1,0:T(8,128)(2,1)} %bitcast.98), calls=%async_computation | async-start | bytes 3145728 | tf_op jit(solution)/shard_map/all_to_all | solution.py:26
  43.6 3.1 %collective-permute-start.2 = (f16[8,96,256]{2,1,0:T(8,128)(2,1)}, f16[8,96,256]{2,1,0:T(8,128)(2,1)}, u32[]{:S(2)}, u32[]{:S(2)}) collective-permute-start(f16[8,96,256]{2,1,0:T(8,128)(2,1)} %get-tuple-element.35), channel_id=1, source_target_pairs={{0,4},{4,8},{8,12},{12,0},{1,5},{5,9},{9,13},{13,1},{2,6},{6,10},{... | collective-permute-start | bytes 1179656 | tf_op jit(solution)/shard_map/ppermute | solution.py:42
  46.7 3.4 %collective-permute-start.4 = (f16[8,96,256]{2,1,0:T(8,128)(2,1)S(1)}, f16[8,96,256]{2,1,0:T(8,128)(2,1)}, u32[]{:S(2)}, u32[]{:S(2)}) collective-permute-start(f16[8,96,256]{2,1,0:T(8,128)(2,1)S(1)} %get-tuple-element.36), channel_id=1, source_target_pairs={{0,12},{4,0},{8,4},{12,8},{1,13},{5,1},{9,5},{13,9},{2,14},{6,2},{... | collective-permute-start | bytes 1179656 | tf_op jit(solution)/shard_map/ppermute | solution.py:42
  50.1 3.4 %collective-permute-start.3 = (f16[8,96,256]{2,1,0:T(8,128)(2,1)S(1)}, f16[8,96,256]{2,1,0:T(8,128)(2,1)}, u32[]{:S(2)}, u32[]{:S(2)}) collective-permute-start(f16[8,96,256]{2,1,0:T(8,128)(2,1)S(1)} %get-tuple-element.37), channel_id=1, source_target_pairs={{0,8},{4,12},{8,0},{12,4},{1,9},{5,13},{9,1},{13,5},{2,10},{6,14},... | collective-permute-start | bytes 1179656 | tf_op jit(solution)/shard_map/ppermute | solution.py:42
  53.6 3.3 %collective-permute-done.2 = f16[8,96,256]{2,1,0:T(8,128)(2,1)} collective-permute-done((f16[8,96,256]{2,1,0:T(8,128)(2,1)}, f16[8,96,256]{2,1,0:T(8,128)(2,1)}, u32[]{:S(2)}, u32[]{:S(2)}) %collective-permute-start.2) | collective-permute-done | bytes 393248 | tf_op jit(solution)/shard_map/ppermute | solution.py:42
  57.0 3.9 %collective-permute-start.5 = (f32[36,512]{1,0:T(8,128)S(1)}, f32[36,512]{1,0:T(8,128)S(1)}, u32[]{:S(2)}, u32[]{:S(2)}) collective-permute-start(f32[36,512]{1,0:T(8,128)S(1)} %get-tuple-element.42), channel_id=1, source_target_pairs={{0,128},{128,0},{1,129},{129,1},{2,130},{130,2},{3,131},{131,3},{4... | collective-permute-start | bytes 221192 | tf_op jit(solution)/shard_map/ppermute | solution.py:42
  60.8 5.4 %collective-permute-done.3 = f16[8,96,256]{2,1,0:T(8,128)(2,1)} collective-permute-done((f16[8,96,256]{2,1,0:T(8,128)(2,1)S(1)}, f16[8,96,256]{2,1,0:T(8,128)(2,1)}, u32[]{:S(2)}, u32[]{:S(2)}) %collective-permute-start.3) | collective-permute-done | bytes 393248 | tf_op jit(solution)/shard_map/ppermute | solution.py:42
  69.4 9.6 %all-to-all-done = f16[32,4,24,256]{3,2,1,0:T(8,128)(2,1)} async-done(((f16[32,4,24,256]{3,2,1,0:T(8,128)(2,1)}), f16[32,4,24,256]{3,2,1,0:T(8,128)(2,1)}, u32[]{:S(2)}, u32[]{:S(2)}) %all-to-all-start) | async-done | bytes 1572896 | tf_op jit(solution)/shard_map/all_to_all | solution.py:26
  80.7 6.9 %all-to-all-start.1 = ((f16[32,24,256]{2,1,0:T(8,128)(2,1)}), f16[32,24,256]{2,1,0:T(8,128)(2,1)S(1)}, u32[]{:S(2)}, u32[]{:S(2)}) async-start(f16[32,24,256]{2,1,0:T(8,128)(2,1)} %bitcast.13), calls=%async_computation.1 | async-start | bytes 786432 | tf_op jit(solution)/shard_map/all_to_all | solution.py:26
  87.6 3.1 %collective-permute-start.6 = (f16[24,256]{1,0:T(8,128)(2,1)S(1)}, f16[24,256]{1,0:T(8,128)(2,1)S(1)}, u32[]{:S(2)}, u32[]{:S(2)}) collective-permute-start(f16[24,256]{1,0:T(8,128)(2,1)S(1)} %get-tuple-element.45), channel_id=1, source_target_pairs={{0,4},{4,8},{8,12},{12,0},{1,5},{5,9},{9,13},{13,1},{2,6},{6,10},{... | collective-permute-start | bytes 36872 | tf_op jit(solution)/shard_map/ppermute | solution.py:42
  90.8 3.4 %collective-permute-start.8 = (f16[24,256]{1,0:T(8,128)(2,1)S(1)}, f16[24,256]{1,0:T(8,128)(2,1)S(1)}, u32[]{:S(2)}, u32[]{:S(2)}) collective-permute-start(f16[24,256]{1,0:T(8,128)(2,1)S(1)} %get-tuple-element.46), channel_id=1, source_target_pairs={{0,12},{4,0},{8,4},{12,8},{1,13},{5,1},{9,5},{13,9},{2,14},{6,2},{... | collective-permute-start | bytes 36872 | tf_op jit(solution)/shard_map/ppermute | solution.py:42
  94.1 3.4 %collective-permute-start.7 = (f16[24,256]{1,0:T(8,128)(2,1)S(1)}, f16[24,256]{1,0:T(8,128)(2,1)S(1)}, u32[]{:S(2)}, u32[]{:S(2)}) collective-permute-start(f16[24,256]{1,0:T(8,128)(2,1)S(1)} %get-tuple-element.47), channel_id=1, source_target_pairs={{0,8},{4,12},{8,0},{12,4},{1,9},{5,13},{9,1},{13,5},{2,10},{6,14},... | collective-permute-start | bytes 36872 | tf_op jit(solution)/shard_map/ppermute | solution.py:42
  97.6 2.8 %collective-permute-done.7 = f16[24,256]{1,0:T(8,128)(2,1)S(1)} collective-permute-done((f16[24,256]{1,0:T(8,128)(2,1)S(1)}, f16[24,256]{1,0:T(8,128)(2,1)S(1)}, u32[]{:S(2)}, u32[]{:S(2)}) %collective-permute-start.7) | collective-permute-done | bytes 12320 | tf_op jit(solution)/shard_map/ppermute | solution.py:42
  101.4 9.2 %all-to-all-start.2 = ((bf16[32,16,512]{2,1,0:T(8,128)(2,1)}), bf16[32,16,512]{2,1,0:T(8,128)(2,1)S(1)}, u32[]{:S(2)}, u32[]{:S(2)}) async-start(bf16[32,16,512]{2,1,0:T(8,128)(2,1)} %broadcast_in_dim.6), calls=%async_computation.2 | async-start | bytes 1048576 | tf_op jit(solution)/shard_map/all_to_all | solution.py:26
  110.7 3.4 %collective-permute-start.10 = (bf16[8,512]{1,0:T(8,128)(2,1)S(1)}, bf16[8,512]{1,0:T(8,128)(2,1)S(1)}, u32[]{:S(2)}, u32[]{:S(2)}) collective-permute-start(bf16[8,512]{1,0:T(8,128)(2,1)S(1)} %get-tuple-element.53), channel_id=1, source_target_pairs={{0,8},{4,12},{8,0},{12,4},{1,9},{5,13},{9,1},{13,5},{2,10},{6,14},... | collective-permute-start | bytes 24584 | tf_op jit(solution)/shard_map/ppermute | solution.py:42
  116.4 4.3 %collective-permute-start.11 = (bf16[8,512]{1,0:T(8,128)(2,1)S(1)}, bf16[8,512]{1,0:T(8,128)(2,1)S(1)}, u32[]{:S(2)}, u32[]{:S(2)}) collective-permute-start(bf16[8,512]{1,0:T(8,128)(2,1)S(1)} %get-tuple-element.53), channel_id=1, source_target_pairs={{0,12},{4,0},{8,4},{12,8},{1,13},{5,1},{9,5},{13,9},{2,14},{6,2},{... | collective-permute-start | bytes 24584 | tf_op jit(solution)/shard_map/ppermute | solution.py:42
  121.4 2.8 %all-to-all-done.2 = bf16[32,16,512]{2,1,0:T(8,128)(2,1)S(1)} async-done(((bf16[32,16,512]{2,1,0:T(8,128)(2,1)}), bf16[32,16,512]{2,1,0:T(8,128)(2,1)S(1)}, u32[]{:S(2)}, u32[]{:S(2)}) %all-to-all-start.2) | async-done | bytes 524320 | tf_op jit(solution)/shard_map/all_to_all | solution.py:26
  125.4 7.5 %all-to-all-start.3 = ((bf16[32,4,8,512]{3,2,1,0:T(8,128)(2,1)}), bf16[32,4,8,512]{3,2,1,0:T(8,128)(2,1)S(1)}, u32[]{:S(2)}, u32[]{:S(2)}) async-start(bf16[32,4,8,512]{3,2,1,0:T(8,128)(2,1)} %broadcast_in_dim.7), calls=%async_computation.3 | async-start | bytes 2097152 | tf_op jit(solution)/shard_map/all_to_all | solution.py:26
  132.9 4.4 %collective-permute-start.14 = (bf16[32,16,512]{2,1,0:T(8,128)(2,1)}, bf16[32,16,512]{2,1,0:T(8,128)(2,1)S(1)}, u32[]{:S(2)}, u32[]{:S(2)}) collective-permute-start(bf16[32,16,512]{2,1,0:T(8,128)(2,1)} %copy-done.3), channel_id=1, source_target_pairs={{0,12},{4,0},{8,4},{12,8},{1,13},{5,1},{9,5},{13,9},{2,14},{6,2},{... | collective-permute-start | bytes 1572872 | tf_op jit(solution)/shard_map/ppermute | solution.py:42
  145.3 4.0 %collective-permute-done.13 = bf16[32,16,512]{2,1,0:T(8,128)(2,1)S(1)} collective-permute-done((bf16[32,16,512]{2,1,0:T(8,128)(2,1)}, bf16[32,16,512]{2,1,0:T(8,128)(2,1)S(1)}, u32[]{:S(2)}, u32[]{:S(2)}) %collective-permute-start.13) | collective-permute-done | bytes 524320 | tf_op jit(solution)/shard_map/ppermute | solution.py:42
  150.1 13.8 %collective-permute-done.12 = bf16[32,16,512]{2,1,0:T(8,128)(2,1)} collective-permute-done((bf16[32,16,512]{2,1,0:T(8,128)(2,1)}, bf16[32,16,512]{2,1,0:T(8,128)(2,1)}, u32[]{:S(2)}, u32[]{:S(2)}) %collective-permute-start.12) | collective-permute-done | bytes 524320 | tf_op jit(solution)/shard_map/ppermute | solution.py:42
  164.9 3.2 %joined.1 = bf16[8,4,96,512]{3,2,1,0:T(8,128)(2,1)} custom-call(s32[1]{0:T(128)} %bitcast.me_ref, bf16[8,4,16,512]{3,2,1,0:T(8,128)(2,1)} %bitcast.101, bf16[8,4,16,512]{3,2,1,0:T(8,128)(2,1)} %bitcast.40.refs_1_, bf16[8,4,16,512]{3,2,1,0:T(8,128)(2,1)} %bitcast.106, bf16[8,4,16,512]{3,2,1,0:T(8,128)(2,1)} %bitcast.105, bf16[8,4,4,8,512]{4,3,2,1,0:T(8,128)(2,1)} %bitcast.99), custom_call_target="tpu_custom_call" | custom-call | tf_op jit(solution)/shard_map/joined/pallas_call | solution.py:115
  (73 shorter events, 29.4 us)
Async XLA Ops:
  1.6 20.6 %collective-permute-start.1 = (f32[28,512]{1,0:T(8,128)S(1)}, f32[28,512]{1,0:T(8,128)S(1)}, u32[]{:S(2)}, u32[]{:S(2)}) collective-permute-start(f32[28,512]{1,0:T(8,128)S(1)} %pad_maximum_fusion.4), channel_id=1, source_target_pairs={{0,512},{256,0},{512,256},{1,513},{257,1},{513,257},{2,514},{258,2... | collective-permute-start | bytes 172040 | tf_op jit(solution)/shard_map/ppermute | solution.py:42
  16.7 9.5 %collective-permute-start = (f32[28,512]{1,0:T(8,128)S(1)}, f32[28,512]{1,0:T(8,128)S(1)}, u32[]{:S(2)}, u32[]{:S(2)}) collective-permute-start(f32[28,512]{1,0:T(8,128)S(1)} %pad_maximum_fusion.4), channel_id=1, source_target_pairs={{0,256},{256,512},{512,0},{1,257},{257,513},{513,1},{2,258},{258,5... | collective-permute-start | bytes 172040 | tf_op jit(solution)/shard_map/ppermute | solution.py:42
  26.2 52.8 %all-to-all-start = ((f16[32,4,24,256]{3,2,1,0:T(8,128)(2,1)}), f16[32,4,24,256]{3,2,1,0:T(8,128)(2,1)}, u32[]{:S(2)}, u32[]{:S(2)}) async-start(f16[32,4,24,256]{3,2,1,0:T(8,128)(2,1)} %bitcast.98), calls=%async_computation | async-start | bytes 3145728 | tf_op jit(solution)/shard_map/all_to_all | solution.py:26
  43.6 13.3 %collective-permute-start.2 = (f16[8,96,256]{2,1,0:T(8,128)(2,1)}, f16[8,96,256]{2,1,0:T(8,128)(2,1)}, u32[]{:S(2)}, u32[]{:S(2)}) collective-permute-start(f16[8,96,256]{2,1,0:T(8,128)(2,1)} %get-tuple-element.35), channel_id=1, source_target_pairs={{0,4},{4,8},{8,12},{12,0},{1,5},{5,9},{9,13},{13,1},{2,6},{6,10},{... | collective-permute-start | bytes 1179656 | tf_op jit(solution)/shard_map/ppermute | solution.py:42
  46.7 14.1 %collective-permute-start.4 = (f16[8,96,256]{2,1,0:T(8,128)(2,1)S(1)}, f16[8,96,256]{2,1,0:T(8,128)(2,1)}, u32[]{:S(2)}, u32[]{:S(2)}) collective-permute-start(f16[8,96,256]{2,1,0:T(8,128)(2,1)S(1)} %get-tuple-element.36), channel_id=1, source_target_pairs={{0,12},{4,0},{8,4},{12,8},{1,13},{5,1},{9,5},{13,9},{2,14},{6,2},{... | collective-permute-start | bytes 1179656 | tf_op jit(solution)/shard_map/ppermute | solution.py:42
  50.1 16.2 %collective-permute-start.3 = (f16[8,96,256]{2,1,0:T(8,128)(2,1)S(1)}, f16[8,96,256]{2,1,0:T(8,128)(2,1)}, u32[]{:S(2)}, u32[]{:S(2)}) collective-permute-start(f16[8,96,256]{2,1,0:T(8,128)(2,1)S(1)} %get-tuple-element.37), channel_id=1, source_target_pairs={{0,8},{4,12},{8,0},{12,4},{1,9},{5,13},{9,1},{13,5},{2,10},{6,14},... | collective-permute-start | bytes 1179656 | tf_op jit(solution)/shard_map/ppermute | solution.py:42
  57.0 11.7 %collective-permute-start.5 = (f32[36,512]{1,0:T(8,128)S(1)}, f32[36,512]{1,0:T(8,128)S(1)}, u32[]{:S(2)}, u32[]{:S(2)}) collective-permute-start(f32[36,512]{1,0:T(8,128)S(1)} %get-tuple-element.42), channel_id=1, source_target_pairs={{0,128},{128,0},{1,129},{129,1},{2,130},{130,2},{3,131},{131,3},{4... | collective-permute-start | bytes 221192 | tf_op jit(solution)/shard_map/ppermute | solution.py:42
  68.6 31.8 %copy-start.9 = (f32[1,24,512]{2,1,0:T(8,128)S(1)}, f32[1,24,512]{2,1,0:T(8,128)}, u32[]{:S(2)}) copy-start(f32[1,24,512]{2,1,0:T(8,128)} %param.9) | copy-start | bytes 147460
  68.6 31.8 %copy-start.10 = (f32[1,24,512]{2,1,0:T(8,128)S(1)}, f32[1,24,512]{2,1,0:T(8,128)}, u32[]{:S(2)}) copy-start(f32[1,24,512]{2,1,0:T(8,128)} %param.13) | copy-start | bytes 147460
  68.6 31.9 %copy-start.11 = (f32[1,24,512]{2,1,0:T(8,128)S(1)}, f32[1,24,512]{2,1,0:T(8,128)}, u32[]{:S(2)}) copy-start(f32[1,24,512]{2,1,0:T(8,128)} %param.12) | copy-start | bytes 147460
  68.8 32.6 %copy-start.8 = (f32[24,512]{1,0:T(8,128)}, f32[24,512]{1,0:T(8,128)S(1)}, u32[]{:S(2)}) copy-start(f32[24,512]{1,0:T(8,128)S(1)} %get-tuple-element.15) | copy-start | bytes 147460
  80.7 19.7 %all-to-all-start.1 = ((f16[32,24,256]{2,1,0:T(8,128)(2,1)}), f16[32,24,256]{2,1,0:T(8,128)(2,1)S(1)}, u32[]{:S(2)}, u32[]{:S(2)}) async-start(f16[32,24,256]{2,1,0:T(8,128)(2,1)} %bitcast.13), calls=%async_computation.1 | async-start | bytes 786432 | tf_op jit(solution)/shard_map/all_to_all | solution.py:26
  87.6 10.0 %collective-permute-start.6 = (f16[24,256]{1,0:T(8,128)(2,1)S(1)}, f16[24,256]{1,0:T(8,128)(2,1)S(1)}, u32[]{:S(2)}, u32[]{:S(2)}) collective-permute-start(f16[24,256]{1,0:T(8,128)(2,1)S(1)} %get-tuple-element.45), channel_id=1, source_target_pairs={{0,4},{4,8},{8,12},{12,0},{1,5},{5,9},{9,13},{13,1},{2,6},{6,10},{... | collective-permute-start | bytes 36872 | tf_op jit(solution)/shard_map/ppermute | solution.py:42
  90.8 6.8 %collective-permute-start.8 = (f16[24,256]{1,0:T(8,128)(2,1)S(1)}, f16[24,256]{1,0:T(8,128)(2,1)S(1)}, u32[]{:S(2)}, u32[]{:S(2)}) collective-permute-start(f16[24,256]{1,0:T(8,128)(2,1)S(1)} %get-tuple-element.46), channel_id=1, source_target_pairs={{0,12},{4,0},{8,4},{12,8},{1,13},{5,1},{9,5},{13,9},{2,14},{6,2},{... | collective-permute-start | bytes 36872 | tf_op jit(solution)/shard_map/ppermute | solution.py:42
  94.1 6.2 %collective-permute-start.7 = (f16[24,256]{1,0:T(8,128)(2,1)S(1)}, f16[24,256]{1,0:T(8,128)(2,1)S(1)}, u32[]{:S(2)}, u32[]{:S(2)}) collective-permute-start(f16[24,256]{1,0:T(8,128)(2,1)S(1)} %get-tuple-element.47), channel_id=1, source_target_pairs={{0,8},{4,12},{8,0},{12,4},{1,9},{5,13},{9,1},{13,5},{2,10},{6,14},... | collective-permute-start | bytes 36872 | tf_op jit(solution)/shard_map/ppermute | solution.py:42
  101.4 22.8 %all-to-all-start.2 = ((bf16[32,16,512]{2,1,0:T(8,128)(2,1)}), bf16[32,16,512]{2,1,0:T(8,128)(2,1)S(1)}, u32[]{:S(2)}, u32[]{:S(2)}) async-start(bf16[32,16,512]{2,1,0:T(8,128)(2,1)} %broadcast_in_dim.6), calls=%async_computation.2 | async-start | bytes 1048576 | tf_op jit(solution)/shard_map/all_to_all | solution.py:26
  110.7 32.1 %copy-start.12 = (f32[1,24,512]{2,1,0:T(8,128)S(1)}, f32[1,24,512]{2,1,0:T(8,128)}, u32[]{:S(2)}) copy-start(f32[1,24,512]{2,1,0:T(8,128)} %param.12) | copy-start | bytes 147460
  110.7 10.0 %collective-permute-start.10 = (bf16[8,512]{1,0:T(8,128)(2,1)S(1)}, bf16[8,512]{1,0:T(8,128)(2,1)S(1)}, u32[]{:S(2)}, u32[]{:S(2)}) collective-permute-start(bf16[8,512]{1,0:T(8,128)(2,1)S(1)} %get-tuple-element.53), channel_id=1, source_target_pairs={{0,8},{4,12},{8,0},{12,4},{1,9},{5,13},{9,1},{13,5},{2,10},{6,14},... | collective-permute-start | bytes 24584 | tf_op jit(solution)/shard_map/ppermute | solution.py:42
  114.1 6.5 %collective-permute-start.9 = (bf16[8,512]{1,0:T(8,128)(2,1)S(1)}, bf16[8,512]{1,0:T(8,128)(2,1)S(1)}, u32[]{:S(2)}, u32[]{:S(2)}) collective-permute-start(bf16[8,512]{1,0:T(8,128)(2,1)S(1)} %get-tuple-element.53), channel_id=1, source_target_pairs={{0,4},{4,8},{8,12},{12,0},{1,5},{5,9},{9,13},{13,1},{2,6},{6,10},{... | collective-permute-start | bytes 24584 | tf_op jit(solution)/shard_map/ppermute | solution.py:42
  116.4 5.1 %collective-permute-start.11 = (bf16[8,512]{1,0:T(8,128)(2,1)S(1)}, bf16[8,512]{1,0:T(8,128)(2,1)S(1)}, u32[]{:S(2)}, u32[]{:S(2)}) collective-permute-start(bf16[8,512]{1,0:T(8,128)(2,1)S(1)} %get-tuple-element.53), channel_id=1, source_target_pairs={{0,12},{4,0},{8,4},{12,8},{1,13},{5,1},{9,5},{13,9},{2,14},{6,2},{... | collective-permute-start | bytes 24584 | tf_op jit(solution)/shard_map/ppermute | solution.py:42
  125.4 38.4 %all-to-all-start.3 = ((bf16[32,4,8,512]{3,2,1,0:T(8,128)(2,1)}), bf16[32,4,8,512]{3,2,1,0:T(8,128)(2,1)S(1)}, u32[]{:S(2)}, u32[]{:S(2)}) async-start(bf16[32,4,8,512]{3,2,1,0:T(8,128)(2,1)} %broadcast_in_dim.7), calls=%async_computation.3 | async-start | bytes 2097152 | tf_op jit(solution)/shard_map/all_to_all | solution.py:26
  132.9 12.4 %collective-permute-start.14 = (bf16[32,16,512]{2,1,0:T(8,128)(2,1)}, bf16[32,16,512]{2,1,0:T(8,128)(2,1)S(1)}, u32[]{:S(2)}, u32[]{:S(2)}) collective-permute-start(bf16[32,16,512]{2,1,0:T(8,128)(2,1)} %copy-done.3), channel_id=1, source_target_pairs={{0,12},{4,0},{8,4},{12,8},{1,13},{5,1},{9,5},{13,9},{2,14},{6,2},{... | collective-permute-start | bytes 1572872 | tf_op jit(solution)/shard_map/ppermute | solution.py:42
  137.3 12.0 %collective-permute-start.13 = (bf16[32,16,512]{2,1,0:T(8,128)(2,1)}, bf16[32,16,512]{2,1,0:T(8,128)(2,1)S(1)}, u32[]{:S(2)}, u32[]{:S(2)}) collective-permute-start(bf16[32,16,512]{2,1,0:T(8,128)(2,1)} %copy-done.3), channel_id=1, source_target_pairs={{0,8},{4,12},{8,0},{12,4},{1,9},{5,13},{9,1},{13,5},{2,10},{6,14},... | collective-permute-start | bytes 1572872 | tf_op jit(solution)/shard_map/ppermute | solution.py:42
  139.2 24.7 %collective-permute-start.12 = (bf16[32,16,512]{2,1,0:T(8,128)(2,1)}, bf16[32,16,512]{2,1,0:T(8,128)(2,1)}, u32[]{:S(2)}, u32[]{:S(2)}) collective-permute-start(bf16[32,16,512]{2,1,0:T(8,128)(2,1)} %copy-done.3), channel_id=1, source_target_pairs={{0,4},{4,8},{8,12},{12,0},{1,5},{5,9},{9,13},{13,1},{2,6},{6,10},{... | collective-permute-start | bytes 1572872 | tf_op jit(solution)/shard_map/ppermute | solution.py:42
  (9 other events, 84.8 us)

commit v6 on v4

--- a/solution.py
+++ b/solution.py
@@ -50,25 +50,19 @@
     return lax.dynamic_index_in_dim(x, index, dim, keepdims=False)
 
 
-def blocks_along(x, axis, dim):
+def arrived_along(x, axis):
+    return [x] + [passed(x, axis, k) for k in range(1, lax.axis_size(axis))]
+
+
+def in_order(arrived, axis):
     n = lax.axis_size(axis)
     me = lax.axis_index(axis)
-    return [block_of(x, turned(me + k, n), dim) for k in range(n)]
-
-
-def terms_along(blocks, axis):
-    return blocks[:1] + [passed(blocks[k], axis, k) for k in range(1, len(blocks))]
-
-
-def arrived_along(x, axis):
-    return [x] + [passed(x, axis, k) for k in range(1, lax.axis_size(axis))]
+    blocks = jnp.stack(arrived)
+    return jnp.stack([block_of(blocks, turned(me + n - i, n), 0) for i in range(n)])
 
 
 def placed_along(x, axis):
-    n = lax.axis_size(axis)
-    me = lax.axis_index(axis)
-    blocks = jnp.stack(arrived_along(x, axis))
-    return jnp.stack([block_of(blocks, turned(me + n - i, n), 0) for i in range(n)])
+    return in_order(arrived_along(x, axis), axis)
 
 
 def joining(me_ref, *refs):
@@ -145,22 +139,15 @@
     mine = jnp.concatenate([deltas, outer_momentum[0]], 0)
     other = passed(mine, CORE, 1)
 
-    half = width // 2
-
-    def product(columns):
-        return lax.dot_general(
-            features, columns, (((0,), (0,)), ((), ())), preferred_element_type=jnp.float32
-        ).astype(jnp.float16)
-
-    term_b = product(cotangent[:, half:]).reshape(ny, nx, nz, rows, half)
-    got_b = exchanged(term_b.transpose(0, 2, 1, 3, 4).reshape(plane, nx, rows, half), YZ)
-    term_a = product(cotangent[:, :half]).reshape(ny, nx, nz * rows, half)
-    got_a = terms_along(blocks_along(term_a, X, 1), X)
-
-    first, second = jnp.where(core == 0, mine, other), jnp.where(core == 0, other, mine)
-    pair = jnp.concatenate([mine[:rows] + other[:rows], first[rows:], second[rows:]], 0)
-    pair, got_a[1], got_a[3] = lax.optimization_barrier((pair, got_a[1], got_a[3]))
-    by_chip = placed_along(pair, HI)
+    term = lax.dot_general(
+        features, cotangent, (((0,), (0,)), ((), ())), preferred_element_type=jnp.float32
+    ).astype(jnp.float16)
+    along_x = exchanged(term.reshape(ny, nx, nz * rows, width).transpose(1, 0, 2, 3), X)
+
+    upper, lower = jnp.where(core == 0, mine, other), jnp.where(core == 0, other, mine)
+    pair = jnp.concatenate([mine[:rows] + other[:rows], upper[rows:], lower[rows:]], 0)
+    along_x, chips = lax.optimization_barrier((along_x, arrived_along(pair, HI)))
+    by_chip = in_order(chips, HI)
     outer_grad = sum(p[:rows] for p in by_chip) / replicas
     old_rows = jnp.concatenate([p[rows:] for p in by_chip], 0)
     momentum_all = outer_mu * old_rows + outer_grad
@@ -169,14 +156,8 @@
         momentum_all, (hi * n_core + core) * sub_rows, sub_rows, 0
     )
 
-    part_a = total(got_a).astype(jnp.float16).reshape(plane, rows, half)
-    part_b = total(got_b).astype(jnp.float16)
-    part_a, part_b, global_new, momentum_new = lax.optimization_barrier(
-        (part_a, part_b, global_new, momentum_new)
-    )
-    sum_a = exchanged(part_a, YZ)
-    sum_b = terms_along(blocks_along(part_b, X, 0), X)
-    gradient = jnp.concatenate([total(sum_a), total(sum_b)], 1)
+    part = total(along_x).astype(jnp.float16).reshape(plane, rows, width)
+    gradient = total(exchanged(part, YZ))
 
     first_new = beta_one * adam_first[0] + (1.0 - beta_one) * gradient
     second_new = beta_two * adam_second[0] + (1.0 - beta_two) * gradient * gradient

time: 169 us -> 154 us (0.911)
  starting transfers between devices: 99 us -> 80 us
  waiting for transfers between devices: 45.9 us -> 52.2 us
  local copies, waits for them, and re-layouts: 9.94 us -> 7.82 us
    all_to_all x4, waiting for transfers between devices: 3.28 us -> 24.5 us  [exchanged(): return lax.all_to_all(x, axes, 0, 0, tiled=True)]
    ppermute x15 -> x9, starting transfers between devices: 53.6 us -> 37.8 us  [passed(): return lax.ppermute(x, axis, [(i, (i + step) % n) for i in range(n)])]
    ppermute x15 -> x9, waiting for transfers between devices: 42.6 us -> 27.8 us  [passed(): return lax.ppermute(x, axis, [(i, (i + step) % n) for i in range(n)])]
    all_to_all x4, starting transfers between devices: 45.4 us -> 42.2 us  [exchanged(): return lax.all_to_all(x, axes, 0, 0, tiled=True)]
    reshape x0 -> x1, local copies, waits for them, and re-layouts: none -> 2.51 us  [per_device(): term.reshape(ny, nx, nz * rows, width).transpose(1, 0, 2, 3)]
    unnamed x30 -> x16, local copies, waits for them, and re-layouts: 4.68 us -> 2.67 us
    convert_element_type x2 -> x1, other arithmetic: 4.03 us -> 3.26 us  [per_device(): part = total(along_x).astype(jnp.float16).reshape(plane, rows, width)]
  transfers between devices with their start and end apart: 19 -> 13, of which waited for: 10 -> 10; matrix products, arithmetic and copies ran while one was open for 4% -> 1% of each run, Pallas kernels for 0% -> 0%
where the time goes in v6:
time: 154 us; the launch traced here: 153 us
  starting transfers between devices  80 us (52%)
  waiting for transfers between devices  52.2 us (34%)
  local copies, waits for them, and re-layouts  7.82 us (5%)
  other arithmetic  6.22 us (4%)
  Pallas kernels  3.18 us (2%)
  matrix products  2.83 us (2%)
    all_to_all x4, starting transfers between devices, exchanged(): return lax.all_to_all(x, axes, 0, 0, tiled=True)  42.2 us
    ppermute x9, starting transfers between devices, passed(): return lax.ppermute(x, axis, [(i, (i + step) % n) for i in range(n)])  37.8 us
    ppermute x9, waiting for transfers between devices, passed(): return lax.ppermute(x, axis, [(i, (i + step) % n) for i in range(n)])  27.8 us
    all_to_all x4, waiting for transfers between devices, exchanged(): return lax.all_to_all(x, axes, 0, 0, tiled=True)  24.5 us
    convert_element_type x1, other arithmetic, per_device(): part = total(along_x).astype(jnp.float16).reshape(plane, rows, width)  3.26 us
    pallas_call x1, Pallas kernels, joined(): pl.pallas_call(joining, in_specs=[pl.BlockSpec(memory_space=pltpu.SMEM)]...  3.18 us
  transfers between devices with their start and end apart: 13, of which 10 were waited for; matrix products, arithmetic and copies ran while one was open for 1% of the time, Pallas kernels for 0%

profile of v6, /device:TPU:1, one launch (start us, length us, event | category | flops | bytes accessed | tf_op | source)
XLA Modules:
  0.0 153.2 jit_solution(1130604954334499319)
XLA Ops:
  2.3 2.8 %convolution_convert_fusion = f16[3072,512]{1,0:T(8,128)(2,1)S(1)} fusion(bf16[1,384,3072]{2,1,0:T(8,128)(2,1)S(1)} %copy-done, bf16[1,384,512]{2,1,0:T(8,128)(2,1)} %param.8), kind=kOutput, calls=%fused_computation | convolution fusion | flops 1209532416 | bytes 5898240 | tf_op jit(solution)/shard_map/dot_general | solution.py:142
  5.1 2.5 %copy.14 = f16[8,4,96,512]{3,2,0,1:T(8,128)(2,1)} copy(f16[8,4,96,512]{3,2,1,0:T(8,128)(2,1)S(1)} %bitcast.67) | data formatting | bytes 6291456 | tf_op jit(solution)/shard_map/reshape | solution.py:145
  7.7 5.0 %all-to-all-start = ((f16[4,8,96,512]{3,2,1,0:T(8,128)(2,1)}), f16[4,8,96,512]{3,2,1,0:T(8,128)(2,1)}, u32[]{:S(2)}, u32[]{:S(2)}) async-start(f16[4,8,96,512]{3,2,1,0:T(8,128)(2,1)} %bitcast.64), calls=%async_computation | async-start | bytes 6291456 | tf_op jit(solution)/shard_map/all_to_all | solution.py:26
  12.7 12.3 %collective-permute-start = (f32[28,512]{1,0:T(8,128)S(1)}, f32[28,512]{1,0:T(8,128)S(1)}, u32[]{:S(2)}, u32[]{:S(2)}) collective-permute-start(f32[28,512]{1,0:T(8,128)S(1)} %pad_maximum_fusion.1), channel_id=1, source_target_pairs={{0,128},{128,0},{1,129},{129,1},{2,130},{130,2},{3,131},{131,3},{4... | collective-permute-start | bytes 172040 | tf_op jit(solution)/shard_map/ppermute | solution.py:42
  25.9 2.1 %collective-permute-start.1 = (f32[32,512]{1,0:T(8,128)S(1)}, f32[32,512]{1,0:T(8,128)S(1)}, u32[]{:S(2)}, u32[]{:S(2)}) collective-permute-start(f32[32,512]{1,0:T(8,128)S(1)} %pad_maximum_fusion.2), channel_id=1, source_target_pairs={{0,256},{256,512},{512,0},{1,257},{257,513},{513,1},{2,258},{258,5... | collective-permute-start | bytes 196616 | tf_op jit(solution)/shard_map/ppermute | solution.py:42
  27.9 7.3 %collective-permute-start.2 = (f32[32,512]{1,0:T(8,128)S(1)}, f32[32,512]{1,0:T(8,128)}, u32[]{:S(2)}, u32[]{:S(2)}) collective-permute-start(f32[32,512]{1,0:T(8,128)S(1)} %pad_maximum_fusion.2), channel_id=1, source_target_pairs={{0,512},{256,0},{512,256},{1,513},{257,1},{513,257},{2,514},{258,2... | collective-permute-start | bytes 196616 | tf_op jit(solution)/shard_map/ppermute | solution.py:42
  35.2 2.6 %collective-permute-done.2 = f32[32,512]{1,0:T(8,128)} collective-permute-done((f32[32,512]{1,0:T(8,128)S(1)}, f32[32,512]{1,0:T(8,128)}, u32[]{:S(2)}, u32[]{:S(2)}) %collective-permute-start.2) | collective-permute-done | bytes 65568 | tf_op jit(solution)/shard_map/ppermute | solution.py:42
  37.9 3.0 %all-to-all-done = f16[4,8,96,512]{3,2,1,0:T(8,128)(2,1)} async-done(((f16[4,8,96,512]{3,2,1,0:T(8,128)(2,1)}), f16[4,8,96,512]{3,2,1,0:T(8,128)(2,1)}, u32[]{:S(2)}, u32[]{:S(2)}) %all-to-all-start) | async-done | bytes 3145760 | tf_op jit(solution)/shard_map/all_to_all | solution.py:26
  40.8 3.3 %add_convert_fusion = f16[1,8,96,512]{3,2,1,0:T(8,128)(2,1)} fusion(f16[4,8,96,512]{3,2,1,0:T(8,128)(2,1)} %all-to-all-done), kind=kLoop, calls=%fused_computation.3 | loop fusion | flops 3145728 | bytes 3932160 | tf_op jit(solution)/shard_map/convert_element_type | solution.py:159
  44.1 22.2 %all-to-all-start.1 = ((f16[32,24,512]{2,1,0:T(8,128)(2,1)}), f16[32,24,512]{2,1,0:T(8,128)(2,1)S(1)}, u32[]{:S(2)}, u32[]{:S(2)}) async-start(f16[32,24,512]{2,1,0:T(8,128)(2,1)} %bitcast.68), calls=%async_computation.1 | async-start | bytes 1572864 | tf_op jit(solution)/shard_map/all_to_all | solution.py:26
  67.3 19.0 %all-to-all-done.1 = f16[32,24,512]{2,1,0:T(8,128)(2,1)S(1)} async-done(((f16[32,24,512]{2,1,0:T(8,128)(2,1)}), f16[32,24,512]{2,1,0:T(8,128)(2,1)S(1)}, u32[]{:S(2)}, u32[]{:S(2)}) %all-to-all-start.1) | async-done | bytes 786464 | tf_op jit(solution)/shard_map/all_to_all | solution.py:26
  88.6 7.5 %all-to-all-start.2 = ((bf16[32,16,512]{2,1,0:T(8,128)(2,1)}), bf16[32,16,512]{2,1,0:T(8,128)(2,1)S(1)}, u32[]{:S(2)}, u32[]{:S(2)}) async-start(bf16[32,16,512]{2,1,0:T(8,128)(2,1)} %broadcast_in_dim.6), calls=%async_computation.2 | async-start | bytes 1048576 | tf_op jit(solution)/shard_map/all_to_all | solution.py:26
  96.1 2.8 %collective-permute-start.5 = (bf16[8,512]{1,0:T(8,128)(2,1)S(1)}, bf16[8,512]{1,0:T(8,128)(2,1)S(1)}, u32[]{:S(2)}, u32[]{:S(2)}) collective-permute-start(bf16[8,512]{1,0:T(8,128)(2,1)S(1)} %get-tuple-element.33), channel_id=1, source_target_pairs={{0,12},{4,0},{8,4},{12,8},{1,13},{5,1},{9,5},{13,9},{2,14},{6,2},{... | collective-permute-start | bytes 24584 | tf_op jit(solution)/shard_map/ppermute | solution.py:42
  98.9 3.1 %collective-permute-start.4 = (bf16[8,512]{1,0:T(8,128)(2,1)S(1)}, bf16[8,512]{1,0:T(8,128)(2,1)S(1)}, u32[]{:S(2)}, u32[]{:S(2)}) collective-permute-start(bf16[8,512]{1,0:T(8,128)(2,1)S(1)} %get-tuple-element.33), channel_id=1, source_target_pairs={{0,8},{4,12},{8,0},{12,4},{1,9},{5,13},{9,1},{13,5},{2,10},{6,14},... | collective-permute-start | bytes 24584 | tf_op jit(solution)/shard_map/ppermute | solution.py:42
  105.1 2.8 %collective-permute-done.3 = bf16[8,512]{1,0:T(8,128)(2,1)S(1)} collective-permute-done((bf16[8,512]{1,0:T(8,128)(2,1)S(1)}, bf16[8,512]{1,0:T(8,128)(2,1)S(1)}, u32[]{:S(2)}, u32[]{:S(2)}) %collective-permute-start.3) | collective-permute-done | bytes 8224 | tf_op jit(solution)/shard_map/ppermute | solution.py:42
  107.9 2.5 %all-to-all-done.2 = bf16[32,16,512]{2,1,0:T(8,128)(2,1)S(1)} async-done(((bf16[32,16,512]{2,1,0:T(8,128)(2,1)}), bf16[32,16,512]{2,1,0:T(8,128)(2,1)S(1)}, u32[]{:S(2)}, u32[]{:S(2)}) %all-to-all-start.2) | async-done | bytes 524320 | tf_op jit(solution)/shard_map/all_to_all | solution.py:26
  111.6 7.5 %all-to-all-start.3 = ((bf16[32,4,8,512]{3,2,1,0:T(8,128)(2,1)}), bf16[32,4,8,512]{3,2,1,0:T(8,128)(2,1)S(1)}, u32[]{:S(2)}, u32[]{:S(2)}) async-start(bf16[32,4,8,512]{3,2,1,0:T(8,128)(2,1)} %broadcast_in_dim.7), calls=%async_computation.3 | async-start | bytes 2097152 | tf_op jit(solution)/shard_map/all_to_all | solution.py:26
  119.1 2.2 %collective-permute-start.6 = (bf16[32,16,512]{2,1,0:T(8,128)(2,1)}, bf16[32,16,512]{2,1,0:T(8,128)(2,1)}, u32[]{:S(2)}, u32[]{:S(2)}) collective-permute-start(bf16[32,16,512]{2,1,0:T(8,128)(2,1)} %copy-done.2), channel_id=1, source_target_pairs={{0,4},{4,8},{8,12},{12,0},{1,5},{5,9},{9,13},{13,1},{2,6},{6,10},{... | collective-permute-start | bytes 1572872 | tf_op jit(solution)/shard_map/ppermute | solution.py:42
  121.3 3.7 %collective-permute-start.7 = (bf16[32,16,512]{2,1,0:T(8,128)(2,1)}, bf16[32,16,512]{2,1,0:T(8,128)(2,1)}, u32[]{:S(2)}, u32[]{:S(2)}) collective-permute-start(bf16[32,16,512]{2,1,0:T(8,128)(2,1)} %copy-done.2), channel_id=1, source_target_pairs={{0,8},{4,12},{8,0},{12,4},{1,9},{5,13},{9,1},{13,5},{2,10},{6,14},... | collective-permute-start | bytes 1572872 | tf_op jit(solution)/shard_map/ppermute | solution.py:42
  125.0 2.5 %collective-permute-start.8 = (bf16[32,16,512]{2,1,0:T(8,128)(2,1)}, bf16[32,16,512]{2,1,0:T(8,128)(2,1)}, u32[]{:S(2)}, u32[]{:S(2)}) collective-permute-start(bf16[32,16,512]{2,1,0:T(8,128)(2,1)} %copy-done.2), channel_id=1, source_target_pairs={{0,12},{4,0},{8,4},{12,8},{1,13},{5,1},{9,5},{13,9},{2,14},{6,2},{... | collective-permute-start | bytes 1572872 | tf_op jit(solution)/shard_map/ppermute | solution.py:42
  128.7 4.1 %collective-permute-done.6 = bf16[32,16,512]{2,1,0:T(8,128)(2,1)} collective-permute-done((bf16[32,16,512]{2,1,0:T(8,128)(2,1)}, bf16[32,16,512]{2,1,0:T(8,128)(2,1)}, u32[]{:S(2)}, u32[]{:S(2)}) %collective-permute-start.6) | collective-permute-done | bytes 524320 | tf_op jit(solution)/shard_map/ppermute | solution.py:42
  132.9 10.7 %collective-permute-done.7 = bf16[32,16,512]{2,1,0:T(8,128)(2,1)} collective-permute-done((bf16[32,16,512]{2,1,0:T(8,128)(2,1)}, bf16[32,16,512]{2,1,0:T(8,128)(2,1)}, u32[]{:S(2)}, u32[]{:S(2)}) %collective-permute-start.7) | collective-permute-done | bytes 524320 | tf_op jit(solution)/shard_map/ppermute | solution.py:42
  143.6 5.4 %collective-permute-done.8 = bf16[32,16,512]{2,1,0:T(8,128)(2,1)} collective-permute-done((bf16[32,16,512]{2,1,0:T(8,128)(2,1)}, bf16[32,16,512]{2,1,0:T(8,128)(2,1)}, u32[]{:S(2)}, u32[]{:S(2)}) %collective-permute-start.8) | collective-permute-done | bytes 524320 | tf_op jit(solution)/shard_map/ppermute | solution.py:42
  150.0 3.2 %joined.1 = bf16[8,4,96,512]{3,2,1,0:T(8,128)(2,1)} custom-call(s32[1]{0:T(128)} %bitcast.me_ref, bf16[8,4,16,512]{3,2,1,0:T(8,128)(2,1)} %bitcast.69, bf16[8,4,16,512]{3,2,1,0:T(8,128)(2,1)} %bitcast.23.refs_1_, bf16[8,4,16,512]{3,2,1,0:T(8,128)(2,1)} %bitcast.24.refs_2_, bf16[8,4,16,512]{3,2,1,0:T(8,128)(2,1)} %bitcast.25.refs_3_, ...), custom_call_target="tpu_custom_call" | custom-call | tf_op jit(solution)/shard_map/joined/pallas_call | solution.py:105
  (41 shorter events, 12.2 us)
Async XLA Ops:
  0.6 1.7 %copy-start = (bf16[1,384,3072]{2,1,0:T(8,128)(2,1)S(1)}, bf16[1,384,3072]{2,1,0:T(8,128)(2,1)}, u32[]{:S(2)}) copy-start(bf16[1,384,3072]{2,1,0:T(8,128)(2,1)} %param.7) | copy-start | bytes 7077892
  7.6 5.0 %copy-start.4 = (f32[1,24,512]{2,1,0:T(8,128)S(1)}, f32[1,24,512]{2,1,0:T(8,128)}, u32[]{:S(2)}) copy-start(f32[1,24,512]{2,1,0:T(8,128)} %param.9) | copy-start | bytes 147460
  7.6 5.0 %copy-start.5 = (f32[24,512]{1,0:T(8,128)S(1)}, f32[24,512]{1,0:T(8,128)}, u32[]{:S(2)}) copy-start(f32[24,512]{1,0:T(8,128)} %param.10) | copy-start | bytes 147460
  7.7 5.0 %copy-start.7 = (f32[1,4,512]{2,1,0:T(4,128)S(1)}, f32[1,4,512]{2,1,0:T(4,128)}, u32[]{:S(2)}) copy-start(f32[1,4,512]{2,1,0:T(4,128)} %param.11) | copy-start | bytes 24580
  7.7 33.2 %all-to-all-start = ((f16[4,8,96,512]{3,2,1,0:T(8,128)(2,1)}), f16[4,8,96,512]{3,2,1,0:T(8,128)(2,1)}, u32[]{:S(2)}, u32[]{:S(2)}) async-start(f16[4,8,96,512]{3,2,1,0:T(8,128)(2,1)} %bitcast.64), calls=%async_computation | async-start | bytes 6291456 | tf_op jit(solution)/shard_map/all_to_all | solution.py:26
  12.7 13.2 %collective-permute-start = (f32[28,512]{1,0:T(8,128)S(1)}, f32[28,512]{1,0:T(8,128)S(1)}, u32[]{:S(2)}, u32[]{:S(2)}) collective-permute-start(f32[28,512]{1,0:T(8,128)S(1)} %pad_maximum_fusion.1), channel_id=1, source_target_pairs={{0,128},{128,0},{1,129},{129,1},{2,130},{130,2},{3,131},{131,3},{4... | collective-permute-start | bytes 172040 | tf_op jit(solution)/shard_map/ppermute | solution.py:42
  25.9 60.4 %copy-start.3 = (f32[1,24,512]{2,1,0:T(8,128)S(1)}, f32[1,24,512]{2,1,0:T(8,128)}, u32[]{:S(2)}) copy-start(f32[1,24,512]{2,1,0:T(8,128)} %param.13) | copy-start | bytes 147460
  25.9 9.3 %collective-permute-start.1 = (f32[32,512]{1,0:T(8,128)S(1)}, f32[32,512]{1,0:T(8,128)S(1)}, u32[]{:S(2)}, u32[]{:S(2)}) collective-permute-start(f32[32,512]{1,0:T(8,128)S(1)} %pad_maximum_fusion.2), channel_id=1, source_target_pairs={{0,256},{256,512},{512,0},{1,257},{257,513},{513,1},{2,258},{258,5... | collective-permute-start | bytes 196616 | tf_op jit(solution)/shard_map/ppermute | solution.py:42
  27.9 9.9 %collective-permute-start.2 = (f32[32,512]{1,0:T(8,128)S(1)}, f32[32,512]{1,0:T(8,128)}, u32[]{:S(2)}, u32[]{:S(2)}) collective-permute-start(f32[32,512]{1,0:T(8,128)S(1)} %pad_maximum_fusion.2), channel_id=1, source_target_pairs={{0,512},{256,0},{512,256},{1,513},{257,1},{513,257},{2,514},{258,2... | collective-permute-start | bytes 196616 | tf_op jit(solution)/shard_map/ppermute | solution.py:42
  44.1 42.9 %copy-start.6 = (f32[1,24,512]{2,1,0:T(8,128)S(1)}, f32[1,24,512]{2,1,0:T(8,128)}, u32[]{:S(2)}) copy-start(f32[1,24,512]{2,1,0:T(8,128)} %param.12) | copy-start | bytes 147460
  44.1 42.2 %all-to-all-start.1 = ((f16[32,24,512]{2,1,0:T(8,128)(2,1)}), f16[32,24,512]{2,1,0:T(8,128)(2,1)S(1)}, u32[]{:S(2)}, u32[]{:S(2)}) async-start(f16[32,24,512]{2,1,0:T(8,128)(2,1)} %bitcast.68), calls=%async_computation.1 | async-start | bytes 1572864 | tf_op jit(solution)/shard_map/all_to_all | solution.py:26
  88.6 21.9 %all-to-all-start.2 = ((bf16[32,16,512]{2,1,0:T(8,128)(2,1)}), bf16[32,16,512]{2,1,0:T(8,128)(2,1)S(1)}, u32[]{:S(2)}, u32[]{:S(2)}) async-start(bf16[32,16,512]{2,1,0:T(8,128)(2,1)} %broadcast_in_dim.6), calls=%async_computation.2 | async-start | bytes 1048576 | tf_op jit(solution)/shard_map/all_to_all | solution.py:26
  96.1 7.8 %collective-permute-start.5 = (bf16[8,512]{1,0:T(8,128)(2,1)S(1)}, bf16[8,512]{1,0:T(8,128)(2,1)S(1)}, u32[]{:S(2)}, u32[]{:S(2)}) collective-permute-start(bf16[8,512]{1,0:T(8,128)(2,1)S(1)} %get-tuple-element.33), channel_id=1, source_target_pairs={{0,12},{4,0},{8,4},{12,8},{1,13},{5,1},{9,5},{13,9},{2,14},{6,2},{... | collective-permute-start | bytes 24584 | tf_op jit(solution)/shard_map/ppermute | solution.py:42
  98.9 6.2 %collective-permute-start.4 = (bf16[8,512]{1,0:T(8,128)(2,1)S(1)}, bf16[8,512]{1,0:T(8,128)(2,1)S(1)}, u32[]{:S(2)}, u32[]{:S(2)}) collective-permute-start(bf16[8,512]{1,0:T(8,128)(2,1)S(1)} %get-tuple-element.33), channel_id=1, source_target_pairs={{0,8},{4,12},{8,0},{12,4},{1,9},{5,13},{9,1},{13,5},{2,10},{6,14},... | collective-permute-start | bytes 24584 | tf_op jit(solution)/shard_map/ppermute | solution.py:42
  102.0 5.9 %collective-permute-start.3 = (bf16[8,512]{1,0:T(8,128)(2,1)S(1)}, bf16[8,512]{1,0:T(8,128)(2,1)S(1)}, u32[]{:S(2)}, u32[]{:S(2)}) collective-permute-start(bf16[8,512]{1,0:T(8,128)(2,1)S(1)} %get-tuple-element.33), channel_id=1, source_target_pairs={{0,4},{4,8},{8,12},{12,0},{1,5},{5,9},{9,13},{13,1},{2,6},{6,10},{... | collective-permute-start | bytes 24584 | tf_op jit(solution)/shard_map/ppermute | solution.py:42
  110.4 1.1 copy-start.2
  111.6 37.5 %all-to-all-start.3 = ((bf16[32,4,8,512]{3,2,1,0:T(8,128)(2,1)}), bf16[32,4,8,512]{3,2,1,0:T(8,128)(2,1)S(1)}, u32[]{:S(2)}, u32[]{:S(2)}) async-start(bf16[32,4,8,512]{3,2,1,0:T(8,128)(2,1)} %broadcast_in_dim.7), calls=%async_computation.3 | async-start | bytes 2097152 | tf_op jit(solution)/shard_map/all_to_all | solution.py:26
  119.1 13.8 %collective-permute-start.6 = (bf16[32,16,512]{2,1,0:T(8,128)(2,1)}, bf16[32,16,512]{2,1,0:T(8,128)(2,1)}, u32[]{:S(2)}, u32[]{:S(2)}) collective-permute-start(bf16[32,16,512]{2,1,0:T(8,128)(2,1)} %copy-done.2), channel_id=1, source_target_pairs={{0,4},{4,8},{8,12},{12,0},{1,5},{5,9},{9,13},{13,1},{2,6},{6,10},{... | collective-permute-start | bytes 1572872 | tf_op jit(solution)/shard_map/ppermute | solution.py:42
  121.3 22.3 %collective-permute-start.7 = (bf16[32,16,512]{2,1,0:T(8,128)(2,1)}, bf16[32,16,512]{2,1,0:T(8,128)(2,1)}, u32[]{:S(2)}, u32[]{:S(2)}) collective-permute-start(bf16[32,16,512]{2,1,0:T(8,128)(2,1)} %copy-done.2), channel_id=1, source_target_pairs={{0,8},{4,12},{8,0},{12,4},{1,9},{5,13},{9,1},{13,5},{2,10},{6,14},... | collective-permute-start | bytes 1572872 | tf_op jit(solution)/shard_map/ppermute | solution.py:42
  125.0 24.1 %collective-permute-start.8 = (bf16[32,16,512]{2,1,0:T(8,128)(2,1)}, bf16[32,16,512]{2,1,0:T(8,128)(2,1)}, u32[]{:S(2)}, u32[]{:S(2)}) collective-permute-start(bf16[32,16,512]{2,1,0:T(8,128)(2,1)} %copy-done.2), channel_id=1, source_target_pairs={{0,12},{4,0},{8,4},{12,8},{1,13},{5,1},{9,5},{13,9},{2,14},{6,2},{... | collective-permute-start | bytes 1572872 | tf_op jit(solution)/shard_map/ppermute | solution.py:42
  149.0 1.0 copy-start.1

commit v7 on v6

--- a/solution.py
+++ b/solution.py
@@ -65,16 +65,13 @@
     return in_order(arrived_along(x, axis), axis)
 
 
-def joining(me_ref, *refs):
-    *near, far, out, near_in, far_in, held, got, sent = refs
-    places = len(near)
-    ny = far.shape[0]
-    me = me_ref[0]
+def joining(near, far, out, near_in, far_in, held, got, sent):
+    places, ny = near.shape[:2]
 
     def loads(y):
         return [
-            pltpu.make_async_copy(ref.at[y], near_in.at[k, y], got.at[k, y])
-            for k, ref in enumerate(near)
+            pltpu.make_async_copy(near.at[x, y], near_in.at[x, y], got.at[x, y])
+            for x in range(places)
         ] + [pltpu.make_async_copy(far.at[y], far_in.at[y], got.at[places, y])]
 
     def store(y):
@@ -86,10 +83,9 @@
     for y in range(ny):
         for copy in loads(y):
             copy.wait()
-        for k in range(places):
-            x = turned(me + places - k, places)
+        for x in range(places):
             both = jnp.concatenate(
-                [near_in[k, y].astype(jnp.float32), far_in[y, :, x].astype(jnp.float32)], axis=1
+                [near_in[x, y].astype(jnp.float32), far_in[y, :, x].astype(jnp.float32)], axis=1
             )
             held[y, x] = both.reshape(-1, both.shape[-1]).astype(out.dtype)
         store(y).start()
@@ -97,25 +93,24 @@
         store(y).wait()
 
 
-def joined(near, far, me):
-    ny, nz, cut, width = near[0].shape
-    nx, rest = far.shape[2:4]
-    shape = (ny, nx, nz * (cut + rest), width)
+def joined(near, far):
+    nx, ny, nz, cut, width = near.shape
+    shape = (ny, nx, nz * (cut + far.shape[3]), width)
     place = pl.BlockSpec(memory_space=pl.ANY)
     out = pl.pallas_call(
         joining,
-        in_specs=[pl.BlockSpec(memory_space=pltpu.SMEM)] + [place] * (nx + 1),
+        in_specs=[place, place],
         out_specs=place,
         out_shape=jax.ShapeDtypeStruct(shape, far.dtype),
         scratch_shapes=[
-            pltpu.VMEM((nx, *near[0].shape), far.dtype),
+            pltpu.VMEM(near.shape, far.dtype),
             pltpu.VMEM(far.shape, far.dtype),
             pltpu.VMEM(shape, far.dtype),
             pltpu.SemaphoreType.DMA((nx + 1, ny)),
             pltpu.SemaphoreType.DMA((ny,)),
         ],
         name="joined",
-    )(me.reshape(1), *near, far)
+    )(near, far)
     return out.reshape(-1, width)
 
 
@@ -169,9 +164,9 @@
     merged_a, merged_b = merged[:cut], merged[cut:]
     near_b = placed_along(merged_b, X)
     near_a, near_b = lax.optimization_barrier((exchanged(copies(merged_a, plane), YZ), near_b))
-    all_a = [n.reshape(ny, nz, cut, width) for n in arrived_along(near_a, X)]
+    all_a = lax.all_gather(near_a, X).reshape(nx, ny, nz, cut, width)
     all_b = exchanged(copies(near_b, plane), YZ).reshape(ny, nz, nx, rows - cut, width)
-    gathered = joined(all_a, all_b, lax.axis_index(X))
+    gathered = joined(all_a, all_b)
     return (gathered[None], global_new, momentum_new[None], first_new[None], second_new[None])
 
 

time: 154 us -> 169 us (1.097)
  between operations: 0.92 us -> 14.3 us
  waiting for transfers between devices: 52.2 us -> 62.8 us
  starting transfers between devices: 80 us -> 71.6 us
    all_to_all x4, waiting for transfers between devices: 24.5 us -> 50.7 us  [exchanged(): return lax.all_to_all(x, axes, 0, 0, tiled=True)]
    ppermute x9 -> x6, waiting for transfers between devices: 27.8 us -> 7.47 us  [passed(): return lax.ppermute(x, axis, [(i, (i + step) % n) for i in range(n)])]
    ppermute x9 -> x6, starting transfers between devices: 37.8 us -> 29.4 us  [passed(): return lax.ppermute(x, axis, [(i, (i + step) % n) for i in range(n)])]
    all_gather x0 -> x1, waiting for transfers between devices: none -> 4.59 us  [per_device(): all_a = lax.all_gather(near_a, X).reshape(nx, ny, nz, cut, width)]
  transfers between devices with their start and end apart: 13 -> 11, of which waited for: 10 -> 9; matrix products, arithmetic and copies ran while one was open for 1% -> 2% of each run, Pallas kernels for 0% -> 0%
where the time goes in v7:
time: 169 us
  starting transfers between devices  71.6 us (42%)
  waiting for transfers between devices  62.8 us (37%)
  between operations  14.3 us (8%)
  local copies, waits for them, and re-layouts  7.6 us (4%)
  other arithmetic  6.22 us (4%)
  Pallas kernels  3.18 us (2%)
  matrix products  2.83 us (2%)
    all_to_all x4, waiting for transfers between devices, exchanged(): return lax.all_to_all(x, axes, 0, 0, tiled=True)  50.7 us
    all_to_all x4, starting transfers between devices, exchanged(): return lax.all_to_all(x, axes, 0, 0, tiled=True)  42.2 us
    ppermute x6, starting transfers between devices, passed(): return lax.ppermute(x, axis, [(i, (i + step) % n) for i in range(n)])  29.4 us
    ppermute x6, waiting for transfers between devices, passed(): return lax.ppermute(x, axis, [(i, (i + step) % n) for i in range(n)])  7.47 us
    all_gather x1, waiting for transfers between devices, per_device(): all_a = lax.all_gather(near_a, X).reshape(nx, ny, nz, cut, width)  4.59 us
  transfers between devices with their start and end apart: 11, of which 9 were waited for; matrix products, arithmetic and copies ran while one was open for 2% of the time, Pallas kernels for 0%

profile of v7, /device:TPU:1, one launch (start us, length us, event | category | flops | bytes accessed | tf_op | source)
XLA Modules:
  0.0 168.6 jit_solution(2721754862641021371)
XLA Ops:
  7.2 1.7 copy-done
  8.8 2.8 %convolution_convert_fusion = f16[3072,512]{1,0:T(8,128)(2,1)S(1)} fusion(bf16[1,384,3072]{2,1,0:T(8,128)(2,1)S(1)} %copy-done, bf16[1,384,512]{2,1,0:T(8,128)(2,1)} %param.8), kind=kOutput, calls=%fused_computation | convolution fusion | flops 1209532416 | bytes 5898240 | tf_op jit(solution)/shard_map/dot_general | solution.py:137
  11.7 2.5 %copy.14 = f16[8,4,96,512]{3,2,0,1:T(8,128)(2,1)} copy(f16[8,4,96,512]{3,2,1,0:T(8,128)(2,1)S(1)} %bitcast.63) | data formatting | bytes 6291456 | tf_op jit(solution)/shard_map/reshape | solution.py:140
  14.2 5.0 %all-to-all-start = ((f16[4,8,96,512]{3,2,1,0:T(8,128)(2,1)}), f16[4,8,96,512]{3,2,1,0:T(8,128)(2,1)}, u32[]{:S(2)}, u32[]{:S(2)}) async-start(f16[4,8,96,512]{3,2,1,0:T(8,128)(2,1)} %bitcast.60), calls=%async_computation | async-start | bytes 6291456 | tf_op jit(solution)/shard_map/all_to_all | solution.py:26
  19.2 12.3 %collective-permute-start = (f32[28,512]{1,0:T(8,128)S(1)}, f32[28,512]{1,0:T(8,128)S(1)}, u32[]{:S(2)}, u32[]{:S(2)}) collective-permute-start(f32[28,512]{1,0:T(8,128)S(1)} %pad_maximum_fusion.1), channel_id=1, source_target_pairs={{0,128},{128,0},{1,129},{129,1},{2,130},{130,2},{3,131},{131,3},{4... | collective-permute-start | bytes 172040 | tf_op jit(solution)/shard_map/ppermute | solution.py:42
  32.4 2.1 %collective-permute-start.1 = (f32[32,512]{1,0:T(8,128)S(1)}, f32[32,512]{1,0:T(8,128)S(1)}, u32[]{:S(2)}, u32[]{:S(2)}) collective-permute-start(f32[32,512]{1,0:T(8,128)S(1)} %pad_maximum_fusion.2), channel_id=1, source_target_pairs={{0,256},{256,512},{512,0},{1,257},{257,513},{513,1},{2,258},{258,5... | collective-permute-start | bytes 196616 | tf_op jit(solution)/shard_map/ppermute | solution.py:42
  34.5 7.3 %collective-permute-start.2 = (f32[32,512]{1,0:T(8,128)S(1)}, f32[32,512]{1,0:T(8,128)}, u32[]{:S(2)}, u32[]{:S(2)}) collective-permute-start(f32[32,512]{1,0:T(8,128)S(1)} %pad_maximum_fusion.2), channel_id=1, source_target_pairs={{0,512},{256,0},{512,256},{1,513},{257,1},{513,257},{2,514},{258,2... | collective-permute-start | bytes 196616 | tf_op jit(solution)/shard_map/ppermute | solution.py:42
  41.8 2.6 %collective-permute-done.2 = f32[32,512]{1,0:T(8,128)} collective-permute-done((f32[32,512]{1,0:T(8,128)S(1)}, f32[32,512]{1,0:T(8,128)}, u32[]{:S(2)}, u32[]{:S(2)}) %collective-permute-start.2) | collective-permute-done | bytes 65568 | tf_op jit(solution)/shard_map/ppermute | solution.py:42
  44.4 3.0 %all-to-all-done = f16[4,8,96,512]{3,2,1,0:T(8,128)(2,1)} async-done(((f16[4,8,96,512]{3,2,1,0:T(8,128)(2,1)}), f16[4,8,96,512]{3,2,1,0:T(8,128)(2,1)}, u32[]{:S(2)}, u32[]{:S(2)}) %all-to-all-start) | async-done | bytes 3145760 | tf_op jit(solution)/shard_map/all_to_all | solution.py:26
  47.4 3.3 %add_convert_fusion = f16[1,8,96,512]{3,2,1,0:T(8,128)(2,1)} fusion(f16[4,8,96,512]{3,2,1,0:T(8,128)(2,1)} %all-to-all-done), kind=kLoop, calls=%fused_computation.3 | loop fusion | flops 3145728 | bytes 3932160 | tf_op jit(solution)/shard_map/convert_element_type | solution.py:154
  50.6 22.2 %all-to-all-start.1 = ((f16[32,24,512]{2,1,0:T(8,128)(2,1)}), f16[32,24,512]{2,1,0:T(8,128)(2,1)S(1)}, u32[]{:S(2)}, u32[]{:S(2)}) async-start(f16[32,24,512]{2,1,0:T(8,128)(2,1)} %bitcast.64), calls=%async_computation.1 | async-start | bytes 1572864 | tf_op jit(solution)/shard_map/all_to_all | solution.py:26
  73.9 19.0 %all-to-all-done.1 = f16[32,24,512]{2,1,0:T(8,128)(2,1)S(1)} async-done(((f16[32,24,512]{2,1,0:T(8,128)(2,1)}), f16[32,24,512]{2,1,0:T(8,128)(2,1)S(1)}, u32[]{:S(2)}, u32[]{:S(2)}) %all-to-all-start.1) | async-done | bytes 786464 | tf_op jit(solution)/shard_map/all_to_all | solution.py:26
  95.1 7.5 %all-to-all-start.2 = ((bf16[32,16,512]{2,1,0:T(8,128)(2,1)}), bf16[32,16,512]{2,1,0:T(8,128)(2,1)S(1)}, u32[]{:S(2)}, u32[]{:S(2)}) async-start(bf16[32,16,512]{2,1,0:T(8,128)(2,1)} %broadcast_in_dim.6), calls=%async_computation.2 | async-start | bytes 1048576 | tf_op jit(solution)/shard_map/all_to_all | solution.py:26
  102.7 2.8 %collective-permute-start.5 = (bf16[8,512]{1,0:T(8,128)(2,1)S(1)}, bf16[8,512]{1,0:T(8,128)(2,1)S(1)}, u32[]{:S(2)}, u32[]{:S(2)}) collective-permute-start(bf16[8,512]{1,0:T(8,128)(2,1)S(1)} %get-tuple-element.33), channel_id=1, source_target_pairs={{0,12},{4,0},{8,4},{12,8},{1,13},{5,1},{9,5},{13,9},{2,14},{6,2},{... | collective-permute-start | bytes 24584 | tf_op jit(solution)/shard_map/ppermute | solution.py:42
  105.5 3.1 %collective-permute-start.4 = (bf16[8,512]{1,0:T(8,128)(2,1)S(1)}, bf16[8,512]{1,0:T(8,128)(2,1)S(1)}, u32[]{:S(2)}, u32[]{:S(2)}) collective-permute-start(bf16[8,512]{1,0:T(8,128)(2,1)S(1)} %get-tuple-element.33), channel_id=1, source_target_pairs={{0,8},{4,12},{8,0},{12,4},{1,9},{5,13},{9,1},{13,5},{2,10},{6,14},... | collective-permute-start | bytes 24584 | tf_op jit(solution)/shard_map/ppermute | solution.py:42
  108.6 1.9 %collective-permute-start.3 = (bf16[8,512]{1,0:T(8,128)(2,1)S(1)}, bf16[8,512]{1,0:T(8,128)(2,1)S(1)}, u32[]{:S(2)}, u32[]{:S(2)}) collective-permute-start(bf16[8,512]{1,0:T(8,128)(2,1)S(1)} %get-tuple-element.33), channel_id=1, source_target_pairs={{0,4},{4,8},{8,12},{12,0},{1,5},{5,9},{9,13},{13,1},{2,6},{6,10},{... | collective-permute-start | bytes 24584 | tf_op jit(solution)/shard_map/ppermute | solution.py:42
  110.5 1.1 collective-permute-done.4
  111.7 2.8 %collective-permute-done.3 = bf16[8,512]{1,0:T(8,128)(2,1)S(1)} collective-permute-done((bf16[8,512]{1,0:T(8,128)(2,1)S(1)}, bf16[8,512]{1,0:T(8,128)(2,1)S(1)}, u32[]{:S(2)}, u32[]{:S(2)}) %collective-permute-start.3) | collective-permute-done | bytes 8224 | tf_op jit(solution)/shard_map/ppermute | solution.py:42
  114.5 2.4 %all-to-all-done.2 = bf16[32,16,512]{2,1,0:T(8,128)(2,1)S(1)} async-done(((bf16[32,16,512]{2,1,0:T(8,128)(2,1)}), bf16[32,16,512]{2,1,0:T(8,128)(2,1)S(1)}, u32[]{:S(2)}, u32[]{:S(2)}) %all-to-all-start.2) | async-done | bytes 524320 | tf_op jit(solution)/shard_map/all_to_all | solution.py:26
  117.8 1.1 broadcast_in_dim.7
  118.9 7.5 %all-to-all-start.3 = ((bf16[32,4,8,512]{3,2,1,0:T(8,128)(2,1)}), bf16[32,4,8,512]{3,2,1,0:T(8,128)(2,1)S(1)}, u32[]{:S(2)}, u32[]{:S(2)}) async-start(bf16[32,4,8,512]{3,2,1,0:T(8,128)(2,1)} %broadcast_in_dim.7), calls=%async_computation.3 | async-start | bytes 2097152 | tf_op jit(solution)/shard_map/all_to_all | solution.py:26
  127.6 26.3 %all-to-all-done.3 = bf16[32,4,8,512]{3,2,1,0:T(8,128)(2,1)S(1)} async-done(((bf16[32,4,8,512]{3,2,1,0:T(8,128)(2,1)}), bf16[32,4,8,512]{3,2,1,0:T(8,128)(2,1)S(1)}, u32[]{:S(2)}, u32[]{:S(2)}) %all-to-all-start.3) | async-done | bytes 1048608 | tf_op jit(solution)/shard_map/all_to_all | solution.py:26
  153.9 4.6 %all-gather.3.cloned.1.call-done = bf16[128,16,512]{2,1,0:T(8,128)(2,1)} async-done(((bf16[32,16,512]{2,1,0:T(8,128)(2,1)}), bf16[128,16,512]{2,1,0:T(8,128)(2,1)}) %all-gather.3.cloned.1.call-update) | async-done | bytes 2097168 | tf_op jit(solution)/shard_map/all_gather | solution.py:167
  158.5 3.2 %joined.1 = bf16[8,4,96,512]{3,2,1,0:T(8,128)(2,1)} custom-call(bf16[4,8,4,16,512]{4,3,2,1,0:T(8,128)(2,1)} %bitcast.65, bf16[8,4,4,8,512]{4,3,2,1,0:T(8,128)(2,1)} %bitcast.61), custom_call_target="tpu_custom_call" | custom-call | tf_op jit(solution)/shard_map/joined/pallas_call | solution.py:100
  (38 shorter events, 6.2 us)
Async XLA Ops:
  7.2 1.7 copy-start
  14.2 5.0 %copy-start.4 = (f32[1,24,512]{2,1,0:T(8,128)S(1)}, f32[1,24,512]{2,1,0:T(8,128)}, u32[]{:S(2)}) copy-start(f32[1,24,512]{2,1,0:T(8,128)} %param.9) | copy-start | bytes 147460
  14.2 5.0 %copy-start.5 = (f32[24,512]{1,0:T(8,128)S(1)}, f32[24,512]{1,0:T(8,128)}, u32[]{:S(2)}) copy-start(f32[24,512]{1,0:T(8,128)} %param.10) | copy-start | bytes 147460
  14.2 5.0 %copy-start.7 = (f32[1,4,512]{2,1,0:T(4,128)S(1)}, f32[1,4,512]{2,1,0:T(4,128)}, u32[]{:S(2)}) copy-start(f32[1,4,512]{2,1,0:T(4,128)} %param.11) | copy-start | bytes 24580
  14.2 33.2 %all-to-all-start = ((f16[4,8,96,512]{3,2,1,0:T(8,128)(2,1)}), f16[4,8,96,512]{3,2,1,0:T(8,128)(2,1)}, u32[]{:S(2)}, u32[]{:S(2)}) async-start(f16[4,8,96,512]{3,2,1,0:T(8,128)(2,1)} %bitcast.60), calls=%async_computation | async-start | bytes 6291456 | tf_op jit(solution)/shard_map/all_to_all | solution.py:26
  19.2 13.2 %collective-permute-start = (f32[28,512]{1,0:T(8,128)S(1)}, f32[28,512]{1,0:T(8,128)S(1)}, u32[]{:S(2)}, u32[]{:S(2)}) collective-permute-start(f32[28,512]{1,0:T(8,128)S(1)} %pad_maximum_fusion.1), channel_id=1, source_target_pairs={{0,128},{128,0},{1,129},{129,1},{2,130},{130,2},{3,131},{131,3},{4... | collective-permute-start | bytes 172040 | tf_op jit(solution)/shard_map/ppermute | solution.py:42
  32.4 60.4 %copy-start.3 = (f32[1,24,512]{2,1,0:T(8,128)S(1)}, f32[1,24,512]{2,1,0:T(8,128)}, u32[]{:S(2)}) copy-start(f32[1,24,512]{2,1,0:T(8,128)} %param.13) | copy-start | bytes 147460
  32.4 9.3 %collective-permute-start.1 = (f32[32,512]{1,0:T(8,128)S(1)}, f32[32,512]{1,0:T(8,128)S(1)}, u32[]{:S(2)}, u32[]{:S(2)}) collective-permute-start(f32[32,512]{1,0:T(8,128)S(1)} %pad_maximum_fusion.2), channel_id=1, source_target_pairs={{0,256},{256,512},{512,0},{1,257},{257,513},{513,1},{2,258},{258,5... | collective-permute-start | bytes 196616 | tf_op jit(solution)/shard_map/ppermute | solution.py:42
  34.5 9.9 %collective-permute-start.2 = (f32[32,512]{1,0:T(8,128)S(1)}, f32[32,512]{1,0:T(8,128)}, u32[]{:S(2)}, u32[]{:S(2)}) collective-permute-start(f32[32,512]{1,0:T(8,128)S(1)} %pad_maximum_fusion.2), channel_id=1, source_target_pairs={{0,512},{256,0},{512,256},{1,513},{257,1},{513,257},{2,514},{258,2... | collective-permute-start | bytes 196616 | tf_op jit(solution)/shard_map/ppermute | solution.py:42
  50.6 42.9 %copy-start.6 = (f32[1,24,512]{2,1,0:T(8,128)S(1)}, f32[1,24,512]{2,1,0:T(8,128)}, u32[]{:S(2)}) copy-start(f32[1,24,512]{2,1,0:T(8,128)} %param.12) | copy-start | bytes 147460
  50.6 42.2 %all-to-all-start.1 = ((f16[32,24,512]{2,1,0:T(8,128)(2,1)}), f16[32,24,512]{2,1,0:T(8,128)(2,1)S(1)}, u32[]{:S(2)}, u32[]{:S(2)}) async-start(f16[32,24,512]{2,1,0:T(8,128)(2,1)} %bitcast.64), calls=%async_computation.1 | async-start | bytes 1572864 | tf_op jit(solution)/shard_map/all_to_all | solution.py:26
  95.1 21.9 %all-to-all-start.2 = ((bf16[32,16,512]{2,1,0:T(8,128)(2,1)}), bf16[32,16,512]{2,1,0:T(8,128)(2,1)S(1)}, u32[]{:S(2)}, u32[]{:S(2)}) async-start(bf16[32,16,512]{2,1,0:T(8,128)(2,1)} %broadcast_in_dim.6), calls=%async_computation.2 | async-start | bytes 1048576 | tf_op jit(solution)/shard_map/all_to_all | solution.py:26
  102.6 55.9 %all-gather.3.cloned.1.call-start = ((), (), s32[]{:S(2)}) async-start(), calls=%async_computation.4 | async-start | bytes 2621440 | tf_op jit(solution)/shard_map/all_gather | solution.py:167
  102.7 7.8 %collective-permute-start.5 = (bf16[8,512]{1,0:T(8,128)(2,1)S(1)}, bf16[8,512]{1,0:T(8,128)(2,1)S(1)}, u32[]{:S(2)}, u32[]{:S(2)}) collective-permute-start(bf16[8,512]{1,0:T(8,128)(2,1)S(1)} %get-tuple-element.33), channel_id=1, source_target_pairs={{0,12},{4,0},{8,4},{12,8},{1,13},{5,1},{9,5},{13,9},{2,14},{6,2},{... | collective-permute-start | bytes 24584 | tf_op jit(solution)/shard_map/ppermute | solution.py:42
  105.5 6.2 %collective-permute-start.4 = (bf16[8,512]{1,0:T(8,128)(2,1)S(1)}, bf16[8,512]{1,0:T(8,128)(2,1)S(1)}, u32[]{:S(2)}, u32[]{:S(2)}) collective-permute-start(bf16[8,512]{1,0:T(8,128)(2,1)S(1)} %get-tuple-element.33), channel_id=1, source_target_pairs={{0,8},{4,12},{8,0},{12,4},{1,9},{5,13},{9,1},{13,5},{2,10},{6,14},... | collective-permute-start | bytes 24584 | tf_op jit(solution)/shard_map/ppermute | solution.py:42
  108.6 5.9 %collective-permute-start.3 = (bf16[8,512]{1,0:T(8,128)(2,1)S(1)}, bf16[8,512]{1,0:T(8,128)(2,1)S(1)}, u32[]{:S(2)}, u32[]{:S(2)}) collective-permute-start(bf16[8,512]{1,0:T(8,128)(2,1)S(1)} %get-tuple-element.33), channel_id=1, source_target_pairs={{0,4},{4,8},{8,12},{12,0},{1,5},{5,9},{9,13},{13,1},{2,6},{6,10},{... | collective-permute-start | bytes 24584 | tf_op jit(solution)/shard_map/ppermute | solution.py:42
  117.0 0.8 copy-start.2
  118.9 35.0 %all-to-all-start.3 = ((bf16[32,4,8,512]{3,2,1,0:T(8,128)(2,1)}), bf16[32,4,8,512]{3,2,1,0:T(8,128)(2,1)S(1)}, u32[]{:S(2)}, u32[]{:S(2)}) async-start(bf16[32,4,8,512]{3,2,1,0:T(8,128)(2,1)} %broadcast_in_dim.7), calls=%async_computation.3 | async-start | bytes 2097152 | tf_op jit(solution)/shard_map/all_to_all | solution.py:26
  153.9 4.6 %copy-start.1 = (bf16[32,4,8,512]{3,2,1,0:T(8,128)(2,1)}, bf16[32,4,8,512]{3,2,1,0:T(8,128)(2,1)S(1)}, u32[]{:S(2)}) copy-start(bf16[32,4,8,512]{3,2,1,0:T(8,128)(2,1)S(1)} %all-to-all-done.3) | copy-start | bytes 3145732
Sparse Core Ops, SparseCore 0:
  117.9 40.5 all-gather.2

commit v8 on v7

v8 whole, which is shorter than its diff:
```python
import jax
import jax.numpy as jnp
import numpy as np
from jax import lax
from jax.sharding import Mesh
from jax.sharding import PartitionSpec as P

DP = ("dp_0", "dp_1", "dp_2")
HI, CORE = REPLICA = ("chip", "core")

outer_mu = 0.9
outer_rate = 0.7
beta_one = 0.9
beta_two = 0.95
adam_eps = 1e-08
weight_decay = 0.1
inner_rate = 0.1
correct_one = 1.0 - 0.9**50
correct_two = 1.0 - 0.95**50


def exchanged(x, groups):
    return lax.all_to_all(x, REPLICA + DP, 0, 0, axis_index_groups=groups, tiled=True)


def copies(x, n):
    return jnp.broadcast_to(x[None], (n, *x.shape))


def total(blocks):
    parts = [b.astype(jnp.float32) for b in blocks]
    while len(parts) > 1:
        parts = [sum(parts[i : i + 2]) for i in range(0, len(parts), 2)]
    return parts[0]


def passed(x, axis, step):
    n = lax.axis_size(axis)
    return lax.ppermute(x, axis, [(i, (i + step) % n) for i in range(n)])


def turned(index, n):
    return index & (n - 1) if n & (n - 1) == 0 else lax.rem(index, n)


def block_of(x, index, dim):
    return lax.dynamic_index_in_dim(x, index, dim, keepdims=False)


def arrived_along(x, axis):
    return [x] + [passed(x, axis, k) for k in range(1, lax.axis_size(axis))]


def in_order(arrived, axis):
    n = lax.axis_size(axis)
    me = lax.axis_index(axis)
    blocks = jnp.stack(arrived)
    return jnp.stack([block_of(blocks, turned(me + n - i, n), 0) for i in range(n)])


def crossing_groups(replicas, sizes, n_core):
    ny, nx, nz = sizes
    dp = ny * nx * nz
    at = np.arange(dp).reshape(ny, nx, nz)
    tables = (
        at.transpose(1, 0, 2).reshape(nx, -1),
        at.reshape(ny // 2, 2, nx, nz // 2, 2).transpose(1, 4, 0, 2, 3).reshape(4, -1),
    )
    near, far = [], []
    for replica in range(replicas):
        table = tables[replica % n_core] + replica * dp
        near += table.T.tolist()
        far += table.tolist()
    return near, far


def per_core(core, ways, x):
    return lax.cond(core == 0, ways[0], ways[1], x)


def per_device(
    layer_input, key_cotangent, local_params, global_params, outer_momentum, adam_first, adam_second
):
    features = layer_input[0]
    cotangent = key_cotangent[0]
    own_local = local_params[0]
    rows, width = global_params.shape
    ny, nx, nz = (lax.axis_size(a) for a in DP)
    plane = ny * nz
    n_hi, n_core = lax.axis_size(HI), lax.axis_size(CORE)
    replicas = n_hi * n_core
    sub_rows = outer_momentum.shape[1]
    near, far = crossing_groups(replicas, (ny, nx, nz), n_core)

    core = lax.axis_index(CORE)
    hi = lax.axis_index(HI)
    deltas = global_params - own_local
    mine = jnp.concatenate([deltas, outer_momentum[0]], 0)
    other = passed(mine, CORE, 1)

    term = lax.dot_general(
        features, cotangent, (((0,), (0,)), ((), ())), preferred_element_type=jnp.float32
    ).astype(jnp.float16)
    blocks = per_core(
        core,
        (
            lambda t: t.reshape(ny, nx, nz * rows, width).transpose(1, 0, 2, 3).reshape(4, -1, rows, width),
            lambda t: t.reshape(ny // 2, 2, nx, nz // 2, 2, rows, width)
            .transpose(1, 4, 0, 2, 3, 5, 6)
            .reshape(4, -1, rows, width),
        ),
        term,
    )
    summed_near = exchanged(blocks, near)

    upper, lower = jnp.where(core == 0, mine, other), jnp.where(core == 0, other, mine)
    pair = jnp.concatenate([mine[:rows] + other[:rows], upper[rows:], lower[rows:]], 0)
    summed_near, chips = lax.optimization_barrier((summed_near, arrived_along(pair, HI)))
    by_chip = in_order(chips, HI)
    outer_grad = sum(p[:rows] for p in by_chip) / replicas
    old_rows = jnp.concatenate([p[rows:] for p in by_chip], 0)
    momentum_all = outer_mu * old_rows + outer_grad
    global_new = global_params - outer_rate * (outer_grad + outer_mu * momentum_all)
    momentum_new = lax.dynamic_slice_in_dim(
        momentum_all, (hi * n_core + core) * sub_rows, sub_rows, 0
    )

    part = total(summed_near).astype(jnp.float16)
    gradient = total(exchanged(part, far))

    first_new = beta_one * adam_first[0] + (1.0 - beta_one) * gradient
    second_new = beta_two * adam_second[0] + (1.0 - beta_two) * gradient * gradient
    adam_step = (
        first_new / correct_one / (jnp.sqrt(second_new / correct_two) + adam_eps)
        + weight_decay * own_local
    )
    merged = (global_new - inner_rate * adam_step).astype(jnp.bfloat16)
    held = exchanged(copies(merged, plane), far)
    held = exchanged(copies(held, nx), near)
    gathered = per_core(
        core,
        (
            lambda t: t.reshape(nx, ny, nz * rows, width).transpose(1, 0, 2, 3).reshape(-1, width),
            lambda t: t.reshape(2, 2, ny // 2, nx, nz // 2, rows, width)
            .transpose(2, 0, 3, 4, 1, 5, 6)
            .reshape(-1, width),
        ),
        held,
    )
    return (gathered[None], global_new, momentum_new[None], first_new[None], second_new[None])


def solution(mesh):
    torus = Mesh(
        mesh.devices.reshape(mesh.shape["replica"] // 2, 2, 8, 4, 4), REPLICA + DP
    )
    in_specs = (
        P(REPLICA, DP, None),
        P(REPLICA, DP, None),
        P(REPLICA, DP, None),
        P(DP, None),
        P(DP, REPLICA, None),
        P(REPLICA, DP, None),
        P(REPLICA, DP, None),
    )
    out_specs = (
        P(REPLICA, None, None),
        P(DP, None),
        P(DP, REPLICA, None),
        P(REPLICA, DP, None),
        P(REPLICA, DP, None),
    )
    return jax.shard_map(
        per_device, mesh=torus, in_specs=in_specs, out_specs=out_specs, check_vma=False
    )
```

time: 169 us -> 145 us (0.86)
  starting transfers between devices: 71.6 us -> 43.3 us
  blocking collectives: 0 us -> 28.1 us
  between operations: 14.3 us -> 0.82 us
  waiting for transfers between devices: 62.8 us -> 52.4 us
  Pallas kernels: 3.18 us -> 0 us
  local copies, waits for them, and re-layouts: 7.6 us -> 10.7 us
    all_to_all x0 -> x1, blocking collectives: none -> 28.1 us  [exchanged(): lax.all_to_all(x, REPLICA + DP, 0, 0, axis_index_groups=groups, tiled=True)]
    all_to_all x4 -> x3, starting transfers between devices: 42.2 us -> 22.1 us  [exchanged(): lax.all_to_all(x, REPLICA + DP, 0, 0, axis_index_groups=groups, tiled=True)]
    all_to_all x4 -> x3, waiting for transfers between devices: 50.7 us -> 38.2 us  [exchanged(): lax.all_to_all(x, REPLICA + DP, 0, 0, axis_index_groups=groups, tiled=True)]
    ppermute x6 -> x3, starting transfers between devices: 29.4 us -> 21.3 us  [passed(): return lax.ppermute(x, axis, [(i, (i + step) % n) for i in range(n)])]
    ppermute x6 -> x3, waiting for transfers between devices: 7.47 us -> 14.2 us  [passed(): return lax.ppermute(x, axis, [(i, (i + step) % n) for i in range(n)])]
    all_gather x1 -> x0, waiting for transfers between devices: 4.59 us -> none  [per_device(): all_a = lax.all_gather(near_a, X).reshape(nx, ny, nz, cut, width)]
    reshape x1 -> x2, local copies, waits for them, and re-layouts: 2.51 us -> 6.42 us  [the longest x1 3.97 us: per_device(): t.reshape(2, 2, ny // 2, nx, nz // 2, rows, width)]
    pallas_call x1 -> x0, Pallas kernels: 3.18 us -> none  [joined(): pl.pallas_call(joining, in_specs=[place, place], out_specs=place, out_sha...]
  transfers between devices with their start and end apart: 11 -> 6, of which waited for: 9 -> 4; matrix products, arithmetic and copies ran while one was open for 2% -> 2% of each run, Pallas kernels for 0% -> 0%
where the time goes in v8:
time: 145 us; the launch traced here: 144 us
  waiting for transfers between devices  52.4 us (36%)
  starting transfers between devices  43.3 us (30%)
  blocking collectives  28.1 us (19%)
  local copies, waits for them, and re-layouts  10.7 us (7%)
  other arithmetic  6.11 us (4%)
  matrix products  2.83 us (2%)
    all_to_all x3, waiting for transfers between devices, exchanged(): lax.all_to_all(x, REPLICA + DP, 0, 0, axis_index_groups=groups, tiled=True)  38.2 us
    all_to_all x1, blocking collectives, exchanged(): lax.all_to_all(x, REPLICA + DP, 0, 0, axis_index_groups=groups, tiled=True)  28.1 us
    all_to_all x3, starting transfers between devices, exchanged(): lax.all_to_all(x, REPLICA + DP, 0, 0, axis_index_groups=groups, tiled=True)  22.1 us
    ppermute x3, starting transfers between devices, passed(): return lax.ppermute(x, axis, [(i, (i + step) % n) for i in range(n)])  21.3 us
    ppermute x3, waiting for transfers between devices, passed(): return lax.ppermute(x, axis, [(i, (i + step) % n) for i in range(n)])  14.2 us
    reshape x1, local copies, waits for them, and re-layouts, per_device(): t.reshape(2, 2, ny // 2, nx, nz // 2, rows, width)  3.97 us
    convert_element_type x1, other arithmetic, per_device(): part = total(summed_near).astype(jnp.float16)  3.17 us
  transfers between devices with their start and end apart: 6, of which 4 were waited for; matrix products, arithmetic and copies ran while one was open for 2% of the time, Pallas kernels for 0%

profile of v8, /device:TPU:1, one launch (start us, length us, event | category | flops | bytes accessed | tf_op | source)
XLA Modules:
  0.0 144.3 jit_solution(1494473579662927790)
XLA Ops:
  0.7 1.6 %copy-done = bf16[1,384,3072]{2,1,0:T(8,128)(2,1)S(1)} copy-done((bf16[1,384,3072]{2,1,0:T(8,128)(2,1)S(1)}, bf16[1,384,3072]{2,1,0:T(8,128)(2,1)}, u32[]{:S(2)}) %copy-start) | copy-done | bytes 2359320
  2.3 2.8 %convolution_convert_fusion = f16[3072,512]{1,0:T(8,128)(2,1)S(1)} fusion(bf16[1,384,3072]{2,1,0:T(8,128)(2,1)S(1)} %copy-done, bf16[1,384,512]{2,1,0:T(8,128)(2,1)} %param.12), kind=kOutput, calls=%fused_computation | convolution fusion | flops 1209532416 | bytes 5898240 | tf_op jit(solution)/shard_map/dot_general | solution.py:101
  5.1 2.5 %conditional.2 = (f16[4,32,24,512]{3,2,1,0:T(8,128)(2,1)}) conditional(s32[]{:T(128)} %convert_element_type.230, f16[3072,512]{1,0:T(8,128)(2,1)S(1)} %convolution_convert_fusion, f16[3072,512]{1,0:T(8,128)(2,1)S(1)} %convolution_convert_fusion), branch_computations={%region_0.0_spmd, %region_1.0_spmd} | conditional | bytes 6291464 | solution.py:78
  5.2 2.5 %copy.12 = f16[4,2,4,2,2,24,512]{6,5,3,2,0,4,1:T(8,128)(2,1)} copy(f16[4,2,4,2,2,24,512]{6,5,4,3,2,1,0:T(8,128)(2,1)S(1)} %bitcast.65) | data formatting | bytes 6291456 | tf_op jit(solution)/shard_map/cond/branch_0_fun/reshape | solution.py:108
  7.6 5.3 %all-to-all-start = ((f16[4,32,24,512]{3,2,1,0:T(8,128)(2,1)}), f16[4,32,24,512]{3,2,1,0:T(8,128)(2,1)}, u32[]{:S(2)}, u32[]{:S(2)}) async-start(f16[4,32,24,512]{3,2,1,0:T(8,128)(2,1)} %get-tuple-element.35), calls=%async_computation | async-start | bytes 6291456 | tf_op jit(solution)/shard_map/all_to_all | solution.py:23
  13.0 11.9 %collective-permute-start = (f32[28,512]{1,0:T(8,128)S(1)}, f32[28,512]{1,0:T(8,128)S(1)}, u32[]{:S(2)}, u32[]{:S(2)}) collective-permute-start(f32[28,512]{1,0:T(8,128)S(1)} %pad_maximum_fusion.1), channel_id=1, source_target_pairs={{0,128},{128,0},{1,129},{129,1},{2,130},{130,2},{3,131},{131,3},{4... | collective-permute-start | bytes 172040 | tf_op jit(solution)/shard_map/ppermute | solution.py:39
  24.9 0.9 collective-permute-done
  25.9 2.1 %collective-permute-start.1 = (f32[32,512]{1,0:T(8,128)S(1)}, f32[32,512]{1,0:T(8,128)S(1)}, u32[]{:S(2)}, u32[]{:S(2)}) collective-permute-start(f32[32,512]{1,0:T(8,128)S(1)} %pad_maximum_fusion.2), channel_id=1, source_target_pairs={{0,256},{256,512},{512,0},{1,257},{257,513},{513,1},{2,258},{258,5... | collective-permute-start | bytes 196616 | tf_op jit(solution)/shard_map/ppermute | solution.py:39
  27.9 7.3 %collective-permute-start.2 = (f32[32,512]{1,0:T(8,128)S(1)}, f32[32,512]{1,0:T(8,128)}, u32[]{:S(2)}, u32[]{:S(2)}) collective-permute-start(f32[32,512]{1,0:T(8,128)S(1)} %pad_maximum_fusion.2), channel_id=1, source_target_pairs={{0,512},{256,0},{512,256},{1,513},{257,1},{513,257},{2,514},{258,2... | collective-permute-start | bytes 196616 | tf_op jit(solution)/shard_map/ppermute | solution.py:39
  35.2 13.4 %collective-permute-done.1 = f32[32,512]{1,0:T(8,128)S(1)} collective-permute-done((f32[32,512]{1,0:T(8,128)S(1)}, f32[32,512]{1,0:T(8,128)S(1)}, u32[]{:S(2)}, u32[]{:S(2)}) %collective-permute-start.1) | collective-permute-done | bytes 65568 | tf_op jit(solution)/shard_map/ppermute | solution.py:39
  48.6 3.2 %fusion.1 = f16[32,24,512]{2,1,0:T(8,128)(2,1)} fusion(f16[4,32,24,512]{3,2,1,0:T(8,128)(2,1)} %all-to-all-done), kind=kLoop, calls=%fused_computation.3 | loop fusion | flops 3145728 | bytes 3932160 | tf_op jit(solution)/shard_map/convert_element_type | solution.py:128
  51.8 12.1 %all-to-all-start.1 = ((f16[32,24,512]{2,1,0:T(8,128)(2,1)}), f16[32,24,512]{2,1,0:T(8,128)(2,1)S(1)}, u32[]{:S(2)}, u32[]{:S(2)}) async-start(f16[32,24,512]{2,1,0:T(8,128)(2,1)} %fusion.1), calls=%async_computation.1 | async-start | bytes 1572864 | tf_op jit(solution)/shard_map/all_to_all | solution.py:23
  63.9 0.9 pad_maximum_fusion
  64.8 19.8 %all-to-all-done.1 = f16[32,24,512]{2,1,0:T(8,128)(2,1)S(1)} async-done(((f16[32,24,512]{2,1,0:T(8,128)(2,1)}), f16[32,24,512]{2,1,0:T(8,128)(2,1)S(1)}, u32[]{:S(2)}, u32[]{:S(2)}) %all-to-all-start.1) | async-done | bytes 786464 | tf_op jit(solution)/shard_map/all_to_all | solution.py:23
  84.7 0.7 fusion.9
  85.4 0.7 subtract_convert_fusion
  86.1 28.1 %all_to_all.26 = bf16[32,24,512]{2,1,0:T(8,128)(2,1)S(1)} all-to-all(bf16[32,24,512]{2,1,0:T(8,128)(2,1)S(1)} %broadcast_in_dim.24), channel_id=1, replica_groups={{0,1,2,3,16,17,18,19,32,33,34,35,48,49,50,51,64,65,66,67,80,81,82,83,96..., dimensions={0} | all-to-all | bytes 1572864 | tf_op jit(solution)/shard_map/all_to_all | solution.py:23
  114.2 1.9 %broadcast_in_dim.25 = bf16[4,32,24,512]{3,2,1,0:T(8,128)(2,1)} broadcast(bf16[32,24,512]{2,1,0:T(8,128)(2,1)S(1)} %all_to_all.26), dimensions={1,2,3} | broadcast | bytes 3932160 | tf_op jit(solution)/shard_map/broadcast_in_dim | solution.py:27
  116.1 4.6 %all-to-all-start.3 = ((bf16[4,32,24,512]{3,2,1,0:T(8,128)(2,1)}), bf16[4,32,24,512]{3,2,1,0:T(8,128)(2,1)}, u32[]{:S(2)}, u32[]{:S(2)}) async-start(bf16[4,32,24,512]{3,2,1,0:T(8,128)(2,1)} %broadcast_in_dim.25), calls=%async_computation.3 | async-start | bytes 6291456 | tf_op jit(solution)/shard_map/all_to_all | solution.py:23
  120.8 0.6 dynamic-slice_bitcast_fusion.3
  121.4 0.6 multiply_add_fusion
  122.0 18.3 %all-to-all-done.3 = bf16[4,32,24,512]{3,2,1,0:T(8,128)(2,1)} async-done(((bf16[4,32,24,512]{3,2,1,0:T(8,128)(2,1)}), bf16[4,32,24,512]{3,2,1,0:T(8,128)(2,1)}, u32[]{:S(2)}, u32[]{:S(2)}) %all-to-all-start.3) | async-done | bytes 3145760 | tf_op jit(solution)/shard_map/all_to_all | solution.py:23
  140.4 4.0 %conditional.3 = (bf16[1,3072,512]{2,1,0:T(8,128)(2,1)}) conditional(s32[]{:T(128)} %convert_element_type.230, bf16[4,32,24,512]{3,2,1,0:T(8,128)(2,1)} %all-to-all-done.3, bf16[4,32,24,512]{3,2,1,0:T(8,128)(2,1)} %all-to-all-done.3), branch_computations={%region_2.3_spmd, %region_3.4_spmd} | conditional | bytes 6291464 | solution.py:78
  140.4 4.0 %copy.14 = bf16[2,2,4,4,2,24,512]{6,5,1,4,3,0,2:T(8,128)(2,1)} copy(bf16[2,2,4,4,2,24,512]{6,5,4,3,2,1,0:T(8,128)(2,1)} %bitcast.6) | data formatting | bytes 6291456 | tf_op jit(solution)/shard_map/cond/branch_0_fun/reshape | solution.py:144
  (21 shorter events, 0.2 us)
Async XLA Ops:
  0.6 1.7 %copy-start = (bf16[1,384,3072]{2,1,0:T(8,128)(2,1)S(1)}, bf16[1,384,3072]{2,1,0:T(8,128)(2,1)}, u32[]{:S(2)}) copy-start(bf16[1,384,3072]{2,1,0:T(8,128)(2,1)} %param.11) | copy-start | bytes 7077892
  7.6 5.3 %copy-start.2 = (f32[1,24,512]{2,1,0:T(8,128)S(1)}, f32[1,24,512]{2,1,0:T(8,128)}, u32[]{:S(2)}) copy-start(f32[1,24,512]{2,1,0:T(8,128)} %param.13) | copy-start | bytes 147460
  7.6 5.3 %copy-start.3 = (f32[24,512]{1,0:T(8,128)S(1)}, f32[24,512]{1,0:T(8,128)}, u32[]{:S(2)}) copy-start(f32[24,512]{1,0:T(8,128)} %param.14) | copy-start | bytes 147460
  7.6 5.4 %copy-start.5 = (f32[1,4,512]{2,1,0:T(4,128)S(1)}, f32[1,4,512]{2,1,0:T(4,128)}, u32[]{:S(2)}) copy-start(f32[1,4,512]{2,1,0:T(4,128)} %param.15) | copy-start | bytes 24580
  7.6 41.0 %all-to-all-start = ((f16[4,32,24,512]{3,2,1,0:T(8,128)(2,1)}), f16[4,32,24,512]{3,2,1,0:T(8,128)(2,1)}, u32[]{:S(2)}, u32[]{:S(2)}) async-start(f16[4,32,24,512]{3,2,1,0:T(8,128)(2,1)} %get-tuple-element.35), calls=%async_computation | async-start | bytes 6291456 | tf_op jit(solution)/shard_map/all_to_all | solution.py:23
  13.0 12.8 %collective-permute-start = (f32[28,512]{1,0:T(8,128)S(1)}, f32[28,512]{1,0:T(8,128)S(1)}, u32[]{:S(2)}, u32[]{:S(2)}) collective-permute-start(f32[28,512]{1,0:T(8,128)S(1)} %pad_maximum_fusion.1), channel_id=1, source_target_pairs={{0,128},{128,0},{1,129},{129,1},{2,130},{130,2},{3,131},{131,3},{4... | collective-permute-start | bytes 172040 | tf_op jit(solution)/shard_map/ppermute | solution.py:39
  25.9 58.8 %copy-start.1 = (f32[1,24,512]{2,1,0:T(8,128)S(1)}, f32[1,24,512]{2,1,0:T(8,128)}, u32[]{:S(2)}) copy-start(f32[1,24,512]{2,1,0:T(8,128)} %param.17) | copy-start | bytes 147460
  25.9 59.5 %copy-start.4 = (f32[1,24,512]{2,1,0:T(8,128)S(1)}, f32[1,24,512]{2,1,0:T(8,128)}, u32[]{:S(2)}) copy-start(f32[1,24,512]{2,1,0:T(8,128)} %param.16) | copy-start | bytes 147460
  25.9 22.7 %collective-permute-start.1 = (f32[32,512]{1,0:T(8,128)S(1)}, f32[32,512]{1,0:T(8,128)S(1)}, u32[]{:S(2)}, u32[]{:S(2)}) collective-permute-start(f32[32,512]{1,0:T(8,128)S(1)} %pad_maximum_fusion.2), channel_id=1, source_target_pairs={{0,256},{256,512},{512,0},{1,257},{257,513},{513,1},{2,258},{258,5... | collective-permute-start | bytes 196616 | tf_op jit(solution)/shard_map/ppermute | solution.py:39
  27.9 20.6 %collective-permute-start.2 = (f32[32,512]{1,0:T(8,128)S(1)}, f32[32,512]{1,0:T(8,128)}, u32[]{:S(2)}, u32[]{:S(2)}) collective-permute-start(f32[32,512]{1,0:T(8,128)S(1)} %pad_maximum_fusion.2), channel_id=1, source_target_pairs={{0,512},{256,0},{512,256},{1,513},{257,1},{513,257},{2,514},{258,2... | collective-permute-start | bytes 196616 | tf_op jit(solution)/shard_map/ppermute | solution.py:39
  51.8 32.9 %all-to-all-start.1 = ((f16[32,24,512]{2,1,0:T(8,128)(2,1)}), f16[32,24,512]{2,1,0:T(8,128)(2,1)S(1)}, u32[]{:S(2)}, u32[]{:S(2)}) async-start(f16[32,24,512]{2,1,0:T(8,128)(2,1)} %fusion.1), calls=%async_computation.1 | async-start | bytes 1572864 | tf_op jit(solution)/shard_map/all_to_all | solution.py:23
  116.1 24.2 %all-to-all-start.3 = ((bf16[4,32,24,512]{3,2,1,0:T(8,128)(2,1)}), bf16[4,32,24,512]{3,2,1,0:T(8,128)(2,1)}, u32[]{:S(2)}, u32[]{:S(2)}) async-start(bf16[4,32,24,512]{3,2,1,0:T(8,128)(2,1)} %broadcast_in_dim.25), calls=%async_computation.3 | async-start | bytes 6291456 | tf_op jit(solution)/shard_map/all_to_all | solution.py:23

commit v9 on v8

--- a/solution.py
+++ b/solution.py
@@ -1,3 +1,6 @@
+import math
+from functools import partial
+
 import jax
 import jax.numpy as jnp
 import numpy as np
@@ -58,24 +61,33 @@
     return jnp.stack([block_of(blocks, turned(me + n - i, n), 0) for i in range(n)])
 
 
-def crossing_groups(replicas, sizes, n_core):
-    ny, nx, nz = sizes
-    dp = ny * nx * nz
-    at = np.arange(dp).reshape(ny, nx, nz)
-    tables = (
-        at.transpose(1, 0, 2).reshape(nx, -1),
-        at.reshape(ny // 2, 2, nx, nz // 2, 2).transpose(1, 4, 0, 2, 3).reshape(4, -1),
-    )
-    near, far = [], []
-    for replica in range(replicas):
-        table = tables[replica % n_core] + replica * dp
-        near += table.T.tolist()
-        far += table.tolist()
-    return near, far
+ORDERS = ((2, 1, 4, 0, 3), (1, 4, 2, 0, 3))
 
 
-def per_core(core, ways, x):
-    return lax.cond(core == 0, ways[0], ways[1], x)
+def crossing_groups(replicas, sizes, n_core):
+    split = (sizes[0] // 2, 2, sizes[1], sizes[2] // 2, 2)
+    dp = math.prod(split)
+    stages = [], [], []
+    for replica in range(replicas):
+        at = np.arange(dp).reshape(split).transpose(ORDERS[replica % n_core])
+        at = at.reshape(4, 4, -1) + replica * dp
+        for stage in range(3):
+            stages[stage].extend(np.moveaxis(at, stage, -1).reshape(-1, at.shape[stage]).tolist())
+    return stages
+
+
+def to_places(order, split, x):
+    parts = x.reshape(*split, -1, x.shape[-1])
+    return parts.transpose(*order, 5, 6).reshape(4, 4, -1, *parts.shape[5:])
+
+
+def from_places(order, split, x):
+    parts = x.reshape(*(split[k] for k in order), *x.shape[-2:])
+    return parts.transpose(*(order.index(k) for k in range(5)), 5, 6).reshape(-1, x.shape[-1])
+
+
+def per_core(core, way, split, x):
+    return lax.cond(core == 0, partial(way, ORDERS[0], split), partial(way, ORDERS[1], split), x)
 
 
 def per_device(
@@ -86,11 +98,11 @@
     own_local = local_params[0]
     rows, width = global_params.shape
     ny, nx, nz = (lax.axis_size(a) for a in DP)
-    plane = ny * nz
     n_hi, n_core = lax.axis_size(HI), lax.axis_size(CORE)
     replicas = n_hi * n_core
     sub_rows = outer_momentum.shape[1]
-    near, far = crossing_groups(replicas, (ny, nx, nz), n_core)
+    near, middle, far = crossing_groups(replicas, (ny, nx, nz), n_core)
+    split = (ny // 2, 2, nx, nz // 2, 2)
 
     core = lax.axis_index(CORE)
     hi = lax.axis_index(HI)
@@ -101,16 +113,7 @@
     term = lax.dot_general(
         features, cotangent, (((0,), (0,)), ((), ())), preferred_element_type=jnp.float32
     ).astype(jnp.float16)
-    blocks = per_core(
-        core,
-        (
-            lambda t: t.reshape(ny, nx, nz * rows, width).transpose(1, 0, 2, 3).reshape(4, -1, rows, width),
-            lambda t: t.reshape(ny // 2, 2, nx, nz // 2, 2, rows, width)
-            .transpose(1, 4, 0, 2, 3, 5, 6)
-            .reshape(4, -1, rows, width),
-        ),
-        term,
-    )
+    blocks = per_core(core, to_places, split, term)
     summed_near = exchanged(blocks, near)
 
     upper, lower = jnp.where(core == 0, mine, other), jnp.where(core == 0, other, mine)
@@ -126,6 +129,7 @@
     )
 
     part = total(summed_near).astype(jnp.float16)
+    part = total(exchanged(part, middle)).astype(jnp.float16)
     gradient = total(exchanged(part, far))
 
     first_new = beta_one * adam_first[0] + (1.0 - beta_one) * gradient
@@ -135,18 +139,10 @@
         + weight_decay * own_local
     )
     merged = (global_new - inner_rate * adam_step).astype(jnp.bfloat16)
-    held = exchanged(copies(merged, plane), far)
-    held = exchanged(copies(held, nx), near)
-    gathered = per_core(
-        core,
-        (
-            lambda t: t.reshape(nx, ny, nz * rows, width).transpose(1, 0, 2, 3).reshape(-1, width),
-            lambda t: t.reshape(2, 2, ny // 2, nx, nz // 2, rows, width)
-            .transpose(2, 0, 3, 4, 1, 5, 6)
-            .reshape(-1, width),
-        ),
-        held,
-    )
+    held = merged
+    for groups in (far, middle, near):
+        held = exchanged(copies(held, len(groups[0])), groups)
+    gathered = per_core(core, from_places, split, held)
     return (gathered[None], global_new, momentum_new[None], first_new[None], second_new[None])
 
 

time: 145 us -> 140 us (0.966)
  waiting for transfers between devices: 52.4 us -> 41.9 us
  blocking collectives: 28.1 us -> 37.2 us
  starting transfers between devices: 43.3 us -> 40.5 us
    all_to_all x3, waiting for transfers between devices: 38.2 us -> 27.6 us  [exchanged(): lax.all_to_all(x, REPLICA + DP, 0, 0, axis_index_groups=groups, tiled=True)]
    all_to_all x1 -> x3, blocking collectives: 28.1 us -> 37.2 us  [exchanged(): lax.all_to_all(x, REPLICA + DP, 0, 0, axis_index_groups=groups, tiled=True)]
    all_to_all x3, starting transfers between devices: 22.1 us -> 19.3 us  [exchanged(): lax.all_to_all(x, REPLICA + DP, 0, 0, axis_index_groups=groups, tiled=True)]
  transfers between devices with their start and end apart: 6 -> 6, of which waited for: 4 -> 4; matrix products, arithmetic and copies ran while one was open for 2% -> 1% of each run, Pallas kernels for 0% -> 0%
where the time goes in v9:
time: 140 us; the launch traced here: 139 us
  waiting for transfers between devices  41.9 us (30%)
  starting transfers between devices  40.5 us (29%)
  blocking collectives  37.2 us (27%)
  local copies, waits for them, and re-layouts  10.8 us (8%)
  other arithmetic  5.15 us (4%)
  matrix products  2.83 us (2%)
    all_to_all x3, blocking collectives, exchanged(): lax.all_to_all(x, REPLICA + DP, 0, 0, axis_index_groups=groups, tiled=True)  37.2 us
    all_to_all x3, waiting for transfers between devices, exchanged(): lax.all_to_all(x, REPLICA + DP, 0, 0, axis_index_groups=groups, tiled=True)  27.6 us
    ppermute x3, starting transfers between devices, passed(): return lax.ppermute(x, axis, [(i, (i + step) % n) for i in range(n)])  21.2 us
    all_to_all x3, starting transfers between devices, exchanged(): lax.all_to_all(x, REPLICA + DP, 0, 0, axis_index_groups=groups, tiled=True)  19.3 us
    ppermute x3, waiting for transfers between devices, passed(): return lax.ppermute(x, axis, [(i, (i + step) % n) for i in range(n)])  14.3 us
    reshape x1, local copies, waits for them, and re-layouts, from_places(): parts = x.reshape(*(split[k] for k in order), *x.shape[-2:])  4.03 us
    dot_general x1, matrix products, per_device(): lax.dot_general(features, cotangent, (((0,), (0,)), ((), ())), preferred_...  2.83 us
  transfers between devices with their start and end apart: 6, of which 4 were waited for; matrix products, arithmetic and copies ran while one was open for 1% of the time, Pallas kernels for 0%

profile of v9, /device:TPU:1, one launch (start us, length us, event | category | flops | bytes accessed | tf_op | source)
XLA Modules:
  0.0 139.2 jit_solution(8081049667386197522)
XLA Ops:
  0.7 1.6 %copy-done = bf16[1,384,3072]{2,1,0:T(8,128)(2,1)S(1)} copy-done((bf16[1,384,3072]{2,1,0:T(8,128)(2,1)S(1)}, bf16[1,384,3072]{2,1,0:T(8,128)(2,1)}, u32[]{:S(2)}) %copy-start) | copy-done | bytes 2359320
  2.3 2.8 %convolution_convert_fusion = f16[3072,512]{1,0:T(8,128)(2,1)S(1)} fusion(bf16[1,384,3072]{2,1,0:T(8,128)(2,1)S(1)} %copy-done, bf16[1,384,512]{2,1,0:T(8,128)(2,1)} %param.12), kind=kOutput, calls=%fused_computation | convolution fusion | flops 1209532416 | bytes 5898240 | tf_op jit(solution)/shard_map/dot_general | solution.py:113
  5.1 2.5 %conditional.2 = (f16[4,4,8,24,512]{4,3,2,1,0:T(8,128)(2,1)}) conditional(s32[]{:T(128)} %convert_element_type.108, f16[3072,512]{1,0:T(8,128)(2,1)S(1)} %convolution_convert_fusion, f16[3072,512]{1,0:T(8,128)(2,1)S(1)} %convolution_convert_fusion), branch_computations={%region_0.0_spmd, %region_1.0_spmd} | conditional | bytes 6291464 | solution.py:90
  5.2 2.5 %copy.12 = f16[4,2,4,2,2,24,512]{6,5,3,0,2,4,1:T(8,128)(2,1)} copy(f16[4,2,4,2,2,24,512]{6,5,4,3,2,1,0:T(8,128)(2,1)S(1)} %bitcast.67) | data formatting | bytes 6291456 | tf_op jit(solution)/shard_map/cond/branch_0_fun/reshape | solution.py:80
  7.6 5.3 %all-to-all-start = ((f16[4,4,8,24,512]{4,3,2,1,0:T(8,128)(2,1)}), f16[4,4,8,24,512]{4,3,2,1,0:T(8,128)(2,1)}, u32[]{:S(2)}, u32[]{:S(2)}) async-start(f16[4,4,8,24,512]{4,3,2,1,0:T(8,128)(2,1)} %get-tuple-element.35), calls=%async_computation | async-start | bytes 6291456 | tf_op jit(solution)/shard_map/all_to_all | solution.py:26
  13.0 11.9 %collective-permute-start = (f32[28,512]{1,0:T(8,128)S(1)}, f32[28,512]{1,0:T(8,128)S(1)}, u32[]{:S(2)}, u32[]{:S(2)}) collective-permute-start(f32[28,512]{1,0:T(8,128)S(1)} %pad_maximum_fusion.1), channel_id=1, source_target_pairs={{0,128},{128,0},{1,129},{129,1},{2,130},{130,2},{3,131},{131,3},{4... | collective-permute-start | bytes 172040 | tf_op jit(solution)/shard_map/ppermute | solution.py:42
  24.9 0.9 collective-permute-done
  25.8 2.1 %collective-permute-start.1 = (f32[32,512]{1,0:T(8,128)S(1)}, f32[32,512]{1,0:T(8,128)S(1)}, u32[]{:S(2)}, u32[]{:S(2)}) collective-permute-start(f32[32,512]{1,0:T(8,128)S(1)} %pad_maximum_fusion.2), channel_id=1, source_target_pairs={{0,256},{256,512},{512,0},{1,257},{257,513},{513,1},{2,258},{258,5... | collective-permute-start | bytes 196616 | tf_op jit(solution)/shard_map/ppermute | solution.py:42
  27.9 7.3 %collective-permute-start.2 = (f32[32,512]{1,0:T(8,128)S(1)}, f32[32,512]{1,0:T(8,128)S(1)}, u32[]{:S(2)}, u32[]{:S(2)}) collective-permute-start(f32[32,512]{1,0:T(8,128)S(1)} %pad_maximum_fusion.2), channel_id=1, source_target_pairs={{0,512},{256,0},{512,256},{1,513},{257,1},{513,257},{2,514},{258,2... | collective-permute-start | bytes 196616 | tf_op jit(solution)/shard_map/ppermute | solution.py:42
  35.2 13.4 %collective-permute-done.1 = f32[32,512]{1,0:T(8,128)S(1)} collective-permute-done((f32[32,512]{1,0:T(8,128)S(1)}, f32[32,512]{1,0:T(8,128)S(1)}, u32[]{:S(2)}, u32[]{:S(2)}) %collective-permute-start.1) | collective-permute-done | bytes 65568 | tf_op jit(solution)/shard_map/ppermute | solution.py:42
  48.6 2.3 %fusion.1 = f16[4,8,24,512]{3,2,1,0:T(8,128)(2,1)S(1)} fusion(f16[4,4,8,24,512]{4,3,2,1,0:T(8,128)(2,1)} %all-to-all-done), kind=kLoop, calls=%fused_computation.3 | loop fusion | flops 3145728 | bytes 3932160 | tf_op jit(solution)/shard_map/convert_element_type | solution.py:131
  50.9 12.2 %all_to_all.36 = f16[4,8,24,512]{3,2,1,0:T(8,128)(2,1)S(1)} all-to-all(f16[4,8,24,512]{3,2,1,0:T(8,128)(2,1)S(1)} %fusion.1), channel_id=1, replica_groups={{0,1,16,17},{2,3,18,19},{32,33,48,49},{34,35,50,51},{64,65,80,81},{66,6..., dimensions={0} | all-to-all | bytes 1572864 | tf_op jit(solution)/shard_map/all_to_all | solution.py:26
  63.1 0.8 fusion.3
  63.9 9.3 %all-to-all-start.2 = ((f16[8,24,512]{2,1,0:T(8,128)(2,1)}), f16[8,24,512]{2,1,0:T(8,128)(2,1)S(1)}, u32[]{:S(2)}, u32[]{:S(2)}) async-start(f16[8,24,512]{2,1,0:T(8,128)(2,1)} %fusion.3), calls=%async_computation.2 | async-start | bytes 393216 | tf_op jit(solution)/shard_map/all_to_all | solution.py:26
  73.3 9.0 %all-to-all-done.2 = f16[8,24,512]{2,1,0:T(8,128)(2,1)S(1)} async-done(((f16[8,24,512]{2,1,0:T(8,128)(2,1)}), f16[8,24,512]{2,1,0:T(8,128)(2,1)S(1)}, u32[]{:S(2)}, u32[]{:S(2)}) %all-to-all-start.2) | async-done | bytes 196640 | tf_op jit(solution)/shard_map/all_to_all | solution.py:26
  82.2 0.7 fusion.10
  82.9 0.7 subtract_convert_fusion
  83.6 11.8 %all_to_all.37 = bf16[8,24,512]{2,1,0:T(8,128)(2,1)S(1)} all-to-all(bf16[8,24,512]{2,1,0:T(8,128)(2,1)S(1)} %broadcast_in_dim.14), channel_id=1, replica_groups={{0,2,32,34,64,66,96,98},{1,3,33,35,65,67,97,99},{16,18,48,50,80,82,112,..., dimensions={0} | all-to-all | bytes 393216 | tf_op jit(solution)/shard_map/all_to_all | solution.py:26
  95.4 13.3 %all_to_all.38 = bf16[4,8,24,512]{3,2,1,0:T(8,128)(2,1)S(1)} all-to-all(bf16[4,8,24,512]{3,2,1,0:T(8,128)(2,1)S(1)} %broadcast_in_dim.15), channel_id=1, replica_groups={{0,1,16,17},{2,3,18,19},{32,33,48,49},{34,35,50,51},{64,65,80,81},{66,6..., dimensions={0} | all-to-all | bytes 1572864 | tf_op jit(solution)/shard_map/all_to_all | solution.py:26
  108.7 2.0 %broadcast_in_dim.32 = bf16[4,4,8,24,512]{4,3,2,1,0:T(8,128)(2,1)} broadcast(bf16[4,8,24,512]{3,2,1,0:T(8,128)(2,1)S(1)} %all_to_all.38), dimensions={1,2,3,4} | broadcast | bytes 3932160 | tf_op jit(solution)/shard_map/broadcast_in_dim | solution.py:30
  110.7 4.6 %all-to-all-start.5 = ((bf16[4,4,8,24,512]{4,3,2,1,0:T(8,128)(2,1)}), bf16[4,4,8,24,512]{4,3,2,1,0:T(8,128)(2,1)}, u32[]{:S(2)}, u32[]{:S(2)}) async-start(bf16[4,4,8,24,512]{4,3,2,1,0:T(8,128)(2,1)} %broadcast_in_dim.32), calls=%async_computation.5 | async-start | bytes 6291456 | tf_op jit(solution)/shard_map/all_to_all | solution.py:26
  116.6 18.6 %all-to-all-done.5 = bf16[4,4,8,24,512]{4,3,2,1,0:T(8,128)(2,1)} async-done(((bf16[4,4,8,24,512]{4,3,2,1,0:T(8,128)(2,1)}), bf16[4,4,8,24,512]{4,3,2,1,0:T(8,128)(2,1)}, u32[]{:S(2)}, u32[]{:S(2)}) %all-to-all-start.5) | async-done | bytes 3145760 | tf_op jit(solution)/shard_map/all_to_all | solution.py:26
  135.2 4.0 %conditional.3 = (bf16[1,3072,512]{2,1,0:T(8,128)(2,1)}) conditional(s32[]{:T(128)} %convert_element_type.108, bf16[4,4,8,24,512]{4,3,2,1,0:T(8,128)(2,1)} %all-to-all-done.5, bf16[4,4,8,24,512]{4,3,2,1,0:T(8,128)(2,1)} %all-to-all-done.5), branch_computations={%region_2.3_spmd, %region_3.4_spmd} | conditional | bytes 6291464 | solution.py:90
  135.2 4.0 %copy.14 = bf16[2,2,4,4,2,24,512]{6,5,1,4,2,0,3:T(8,128)(2,1)} copy(bf16[2,2,4,4,2,24,512]{6,5,4,3,2,1,0:T(8,128)(2,1)} %bitcast.6) | data formatting | bytes 6291456 | tf_op jit(solution)/shard_map/cond/branch_0_fun/reshape | solution.py:85
  (25 shorter events, 1.4 us)
Async XLA Ops:
  0.6 1.7 %copy-start = (bf16[1,384,3072]{2,1,0:T(8,128)(2,1)S(1)}, bf16[1,384,3072]{2,1,0:T(8,128)(2,1)}, u32[]{:S(2)}) copy-start(bf16[1,384,3072]{2,1,0:T(8,128)(2,1)} %param.11) | copy-start | bytes 7077892
  7.6 5.3 %copy-start.1 = (f32[1,24,512]{2,1,0:T(8,128)S(1)}, f32[1,24,512]{2,1,0:T(8,128)}, u32[]{:S(2)}) copy-start(f32[1,24,512]{2,1,0:T(8,128)} %param.13) | copy-start | bytes 147460
  7.6 5.3 %copy-start.2 = (f32[24,512]{1,0:T(8,128)S(1)}, f32[24,512]{1,0:T(8,128)}, u32[]{:S(2)}) copy-start(f32[24,512]{1,0:T(8,128)} %param.14) | copy-start | bytes 147460
  7.6 5.4 %copy-start.5 = (f32[1,4,512]{2,1,0:T(4,128)S(1)}, f32[1,4,512]{2,1,0:T(4,128)}, u32[]{:S(2)}) copy-start(f32[1,4,512]{2,1,0:T(4,128)} %param.15) | copy-start | bytes 24580
  7.6 41.0 %all-to-all-start = ((f16[4,4,8,24,512]{4,3,2,1,0:T(8,128)(2,1)}), f16[4,4,8,24,512]{4,3,2,1,0:T(8,128)(2,1)}, u32[]{:S(2)}, u32[]{:S(2)}) async-start(f16[4,4,8,24,512]{4,3,2,1,0:T(8,128)(2,1)} %get-tuple-element.35), calls=%async_computation | async-start | bytes 6291456 | tf_op jit(solution)/shard_map/all_to_all | solution.py:26
  13.0 12.8 %collective-permute-start = (f32[28,512]{1,0:T(8,128)S(1)}, f32[28,512]{1,0:T(8,128)S(1)}, u32[]{:S(2)}, u32[]{:S(2)}) collective-permute-start(f32[28,512]{1,0:T(8,128)S(1)} %pad_maximum_fusion.1), channel_id=1, source_target_pairs={{0,128},{128,0},{1,129},{129,1},{2,130},{130,2},{3,131},{131,3},{4... | collective-permute-start | bytes 172040 | tf_op jit(solution)/shard_map/ppermute | solution.py:42
  25.8 56.4 %copy-start.4 = (f32[1,24,512]{2,1,0:T(8,128)S(1)}, f32[1,24,512]{2,1,0:T(8,128)}, u32[]{:S(2)}) copy-start(f32[1,24,512]{2,1,0:T(8,128)} %param.17) | copy-start | bytes 147460
  25.8 57.1 %copy-start.3 = (f32[1,24,512]{2,1,0:T(8,128)S(1)}, f32[1,24,512]{2,1,0:T(8,128)}, u32[]{:S(2)}) copy-start(f32[1,24,512]{2,1,0:T(8,128)} %param.16) | copy-start | bytes 147460
  25.8 22.7 %collective-permute-start.1 = (f32[32,512]{1,0:T(8,128)S(1)}, f32[32,512]{1,0:T(8,128)S(1)}, u32[]{:S(2)}, u32[]{:S(2)}) collective-permute-start(f32[32,512]{1,0:T(8,128)S(1)} %pad_maximum_fusion.2), channel_id=1, source_target_pairs={{0,256},{256,512},{512,0},{1,257},{257,513},{513,1},{2,258},{258,5... | collective-permute-start | bytes 196616 | tf_op jit(solution)/shard_map/ppermute | solution.py:42
  27.9 20.7 %collective-permute-start.2 = (f32[32,512]{1,0:T(8,128)S(1)}, f32[32,512]{1,0:T(8,128)S(1)}, u32[]{:S(2)}, u32[]{:S(2)}) collective-permute-start(f32[32,512]{1,0:T(8,128)S(1)} %pad_maximum_fusion.2), channel_id=1, source_target_pairs={{0,512},{256,0},{512,256},{1,513},{257,1},{513,257},{2,514},{258,2... | collective-permute-start | bytes 196616 | tf_op jit(solution)/shard_map/ppermute | solution.py:42
  63.9 18.4 %all-to-all-start.2 = ((f16[8,24,512]{2,1,0:T(8,128)(2,1)}), f16[8,24,512]{2,1,0:T(8,128)(2,1)S(1)}, u32[]{:S(2)}, u32[]{:S(2)}) async-start(f16[8,24,512]{2,1,0:T(8,128)(2,1)} %fusion.3), calls=%async_computation.2 | async-start | bytes 393216 | tf_op jit(solution)/shard_map/all_to_all | solution.py:26
  110.7 24.5 %all-to-all-start.5 = ((bf16[4,4,8,24,512]{4,3,2,1,0:T(8,128)(2,1)}), bf16[4,4,8,24,512]{4,3,2,1,0:T(8,128)(2,1)}, u32[]{:S(2)}, u32[]{:S(2)}) async-start(bf16[4,4,8,24,512]{4,3,2,1,0:T(8,128)(2,1)} %broadcast_in_dim.32), calls=%async_computation.5 | async-start | bytes 6291456 | tf_op jit(solution)/shard_map/all_to_all | solution.py:26

commit v10 on v9

--- a/solution.py
+++ b/solution.py
@@ -106,9 +106,7 @@
 
     core = lax.axis_index(CORE)
     hi = lax.axis_index(HI)
-    deltas = global_params - own_local
-    mine = jnp.concatenate([deltas, outer_momentum[0]], 0)
-    other = passed(mine, CORE, 1)
+    chips = arrived_along(jnp.concatenate([own_local, outer_momentum[0]], 0), HI)
 
     term = lax.dot_general(
         features, cotangent, (((0,), (0,)), ((), ())), preferred_element_type=jnp.float32
@@ -116,12 +114,22 @@
     blocks = per_core(core, to_places, split, term)
     summed_near = exchanged(blocks, near)
 
-    upper, lower = jnp.where(core == 0, mine, other), jnp.where(core == 0, other, mine)
-    pair = jnp.concatenate([mine[:rows] + other[:rows], upper[rows:], lower[rows:]], 0)
-    summed_near, chips = lax.optimization_barrier((summed_near, arrived_along(pair, HI)))
+    summed_near, chips = lax.optimization_barrier((summed_near, chips))
     by_chip = in_order(chips, HI)
-    outer_grad = sum(p[:rows] for p in by_chip) / replicas
-    old_rows = jnp.concatenate([p[rows:] for p in by_chip], 0)
+    summed = jnp.concatenate(
+        [sum(global_params - c[:rows] for c in by_chip)] + [c[rows:] for c in by_chip], 0
+    )
+    other = passed(summed, CORE, 1)
+    outer_grad = (summed[:rows] + other[:rows]) / replicas
+    upper, lower = jnp.where(core == 0, summed, other), jnp.where(core == 0, other, summed)
+    old_rows = jnp.concatenate(
+        [
+            side[lo : lo + sub_rows]
+            for lo in range(rows, rows + n_hi * sub_rows, sub_rows)
+            for side in (upper, lower)
+        ],
+        0,
+    )
     momentum_all = outer_mu * old_rows + outer_grad
     global_new = global_params - outer_rate * (outer_grad + outer_mu * momentum_all)
     momentum_new = lax.dynamic_slice_in_dim(

time: 140 us -> 140 us (level)
  blocking collectives: 37.2 us -> 23.8 us
  waiting for transfers between devices: 41.9 us -> 51.6 us
  other arithmetic: 5.15 us -> 6.76 us
    all_to_all x3 -> x2, blocking collectives: 37.2 us -> 23.8 us  [exchanged(): lax.all_to_all(x, REPLICA + DP, 0, 0, axis_index_groups=groups, tiled=True)]
    all_to_all x3 -> x4, waiting for transfers between devices: 27.6 us -> 32.5 us  [exchanged(): lax.all_to_all(x, REPLICA + DP, 0, 0, axis_index_groups=groups, tiled=True)]
    ppermute x3, waiting for transfers between devices: 14.3 us -> 19.1 us  [passed(): return lax.ppermute(x, axis, [(i, (i + step) % n) for i in range(n)])]
    all_to_all x3 -> x4, starting transfers between devices: 19.3 us -> 23.5 us  [exchanged(): lax.all_to_all(x, REPLICA + DP, 0, 0, axis_index_groups=groups, tiled=True)]
    ppermute x3, starting transfers between devices: 21.2 us -> 18.4 us  [passed(): return lax.ppermute(x, axis, [(i, (i + step) % n) for i in range(n)])]
  transfers between devices with their start and end apart: 6 -> 7, of which waited for: 4 -> 4; matrix products, arithmetic and copies ran while one was open for 1% -> 2% of each run, Pallas kernels for 0% -> 0%
where the time goes in v10:
time: 140 us; the launch traced here: 139 us
  waiting for transfers between devices  51.6 us (37%)
  starting transfers between devices  41.9 us (30%)
  blocking collectives  23.8 us (17%)
  local copies, waits for them, and re-layouts  11.5 us (8%)
  other arithmetic  6.76 us (5%)
  matrix products  2.83 us (2%)
    all_to_all x4, waiting for transfers between devices, exchanged(): lax.all_to_all(x, REPLICA + DP, 0, 0, axis_index_groups=groups, tiled=True)  32.5 us
    all_to_all x2, blocking collectives, exchanged(): lax.all_to_all(x, REPLICA + DP, 0, 0, axis_index_groups=groups, tiled=True)  23.8 us
    all_to_all x4, starting transfers between devices, exchanged(): lax.all_to_all(x, REPLICA + DP, 0, 0, axis_index_groups=groups, tiled=True)  23.5 us
    ppermute x3, waiting for transfers between devices, passed(): return lax.ppermute(x, axis, [(i, (i + step) % n) for i in range(n)])  19.1 us
    ppermute x3, starting transfers between devices, passed(): return lax.ppermute(x, axis, [(i, (i + step) % n) for i in range(n)])  18.4 us
    reshape x1, local copies, waits for them, and re-layouts, from_places(): parts = x.reshape(*(split[k] for k in order), *x.shape[-2:])  4.03 us
    convert_element_type x1, other arithmetic, per_device(): part = total(summed_near).astype(jnp.float16)  3.21 us
    dot_general x1, matrix products, per_device(): lax.dot_general(features, cotangent, (((0,), (0,)), ((), ())), preferred_...  2.83 us
  transfers between devices with their start and end apart: 7, of which 4 were waited for; matrix products, arithmetic and copies ran while one was open for 2% of the time, Pallas kernels for 0%

profile of v10, /device:TPU:1, one launch (start us, length us, event | category | flops | bytes accessed | tf_op | source)
XLA Modules:
  0.0 139.2 jit_solution(15572998516892416467)
XLA Ops:
  0.7 1.6 %copy-done = bf16[1,384,3072]{2,1,0:T(8,128)(2,1)S(1)} copy-done((bf16[1,384,3072]{2,1,0:T(8,128)(2,1)S(1)}, bf16[1,384,3072]{2,1,0:T(8,128)(2,1)}, u32[]{:S(2)}) %copy-start) | copy-done | bytes 2359320
  2.3 2.8 %convolution_convert_fusion = f16[3072,512]{1,0:T(8,128)(2,1)S(1)} fusion(bf16[1,384,3072]{2,1,0:T(8,128)(2,1)S(1)} %copy-done, bf16[1,384,512]{2,1,0:T(8,128)(2,1)} %param.12), kind=kOutput, calls=%fused_computation | convolution fusion | flops 1209532416 | bytes 5898240 | tf_op jit(solution)/shard_map/dot_general | solution.py:111
  5.1 2.5 %conditional.2 = (f16[4,4,8,24,512]{4,3,2,1,0:T(8,128)(2,1)}) conditional(s32[]{:T(128)} %convert_element_type.108, f16[3072,512]{1,0:T(8,128)(2,1)S(1)} %convolution_convert_fusion, f16[3072,512]{1,0:T(8,128)(2,1)S(1)} %convolution_convert_fusion), branch_computations={%region_0.0_spmd, %region_1.0_spmd} | conditional | bytes 6291464 | solution.py:90
  5.2 2.5 %copy.12 = f16[4,2,4,2,2,24,512]{6,5,3,0,2,4,1:T(8,128)(2,1)} copy(f16[4,2,4,2,2,24,512]{6,5,4,3,2,1,0:T(8,128)(2,1)S(1)} %bitcast.79) | data formatting | bytes 6291456 | tf_op jit(solution)/shard_map/cond/branch_0_fun/reshape | solution.py:80
  7.6 5.3 %all-to-all-start = ((f16[4,4,8,24,512]{4,3,2,1,0:T(8,128)(2,1)}), f16[4,4,8,24,512]{4,3,2,1,0:T(8,128)(2,1)}, u32[]{:S(2)}, u32[]{:S(2)}) async-start(f16[4,4,8,24,512]{4,3,2,1,0:T(8,128)(2,1)} %get-tuple-element.43), calls=%async_computation | async-start | bytes 6291456 | tf_op jit(solution)/shard_map/all_to_all | solution.py:26
  13.0 10.9 %collective-permute-start = (f32[28,512]{1,0:T(8,128)S(1)}, f32[28,512]{1,0:T(8,128)S(1)}, u32[]{:S(2)}, u32[]{:S(2)}) collective-permute-start(f32[28,512]{1,0:T(8,128)S(1)} %pad_maximum_fusion.2), channel_id=1, source_target_pairs={{0,256},{256,512},{512,0},{1,257},{257,513},{513,1},{2,258},{258,5... | collective-permute-start | bytes 172040 | tf_op jit(solution)/shard_map/ppermute | solution.py:42
  23.9 5.6 %collective-permute-start.1 = (f32[28,512]{1,0:T(8,128)S(1)}, f32[28,512]{1,0:T(8,128)S(1)}, u32[]{:S(2)}, u32[]{:S(2)}) collective-permute-start(f32[28,512]{1,0:T(8,128)S(1)} %pad_maximum_fusion.2), channel_id=1, source_target_pairs={{0,512},{256,0},{512,256},{1,513},{257,1},{513,257},{2,514},{258,2... | collective-permute-start | bytes 172040 | tf_op jit(solution)/shard_map/ppermute | solution.py:42
  29.5 19.1 %collective-permute-done = f32[28,512]{1,0:T(8,128)S(1)} collective-permute-done((f32[28,512]{1,0:T(8,128)S(1)}, f32[28,512]{1,0:T(8,128)S(1)}, u32[]{:S(2)}, u32[]{:S(2)}) %collective-permute-start) | collective-permute-done | bytes 57376 | tf_op jit(solution)/shard_map/ppermute | solution.py:42
  48.6 3.2 %fusion.1 = f16[4,8,24,512]{3,2,1,0:T(8,128)(2,1)} fusion(f16[4,4,8,24,512]{4,3,2,1,0:T(8,128)(2,1)} %all-to-all-done), kind=kLoop, calls=%fused_computation.3 | loop fusion | flops 3145728 | bytes 3932160 | tf_op jit(solution)/shard_map/convert_element_type | solution.py:139
  51.8 4.1 %all-to-all-start.1 = ((f16[4,8,24,512]{3,2,1,0:T(8,128)(2,1)}), f16[4,8,24,512]{3,2,1,0:T(8,128)(2,1)S(1)}, u32[]{:S(2)}, u32[]{:S(2)}) async-start(f16[4,8,24,512]{3,2,1,0:T(8,128)(2,1)} %fusion.1), calls=%async_computation.1 | async-start | bytes 1572864 | tf_op jit(solution)/shard_map/all_to_all | solution.py:26
  56.7 1.9 %collective-permute-start.2 = (f32[36,512]{1,0:T(8,128)S(1)}, f32[36,512]{1,0:T(8,128)S(1)}, u32[]{:S(2)}, u32[]{:S(2)}) collective-permute-start(f32[36,512]{1,0:T(8,128)S(1)} %pad_maximum_fusion.1), channel_id=1, source_target_pairs={{0,128},{128,0},{1,129},{129,1},{2,130},{130,2},{3,131},{131,3},{4... | collective-permute-start | bytes 221192 | tf_op jit(solution)/shard_map/ppermute | solution.py:42
  58.6 5.7 %all-to-all-done.1 = f16[4,8,24,512]{3,2,1,0:T(8,128)(2,1)S(1)} async-done(((f16[4,8,24,512]{3,2,1,0:T(8,128)(2,1)}), f16[4,8,24,512]{3,2,1,0:T(8,128)(2,1)S(1)}, u32[]{:S(2)}, u32[]{:S(2)}) %all-to-all-start.1) | async-done | bytes 786464 | tf_op jit(solution)/shard_map/all_to_all | solution.py:26
  64.3 0.8 fusion.3
  65.1 9.3 %all-to-all-start.2 = ((f16[8,24,512]{2,1,0:T(8,128)(2,1)}), f16[8,24,512]{2,1,0:T(8,128)(2,1)S(1)}, u32[]{:S(2)}, u32[]{:S(2)}) async-start(f16[8,24,512]{2,1,0:T(8,128)(2,1)} %fusion.3), calls=%async_computation.2 | async-start | bytes 393216 | tf_op jit(solution)/shard_map/all_to_all | solution.py:26
  74.4 0.7 broadcast_select_fusion
  75.3 8.2 %all-to-all-done.2 = f16[8,24,512]{2,1,0:T(8,128)(2,1)S(1)} async-done(((f16[8,24,512]{2,1,0:T(8,128)(2,1)}), f16[8,24,512]{2,1,0:T(8,128)(2,1)S(1)}, u32[]{:S(2)}, u32[]{:S(2)}) %all-to-all-start.2) | async-done | bytes 196640 | tf_op jit(solution)/shard_map/all_to_all | solution.py:26
  84.1 0.7 subtract_convert_fusion
  84.8 11.8 %all_to_all.36 = bf16[8,24,512]{2,1,0:T(8,128)(2,1)S(1)} all-to-all(bf16[8,24,512]{2,1,0:T(8,128)(2,1)S(1)} %broadcast_in_dim.14), channel_id=1, replica_groups={{0,2,32,34,64,66,96,98},{1,3,33,35,65,67,97,99},{16,18,48,50,80,82,112,..., dimensions={0} | all-to-all | bytes 393216 | tf_op jit(solution)/shard_map/all_to_all | solution.py:26
  96.7 12.0 %all_to_all.37 = bf16[4,8,24,512]{3,2,1,0:T(8,128)(2,1)S(1)} all-to-all(bf16[4,8,24,512]{3,2,1,0:T(8,128)(2,1)S(1)} %broadcast_in_dim.15), channel_id=1, replica_groups={{0,1,16,17},{2,3,18,19},{32,33,48,49},{34,35,50,51},{64,65,80,81},{66,6..., dimensions={0} | all-to-all | bytes 1572864 | tf_op jit(solution)/shard_map/all_to_all | solution.py:26
  108.7 2.0 %broadcast_in_dim.32 = bf16[4,4,8,24,512]{4,3,2,1,0:T(8,128)(2,1)} broadcast(bf16[4,8,24,512]{3,2,1,0:T(8,128)(2,1)S(1)} %all_to_all.37), dimensions={1,2,3,4} | broadcast | bytes 3932160 | tf_op jit(solution)/shard_map/broadcast_in_dim | solution.py:30
  110.7 4.7 %all-to-all-start.5 = ((bf16[4,4,8,24,512]{4,3,2,1,0:T(8,128)(2,1)}), bf16[4,4,8,24,512]{4,3,2,1,0:T(8,128)(2,1)}, u32[]{:S(2)}, u32[]{:S(2)}) async-start(bf16[4,4,8,24,512]{4,3,2,1,0:T(8,128)(2,1)} %broadcast_in_dim.32), calls=%async_computation.5 | async-start | bytes 6291456 | tf_op jit(solution)/shard_map/all_to_all | solution.py:26
  116.6 18.6 %all-to-all-done.5 = bf16[4,4,8,24,512]{4,3,2,1,0:T(8,128)(2,1)} async-done(((bf16[4,4,8,24,512]{4,3,2,1,0:T(8,128)(2,1)}), bf16[4,4,8,24,512]{4,3,2,1,0:T(8,128)(2,1)}, u32[]{:S(2)}, u32[]{:S(2)}) %all-to-all-start.5) | async-done | bytes 3145760 | tf_op jit(solution)/shard_map/all_to_all | solution.py:26
  135.2 4.0 %conditional.3 = (bf16[1,3072,512]{2,1,0:T(8,128)(2,1)}) conditional(s32[]{:T(128)} %convert_element_type.108, bf16[4,4,8,24,512]{4,3,2,1,0:T(8,128)(2,1)} %all-to-all-done.5, bf16[4,4,8,24,512]{4,3,2,1,0:T(8,128)(2,1)} %all-to-all-done.5), branch_computations={%region_2.3_spmd, %region_3.4_spmd} | conditional | bytes 6291464 | solution.py:90
  135.2 4.0 %copy.14 = bf16[2,2,4,4,2,24,512]{6,5,1,4,2,0,3:T(8,128)(2,1)} copy(bf16[2,2,4,4,2,24,512]{6,5,4,3,2,1,0:T(8,128)(2,1)} %bitcast.6) | data formatting | bytes 6291456 | tf_op jit(solution)/shard_map/cond/branch_0_fun/reshape | solution.py:85
  (32 shorter events, 2.7 us)
Async XLA Ops:
  0.6 1.7 %copy-start = (bf16[1,384,3072]{2,1,0:T(8,128)(2,1)S(1)}, bf16[1,384,3072]{2,1,0:T(8,128)(2,1)}, u32[]{:S(2)}) copy-start(bf16[1,384,3072]{2,1,0:T(8,128)(2,1)} %param.11) | copy-start | bytes 7077892
  7.6 5.3 %copy-start.1 = (f32[1,24,512]{2,1,0:T(8,128)S(1)}, f32[1,24,512]{2,1,0:T(8,128)}, u32[]{:S(2)}) copy-start(f32[1,24,512]{2,1,0:T(8,128)} %param.13) | copy-start | bytes 147460
  7.6 5.3 %copy-start.8 = (f32[1,4,512]{2,1,0:T(4,128)S(1)}, f32[1,4,512]{2,1,0:T(4,128)}, u32[]{:S(2)}) copy-start(f32[1,4,512]{2,1,0:T(4,128)} %param.15) | copy-start | bytes 24580
  7.6 41.0 %all-to-all-start = ((f16[4,4,8,24,512]{4,3,2,1,0:T(8,128)(2,1)}), f16[4,4,8,24,512]{4,3,2,1,0:T(8,128)(2,1)}, u32[]{:S(2)}, u32[]{:S(2)}) async-start(f16[4,4,8,24,512]{4,3,2,1,0:T(8,128)(2,1)} %get-tuple-element.43), calls=%async_computation | async-start | bytes 6291456 | tf_op jit(solution)/shard_map/all_to_all | solution.py:26
  12.9 43.1 %copy-start.4 = (f32[24,512]{1,0:T(8,128)S(1)}, f32[24,512]{1,0:T(8,128)}, u32[]{:S(2)}) copy-start(f32[24,512]{1,0:T(8,128)} %param.14) | copy-start | bytes 147460
  13.0 35.6 %collective-permute-start = (f32[28,512]{1,0:T(8,128)S(1)}, f32[28,512]{1,0:T(8,128)S(1)}, u32[]{:S(2)}, u32[]{:S(2)}) collective-permute-start(f32[28,512]{1,0:T(8,128)S(1)} %pad_maximum_fusion.2), channel_id=1, source_target_pairs={{0,256},{256,512},{512,0},{1,257},{257,513},{513,1},{2,258},{258,5... | collective-permute-start | bytes 172040 | tf_op jit(solution)/shard_map/ppermute | solution.py:42
  23.9 24.7 %collective-permute-start.1 = (f32[28,512]{1,0:T(8,128)S(1)}, f32[28,512]{1,0:T(8,128)S(1)}, u32[]{:S(2)}, u32[]{:S(2)}) collective-permute-start(f32[28,512]{1,0:T(8,128)S(1)} %pad_maximum_fusion.2), channel_id=1, source_target_pairs={{0,512},{256,0},{512,256},{1,513},{257,1},{513,257},{2,514},{258,2... | collective-permute-start | bytes 172040 | tf_op jit(solution)/shard_map/ppermute | solution.py:42
  51.8 31.7 %copy-start.3 = (f32[1,24,512]{2,1,0:T(8,128)S(1)}, f32[1,24,512]{2,1,0:T(8,128)}, u32[]{:S(2)}) copy-start(f32[1,24,512]{2,1,0:T(8,128)} %param.17) | copy-start | bytes 147460
  51.8 32.3 %copy-start.2 = (f32[1,24,512]{2,1,0:T(8,128)S(1)}, f32[1,24,512]{2,1,0:T(8,128)}, u32[]{:S(2)}) copy-start(f32[1,24,512]{2,1,0:T(8,128)} %param.16) | copy-start | bytes 147460
  51.8 12.5 %all-to-all-start.1 = ((f16[4,8,24,512]{3,2,1,0:T(8,128)(2,1)}), f16[4,8,24,512]{3,2,1,0:T(8,128)(2,1)S(1)}, u32[]{:S(2)}, u32[]{:S(2)}) async-start(f16[4,8,24,512]{3,2,1,0:T(8,128)(2,1)} %fusion.1), calls=%async_computation.1 | async-start | bytes 1572864 | tf_op jit(solution)/shard_map/all_to_all | solution.py:26
  56.0 0.6 copy-start.5
  56.0 0.6 copy-start.6
  56.0 0.6 copy-start.7
  56.7 17.8 %collective-permute-start.2 = (f32[36,512]{1,0:T(8,128)S(1)}, f32[36,512]{1,0:T(8,128)S(1)}, u32[]{:S(2)}, u32[]{:S(2)}) collective-permute-start(f32[36,512]{1,0:T(8,128)S(1)} %pad_maximum_fusion.1), channel_id=1, source_target_pairs={{0,128},{128,0},{1,129},{129,1},{2,130},{130,2},{3,131},{131,3},{4... | collective-permute-start | bytes 221192 | tf_op jit(solution)/shard_map/ppermute | solution.py:42
  65.1 18.4 %all-to-all-start.2 = ((f16[8,24,512]{2,1,0:T(8,128)(2,1)}), f16[8,24,512]{2,1,0:T(8,128)(2,1)S(1)}, u32[]{:S(2)}, u32[]{:S(2)}) async-start(f16[8,24,512]{2,1,0:T(8,128)(2,1)} %fusion.3), calls=%async_computation.2 | async-start | bytes 393216 | tf_op jit(solution)/shard_map/all_to_all | solution.py:26
  110.7 24.5 %all-to-all-start.5 = ((bf16[4,4,8,24,512]{4,3,2,1,0:T(8,128)(2,1)}), bf16[4,4,8,24,512]{4,3,2,1,0:T(8,128)(2,1)}, u32[]{:S(2)}, u32[]{:S(2)}) async-start(bf16[4,4,8,24,512]{4,3,2,1,0:T(8,128)(2,1)} %broadcast_in_dim.32), calls=%async_computation.5 | async-start | bytes 6291456 | tf_op jit(solution)/shard_map/all_to_all | solution.py:26

commit v11 on v10

--- a/solution.py
+++ b/solution.py
@@ -5,6 +5,8 @@
 import jax.numpy as jnp
 import numpy as np
 from jax import lax
+from jax.experimental import pallas as pl
+from jax.experimental.pallas import tpu as pltpu
 from jax.sharding import Mesh
 from jax.sharding import PartitionSpec as P
 
@@ -81,9 +83,27 @@
     return parts.transpose(*order, 5, 6).reshape(4, 4, -1, *parts.shape[5:])
 
 
-def from_places(order, split, x):
-    parts = x.reshape(*(split[k] for k in order), *x.shape[-2:])
-    return parts.transpose(*(order.index(k) for k in range(5)), 5, 6).reshape(-1, x.shape[-1])
+def placing(places, blocks, out, sent):
+    count = blocks.shape[0]
+    moves = [
+        pltpu.make_async_copy(blocks.at[i], out.at[places[i]], sent.at[i]) for i in range(count)
+    ]
+    for move in moves:
+        move.start()
+    for move in moves:
+        move.wait()
+
+
+def placed(blocks, places):
+    anywhere = pl.BlockSpec(memory_space=pl.ANY)
+    return pl.pallas_call(
+        placing,
+        in_specs=[pl.BlockSpec(memory_space=pltpu.SMEM), anywhere],
+        out_specs=anywhere,
+        out_shape=jax.ShapeDtypeStruct(blocks.shape, blocks.dtype),
+        scratch_shapes=[pltpu.SemaphoreType.DMA((blocks.shape[0],))],
+        name="placed",
+    )(places, blocks)
 
 
 def per_core(core, way, split, x):
@@ -119,6 +139,11 @@
     summed = jnp.concatenate(
         [sum(global_params - c[:rows] for c in by_chip)] + [c[rows:] for c in by_chip], 0
     )
+
+    part = total(summed_near).astype(jnp.float16)
+    part = exchanged(part, middle)
+    part, summed = lax.optimization_barrier((part, summed))
+    part = total(part).astype(jnp.float16)
     other = passed(summed, CORE, 1)
     outer_grad = (summed[:rows] + other[:rows]) / replicas
     upper, lower = jnp.where(core == 0, summed, other), jnp.where(core == 0, other, summed)
@@ -136,8 +161,6 @@
         momentum_all, (hi * n_core + core) * sub_rows, sub_rows, 0
     )
 
-    part = total(summed_near).astype(jnp.float16)
-    part = total(exchanged(part, middle)).astype(jnp.float16)
     gradient = total(exchanged(part, far))
 
     first_new = beta_one * adam_first[0] + (1.0 - beta_one) * gradient
@@ -150,7 +173,9 @@
     held = merged
     for groups in (far, middle, near):
         held = exchanged(copies(held, len(groups[0])), groups)
-    gathered = per_core(core, from_places, split, held)
+    tables = [np.arange(ny * nx * nz).reshape(split).transpose(o).reshape(-1) for o in ORDERS]
+    places = jnp.where(core == 0, *(jnp.asarray(t, jnp.int32) for t in tables))
+    gathered = placed(held.reshape(-1, rows, width), places).reshape(-1, width)
     return (gathered[None], global_new, momentum_new[None], first_new[None], second_new[None])
 
 

time: 140 us -> 241 us (1.72); the launches traced: 139 us -> 237 us
  Pallas kernels: 0 us -> 98.3 us
  waiting for transfers between devices: 51.6 us -> 56.2 us
  local copies, waits for them, and re-layouts: 11.5 us -> 6.9 us
    pallas_call x0 -> x1, Pallas kernels: none -> 98.3 us  [placed(): pl.pallas_call(placing, in_specs=[pl.BlockSpec(memory_space=pltpu.SMEM),...]
    all_to_all x4, waiting for transfers between devices: 32.5 us -> 37.1 us  [exchanged(): lax.all_to_all(x, REPLICA + DP, 0, 0, axis_index_groups=groups, tiled=True)]
    reshape x1 -> x0, local copies, waits for them, and re-layouts: 4.03 us -> none  [from_places(): parts = x.reshape(*(split[k] for k in order), *x.shape[-2:])]
  transfers between devices with their start and end apart: 7 -> 7, of which waited for: 4 -> 4; matrix products, arithmetic and copies ran while one was open for 2% -> 1% of each run, Pallas kernels for 0% -> 0%
where the time goes in v11:
time: 241 us; the launch traced here: 237 us
  Pallas kernels  98.3 us (41%)
  waiting for transfers between devices  56.2 us (23%)
  starting transfers between devices  42 us (17%)
  blocking collectives  23 us (10%)
  local copies, waits for them, and re-layouts  6.9 us (3%)
  other arithmetic  6.51 us (3%)
  matrix products  2.83 us (1%)
    pallas_call x1, Pallas kernels, placed(): pl.pallas_call(placing, in_specs=[pl.BlockSpec(memory_space=pltpu.SMEM),...  98.3 us
    all_to_all x4, waiting for transfers between devices, exchanged(): lax.all_to_all(x, REPLICA + DP, 0, 0, axis_index_groups=groups, tiled=True)  37.1 us
    all_to_all x4, starting transfers between devices, exchanged(): lax.all_to_all(x, REPLICA + DP, 0, 0, axis_index_groups=groups, tiled=True)  23.6 us
    all_to_all x2, blocking collectives, exchanged(): lax.all_to_all(x, REPLICA + DP, 0, 0, axis_index_groups=groups, tiled=True)  23 us
    ppermute x3, waiting for transfers between devices, passed(): return lax.ppermute(x, axis, [(i, (i + step) % n) for i in range(n)])  19.1 us
    ppermute x3, starting transfers between devices, passed(): return lax.ppermute(x, axis, [(i, (i + step) % n) for i in range(n)])  18.4 us
  transfers between devices with their start and end apart: 7, of which 4 were waited for; matrix products, arithmetic and copies ran while one was open for 1% of the time, Pallas kernels for 0%

profile of v11, /device:TPU:1, one launch (start us, length us, event | category | flops | bytes accessed | tf_op | source)
XLA Modules:
  0.0 236.6 jit_solution(570005997488632612)
XLA Ops:
  0.7 1.6 copy-done
  2.3 2.8 %convolution_convert_fusion = f16[3072,512]{1,0:T(8,128)(2,1)S(1)} fusion(bf16[1,384,3072]{2,1,0:T(8,128)(2,1)S(1)} %copy-done, bf16[1,384,512]{2,1,0:T(8,128)(2,1)} %param.12), kind=kOutput, calls=%fused_computation | convolution fusion | flops 1209532416 | bytes 5898240 | tf_op jit(solution)/shard_map/dot_general | solution.py:131
  5.1 2.5 %conditional.1 = (f16[4,4,8,24,512]{4,3,2,1,0:T(8,128)(2,1)}) conditional(s32[]{:T(128)} %convert_element_type.107, f16[3072,512]{1,0:T(8,128)(2,1)S(1)} %convolution_convert_fusion, f16[3072,512]{1,0:T(8,128)(2,1)S(1)} %convolution_convert_fusion), branch_computations={%region_0.0_spmd, %region_1.0_spmd} | conditional | bytes 6291464 | solution.py:110
  5.2 2.5 %copy.14 = f16[4,2,4,2,2,24,512]{6,5,3,0,2,4,1:T(8,128)(2,1)} copy(f16[4,2,4,2,2,24,512]{6,5,4,3,2,1,0:T(8,128)(2,1)S(1)} %bitcast.73) | data formatting | bytes 6291456 | tf_op jit(solution)/shard_map/cond/branch_0_fun/reshape | solution.py:82
  7.6 5.3 %all-to-all-start = ((f16[4,4,8,24,512]{4,3,2,1,0:T(8,128)(2,1)}), f16[4,4,8,24,512]{4,3,2,1,0:T(8,128)(2,1)}, u32[]{:S(2)}, u32[]{:S(2)}) async-start(f16[4,4,8,24,512]{4,3,2,1,0:T(8,128)(2,1)} %get-tuple-element.41), calls=%async_computation | async-start | bytes 6291456 | tf_op jit(solution)/shard_map/all_to_all | solution.py:28
  13.0 10.9 %collective-permute-start = (f32[28,512]{1,0:T(8,128)S(1)}, f32[28,512]{1,0:T(8,128)S(1)}, u32[]{:S(2)}, u32[]{:S(2)}) collective-permute-start(f32[28,512]{1,0:T(8,128)S(1)} %pad_maximum_fusion.2), channel_id=1, source_target_pairs={{0,256},{256,512},{512,0},{1,257},{257,513},{513,1},{2,258},{258,5... | collective-permute-start | bytes 172040 | tf_op jit(solution)/shard_map/ppermute | solution.py:44
  23.9 5.6 %collective-permute-start.1 = (f32[28,512]{1,0:T(8,128)S(1)}, f32[28,512]{1,0:T(8,128)S(1)}, u32[]{:S(2)}, u32[]{:S(2)}) collective-permute-start(f32[28,512]{1,0:T(8,128)S(1)} %pad_maximum_fusion.2), channel_id=1, source_target_pairs={{0,512},{256,0},{512,256},{1,513},{257,1},{513,257},{2,514},{258,2... | collective-permute-start | bytes 172040 | tf_op jit(solution)/shard_map/ppermute | solution.py:44
  29.5 19.1 %collective-permute-done = f32[28,512]{1,0:T(8,128)S(1)} collective-permute-done((f32[28,512]{1,0:T(8,128)S(1)}, f32[28,512]{1,0:T(8,128)S(1)}, u32[]{:S(2)}, u32[]{:S(2)}) %collective-permute-start) | collective-permute-done | bytes 57376 | tf_op jit(solution)/shard_map/ppermute | solution.py:44
  48.6 3.2 %fusion.1 = f16[4,8,24,512]{3,2,1,0:T(8,128)(2,1)} fusion(f16[4,4,8,24,512]{4,3,2,1,0:T(8,128)(2,1)} %all-to-all-done), kind=kLoop, calls=%fused_computation.3 | loop fusion | flops 3145728 | bytes 3932160 | tf_op jit(solution)/shard_map/convert_element_type | solution.py:143
  51.8 4.1 %all-to-all-start.1 = ((f16[4,8,24,512]{3,2,1,0:T(8,128)(2,1)}), f16[4,8,24,512]{3,2,1,0:T(8,128)(2,1)S(1)}, u32[]{:S(2)}, u32[]{:S(2)}) async-start(f16[4,8,24,512]{3,2,1,0:T(8,128)(2,1)} %fusion.1), calls=%async_computation.1 | async-start | bytes 1572864 | tf_op jit(solution)/shard_map/all_to_all | solution.py:28
  56.1 8.2 %all-to-all-done.1 = f16[4,8,24,512]{3,2,1,0:T(8,128)(2,1)S(1)} async-done(((f16[4,8,24,512]{3,2,1,0:T(8,128)(2,1)}), f16[4,8,24,512]{3,2,1,0:T(8,128)(2,1)S(1)}, u32[]{:S(2)}, u32[]{:S(2)}) %all-to-all-start.1) | async-done | bytes 786464 | tf_op jit(solution)/shard_map/all_to_all | solution.py:28
  64.3 1.9 collective-permute-start.2
  66.2 0.8 fusion.3
  67.0 9.3 %all-to-all-start.2 = ((f16[8,24,512]{2,1,0:T(8,128)(2,1)}), f16[8,24,512]{2,1,0:T(8,128)(2,1)S(1)}, u32[]{:S(2)}, u32[]{:S(2)}) async-start(f16[8,24,512]{2,1,0:T(8,128)(2,1)} %fusion.3), calls=%async_computation.2 | async-start | bytes 393216 | tf_op jit(solution)/shard_map/all_to_all | solution.py:28
  76.5 10.1 %all-to-all-done.2 = f16[8,24,512]{2,1,0:T(8,128)(2,1)S(1)} async-done(((f16[8,24,512]{2,1,0:T(8,128)(2,1)}), f16[8,24,512]{2,1,0:T(8,128)(2,1)S(1)}, u32[]{:S(2)}, u32[]{:S(2)}) %all-to-all-start.2) | async-done | bytes 196640 | tf_op jit(solution)/shard_map/all_to_all | solution.py:28
  86.6 0.7 fusion.10
  87.2 0.7 subtract_convert_fusion
  87.9 12.3 %all_to_all.30 = bf16[8,24,512]{2,1,0:T(8,128)(2,1)S(1)} all-to-all(bf16[8,24,512]{2,1,0:T(8,128)(2,1)S(1)} %broadcast_in_dim.8), channel_id=1, replica_groups={{0,2,32,34,64,66,96,98},{1,3,33,35,65,67,97,99},{16,18,48,50,80,82,112,..., dimensions={0} | all-to-all | bytes 393216 | tf_op jit(solution)/shard_map/all_to_all | solution.py:28
  100.3 10.7 %all_to_all.31 = bf16[4,8,24,512]{3,2,1,0:T(8,128)(2,1)S(1)} all-to-all(bf16[4,8,24,512]{3,2,1,0:T(8,128)(2,1)S(1)} %broadcast_in_dim.9), channel_id=1, replica_groups={{0,1,16,17},{2,3,18,19},{32,33,48,49},{34,35,50,51},{64,65,80,81},{66,6..., dimensions={0} | all-to-all | bytes 1572864 | tf_op jit(solution)/shard_map/all_to_all | solution.py:28
  111.0 2.0 broadcast_in_dim.10
  113.0 4.8 %all-to-all-start.5 = ((bf16[4,4,8,24,512]{4,3,2,1,0:T(8,128)(2,1)}), bf16[4,4,8,24,512]{4,3,2,1,0:T(8,128)(2,1)}, u32[]{:S(2)}, u32[]{:S(2)}) async-start(bf16[4,4,8,24,512]{4,3,2,1,0:T(8,128)(2,1)} %broadcast_in_dim.10), calls=%async_computation.5 | async-start | bytes 6291456 | tf_op jit(solution)/shard_map/all_to_all | solution.py:28
  118.9 0.6 multiply_add_fusion
  119.5 18.8 %all-to-all-done.5 = bf16[4,4,8,24,512]{4,3,2,1,0:T(8,128)(2,1)} async-done(((bf16[4,4,8,24,512]{4,3,2,1,0:T(8,128)(2,1)}), bf16[4,4,8,24,512]{4,3,2,1,0:T(8,128)(2,1)}, u32[]{:S(2)}, u32[]{:S(2)}) %all-to-all-start.5) | async-done | bytes 3145760 | tf_op jit(solution)/shard_map/all_to_all | solution.py:28
  138.3 98.3 %placed.1 = bf16[128,24,512]{2,1,0:T(8,128)(2,1)} custom-call(s32[128]{0:T(128)} %broadcast_select_fusion.2.places, bf16[128,24,512]{2,1,0:T(8,128)(2,1)} %bitcast.24.blocks), custom_call_target="tpu_custom_call" | custom-call | tf_op jit(solution)/shard_map/placed/pallas_call | solution.py:99
  (30 shorter events, 1.4 us)
Async XLA Ops:
  0.6 1.7 copy-start
  7.6 5.3 %copy-start.1 = (f32[1,24,512]{2,1,0:T(8,128)S(1)}, f32[1,24,512]{2,1,0:T(8,128)}, u32[]{:S(2)}) copy-start(f32[1,24,512]{2,1,0:T(8,128)} %param.13) | copy-start | bytes 147460
  7.6 5.3 %copy-start.5 = (f32[1,4,512]{2,1,0:T(4,128)S(1)}, f32[1,4,512]{2,1,0:T(4,128)}, u32[]{:S(2)}) copy-start(f32[1,4,512]{2,1,0:T(4,128)} %param.15) | copy-start | bytes 24580
  7.6 41.0 %all-to-all-start = ((f16[4,4,8,24,512]{4,3,2,1,0:T(8,128)(2,1)}), f16[4,4,8,24,512]{4,3,2,1,0:T(8,128)(2,1)}, u32[]{:S(2)}, u32[]{:S(2)}) async-start(f16[4,4,8,24,512]{4,3,2,1,0:T(8,128)(2,1)} %get-tuple-element.41), calls=%async_computation | async-start | bytes 6291456 | tf_op jit(solution)/shard_map/all_to_all | solution.py:28
  12.9 43.1 %copy-start.4 = (f32[24,512]{1,0:T(8,128)S(1)}, f32[24,512]{1,0:T(8,128)}, u32[]{:S(2)}) copy-start(f32[24,512]{1,0:T(8,128)} %param.14) | copy-start | bytes 147460
  13.0 35.6 %collective-permute-start = (f32[28,512]{1,0:T(8,128)S(1)}, f32[28,512]{1,0:T(8,128)S(1)}, u32[]{:S(2)}, u32[]{:S(2)}) collective-permute-start(f32[28,512]{1,0:T(8,128)S(1)} %pad_maximum_fusion.2), channel_id=1, source_target_pairs={{0,256},{256,512},{512,0},{1,257},{257,513},{513,1},{2,258},{258,5... | collective-permute-start | bytes 172040 | tf_op jit(solution)/shard_map/ppermute | solution.py:44
  23.9 24.7 %collective-permute-start.1 = (f32[28,512]{1,0:T(8,128)S(1)}, f32[28,512]{1,0:T(8,128)S(1)}, u32[]{:S(2)}, u32[]{:S(2)}) collective-permute-start(f32[28,512]{1,0:T(8,128)S(1)} %pad_maximum_fusion.2), channel_id=1, source_target_pairs={{0,512},{256,0},{512,256},{1,513},{257,1},{513,257},{2,514},{258,2... | collective-permute-start | bytes 172040 | tf_op jit(solution)/shard_map/ppermute | solution.py:44
  51.8 34.8 %copy-start.3 = (f32[1,24,512]{2,1,0:T(8,128)S(1)}, f32[1,24,512]{2,1,0:T(8,128)}, u32[]{:S(2)}) copy-start(f32[1,24,512]{2,1,0:T(8,128)} %param.17) | copy-start | bytes 147460
  51.8 35.4 %copy-start.2 = (f32[1,24,512]{2,1,0:T(8,128)S(1)}, f32[1,24,512]{2,1,0:T(8,128)}, u32[]{:S(2)}) copy-start(f32[1,24,512]{2,1,0:T(8,128)} %param.16) | copy-start | bytes 147460
  51.8 12.5 %all-to-all-start.1 = ((f16[4,8,24,512]{3,2,1,0:T(8,128)(2,1)}), f16[4,8,24,512]{3,2,1,0:T(8,128)(2,1)S(1)}, u32[]{:S(2)}, u32[]{:S(2)}) async-start(f16[4,8,24,512]{3,2,1,0:T(8,128)(2,1)} %fusion.1), calls=%async_computation.1 | async-start | bytes 1572864 | tf_op jit(solution)/shard_map/all_to_all | solution.py:28
  64.3 12.1 %collective-permute-start.2 = (f32[36,512]{1,0:T(8,128)S(1)}, f32[36,512]{1,0:T(8,128)S(1)}, u32[]{:S(2)}, u32[]{:S(2)}) collective-permute-start(f32[36,512]{1,0:T(8,128)S(1)} %pad_maximum_fusion.1), channel_id=1, source_target_pairs={{0,128},{128,0},{1,129},{129,1},{2,130},{130,2},{3,131},{131,3},{4... | collective-permute-start | bytes 221192 | tf_op jit(solution)/shard_map/ppermute | solution.py:44
  67.0 19.6 %all-to-all-start.2 = ((f16[8,24,512]{2,1,0:T(8,128)(2,1)}), f16[8,24,512]{2,1,0:T(8,128)(2,1)S(1)}, u32[]{:S(2)}, u32[]{:S(2)}) async-start(f16[8,24,512]{2,1,0:T(8,128)(2,1)} %fusion.3), calls=%async_computation.2 | async-start | bytes 393216 | tf_op jit(solution)/shard_map/all_to_all | solution.py:28
  113.0 4.8 %copy-start.6 = (s32[128]{0:T(128)S(1)}, s32[128]{0:T(128)}, u32[]{:S(2)}) copy-start(s32[128]{0:T(128)} %constant.60.clone) | copy-start | bytes 1540
  113.0 4.8 %copy-start.7 = (s32[128]{0:T(128)S(1)}, s32[128]{0:T(128)}, u32[]{:S(2)}) copy-start(s32[128]{0:T(128)} %constant.61.clone) | copy-start | bytes 1540
  113.0 25.3 %all-to-all-start.5 = ((bf16[4,4,8,24,512]{4,3,2,1,0:T(8,128)(2,1)}), bf16[4,4,8,24,512]{4,3,2,1,0:T(8,128)(2,1)}, u32[]{:S(2)}, u32[]{:S(2)}) async-start(bf16[4,4,8,24,512]{4,3,2,1,0:T(8,128)(2,1)} %broadcast_in_dim.10), calls=%async_computation.5 | async-start | bytes 6291456 | tf_op jit(solution)/shard_map/all_to_all | solution.py:28
